TPU v7x, 32 devices: a whole 2x2x4 slice. The times are simulated.
32 devices in a mesh: groups: 2 (over x), shard: 16 (over z, y, core).
Axes of the slice: x: 2, y: 2, z: 4, core: 2. Of those that a mesh axis runs over, the one named last changes fastest.
Arguments:
- item_table: bfloat16 [65536, 128], P('shard'), may hold values from -3 to 3
- row_accum: float32 [65536], P('shard'), may hold values from 0.1 to 1
- serving_table: bfloat16 [65536, 128], P('shard'), may hold values from -3 to 3
- grad_rows: bfloat16 [512, 128, 128], P(('groups', 'shard')), parts along dimension 0, may hold values from -6 to 6
- grad_ids: int32 [512, 128], P(('groups', 'shard')), parts along dimension 0, may hold values from 0 to 4095
- grad_counts: int32 [512], P(('groups', 'shard')), parts along dimension 0, may hold values from 1 to 128, as said below
- request_ids: int32 [512, 480], P(('groups', 'shard')), parts along dimension 0, may hold values from 0 to 4095
- request_slots: int32 [32768, 5], P(('groups', 'shard')), parts along dimension 0, may hold values from 0 to 7679, as said below
- cross_weight: bfloat16 [3, 640, 640], replicated, may hold values from -0.25 to 0.25
- cross_bias: bfloat16 [3, 640], replicated, may hold values from -3 to 3
- tower_weight: bfloat16 [640, 4096], replicated, may hold values from -0.25 to 0.25
- tower_bias: bfloat16 [4096], replicated, may hold values from -3 to 3
- score_weight: bfloat16 [4096], replicated, may hold values from -0.09375 to 0.09375
Outputs:
- new_table: bfloat16 [131072, 128], P(('groups', 'shard')), parts along dimension 0
- new_accum: float32 [131072], P(('groups', 'shard')), parts along dimension 0
- new_serving: bfloat16 [131072, 128], P(('groups', 'shard')), parts along dimension 0
- scores: float32 [32768], P(('groups', 'shard')), parts along dimension 0
There are 2 independent parts, one for each index of `groups`. A program takes and returns all parts, laid end to end along the dimension named above; an argument that names none is the same for every part. Nothing has to cross between parts.
Inputs may be any that keep to these rules, and one draw needn't show every extreme that they name: `grad_counts`: one owner, drawn from the seed, has all 128 slots used in the block of every device; slots past a count are padding. `grad_ids`: rows within the owner's block; slots past a count may hold any row. `request_ids`: slots that no request reads may hold any row. `request_slots`: all slots named by the requests of one device are distinct; every device uses all 480 slots of some owner.
All inputs are finite; a program needn't handle non-finite values. Where the computation divides by a largest or mean magnitude, that divisor is 1e-20 or more.
Results may differ from a plain program's by a relative error of at most 0.012.
Values may be sent and summed in bfloat16 or wider, within the bound.
No kernel may reach another device: no remote copies, remote signals or barrier semaphores. Data moves between devices by JAX's collectives and lax.ppermute only.
A program may use at most 64 MiB of HBM per device.

v0:
```python
import jax
import jax.numpy as jnp
from jax import lax
from jax.sharding import PartitionSpec as P

LEARN_RATE = 0.5
SCALE_FLOOR = 0.25


def from_behind(shard, axis, by):
    length = lax.axis_size(axis)
    return lax.ppermute(shard, axis, [(i, (i + by) % length) for i in range(length)])


def encode(row_delta):
    row_total, emb_width = row_delta.shape
    grouped = row_delta.reshape(row_total, emb_width // 32, 32)
    scales = jnp.maximum(jnp.max(jnp.abs(grouped), axis=2), SCALE_FLOOR).astype(jnp.bfloat16)
    payload = (grouped / scales.astype(jnp.float32)[:, :, None]).astype(jnp.bfloat16)
    return (payload.reshape(row_total, emb_width), scales)


def decode(payload, scales):
    row_total, emb_width = payload.shape
    grouped = payload.astype(jnp.float32).reshape(row_total, emb_width // 32, 32)
    return (grouped * scales.astype(jnp.float32)[:, :, None]).reshape(row_total, emb_width)


def adagrad(grad_part, accum_part, table_part):
    accum_next = accum_part + jnp.mean(grad_part * grad_part, axis=1)
    step_rows = LEARN_RATE * grad_part / jnp.sqrt(accum_next)[:, None]
    fresh_rows = (table_part.astype(jnp.float32) - step_rows).astype(jnp.bfloat16)
    row_delta = fresh_rows.astype(jnp.float32) - table_part.astype(jnp.float32)
    return (accum_next, fresh_rows, row_delta)


def tower_scores(request_block, cross_weight, cross_bias, tower_weight, tower_bias, score_weight):
    crossed = request_block
    base_values = request_block.astype(jnp.float32)
    for layer_index in range(cross_weight.shape[0]):
        projected = jnp.dot(crossed, cross_weight[layer_index], preferred_element_type=jnp.float32)
        projected = projected + cross_bias[layer_index].astype(jnp.float32)
        crossed = (base_values * projected + crossed.astype(jnp.float32)).astype(jnp.bfloat16)
    hidden = jnp.dot(crossed, tower_weight, preferred_element_type=jnp.float32) + tower_bias.astype(
        jnp.float32
    )
    hidden = jnp.maximum(hidden, 0.0).astype(jnp.bfloat16)
    return jnp.dot(hidden, score_weight, preferred_element_type=jnp.float32)


def body(
    item_table,
    row_accum,
    serving_table,
    grad_rows,
    grad_ids,
    grad_counts,
    request_ids,
    request_slots,
    cross_weight,
    cross_bias,
    tower_weight,
    tower_bias,
    score_weight,
):
    shards = lax.axis_size("shard")
    row_count, emb_width = item_table.shape
    slot_cap = grad_rows.shape[1]
    got_rows, got_ids, got_counts = (
        lax.all_to_all(grad_rows, "shard", split_axis=0, concat_axis=0, tiled=True),
        lax.all_to_all(grad_ids, "shard", split_axis=0, concat_axis=0, tiled=True),
        lax.all_to_all(grad_counts, "shard", split_axis=0, concat_axis=0, tiled=True),
    )
    is_valid = jnp.arange(slot_cap, dtype=jnp.int32)[None, :] < got_counts[:, None]
    flat_ids = got_ids.reshape(-1)
    values = jnp.where(is_valid[:, :, None], got_rows.astype(jnp.float32), 0.0).reshape(
        -1, emb_width
    )
    grad_sum = jnp.zeros((row_count, emb_width), jnp.float32).at[flat_ids].add(values)
    new_accum, new_table, row_delta = adagrad(grad_sum, row_accum, item_table)
    payload, scales = encode(row_delta)
    got_payload, got_scales = from_behind((payload, scales), "shard", 1)
    new_serving = (serving_table.astype(jnp.float32) + decode(got_payload, got_scales)).astype(
        jnp.bfloat16
    )
    routed = jnp.roll(request_ids, 1, axis=0)
    slot_width = routed.shape[1]
    found_rows = new_serving[
        lax.all_to_all(routed, "shard", split_axis=0, concat_axis=0, tiled=True)
    ]
    fetched = lax.all_to_all(found_rows, "shard", split_axis=0, concat_axis=0, tiled=True)
    slot_total = shards * slot_width
    picked = ((request_slots + slot_width) % slot_total).reshape(-1)
    features = fetched.reshape(-1, emb_width)[picked].reshape(request_slots.shape[0], -1)
    scores = tower_scores(
        features, cross_weight, cross_bias, tower_weight, tower_bias, score_weight
    )
    return (new_table, new_accum, new_serving, scores)


def solution(mesh):
    in_specs = (
        P("shard", None),
        P("shard"),
        P("shard", None),
        P(("groups", "shard"), None, None),
        P(("groups", "shard"), None),
        P(("groups", "shard")),
        P(("groups", "shard"), None),
        P(("groups", "shard"), None),
        P(),
        P(),
        P(),
        P(),
        P(),
    )
    out_specs = (
        P(("groups", "shard"), None),
        P(("groups", "shard")),
        P(("groups", "shard"), None),
        P(("groups", "shard")),
    )
    return jax.shard_map(body, mesh=mesh, in_specs=in_specs, out_specs=out_specs, check_vma=False)
```

profile of v0, /device:TPU:9, one launch (start us, length us, event | category | flops | bytes accessed | tf_op | source)
XLA Modules:
  0.0 194.1 jit_solution(9368163149003629129)
XLA Ops:
  0.6 0.7 copy.26
  1.4 11.1 %all_to_all.40 = s32[16,1,1]{2,1,0:T(1,128)S(1)} all-to-all(s32[16,1,1]{2,1,0:T(1,128)S(1)} %copy.26), channel_id=1, replica_groups=mesh['groups'=2,'shard'=16] {'shard'}, dimensions={0} | all-to-all | bytes 128 | tf_op jit(solution)/shard_map/all_to_all | solution.py:72
  12.4 9.8 %all_to_all.41 = s32[16,1,128]{2,1,0:T(1,128)S(1)} all-to-all(s32[16,1,128]{2,1,0:T(1,128)} %bitcast.38), channel_id=1, replica_groups=mesh['groups'=2,'shard'=16] {'shard'}, dimensions={0} | all-to-all | bytes 16384 | tf_op jit(solution)/shard_map/all_to_all | solution.py:71
  22.2 5.2 %all-to-all-start.2 = ((bf16[16,128,128]{2,1,0:T(8,128)(2,1)}), bf16[16,128,128]{2,1,0:T(8,128)(2,1)S(1)}, u32[]{:S(2)}, u32[]{:S(2)}) async-start(bf16[16,128,128]{2,1,0:T(8,128)(2,1)} %param.16), calls=%async_computation.2 | async-start | bytes 1048576 | tf_op jit(solution)/shard_map/all_to_all | solution.py:70
  27.4 0.4 reduce
  27.9 13.7 %all-to-all-done.2 = bf16[16,128,128]{2,1,0:T(8,128)(2,1)S(1)} async-done(((bf16[16,128,128]{2,1,0:T(8,128)(2,1)}), bf16[16,128,128]{2,1,0:T(8,128)(2,1)S(1)}, u32[]{:S(2)}, u32[]{:S(2)}) %all-to-all-start.2) | async-done | bytes 524320 | tf_op jit(solution)/shard_map/all_to_all | solution.py:70
  41.6 1.3 convert_select_fusion
  42.9 12.4 %scatter_custom_fusion = f32[4096,128]{1,0:T(8,128)S(1)} fusion(s32[2048]{0:T(1024)S(1)} %bitcast.39, f32[2048,128]{1,0:T(8,128)} %bitcast.35, f32[]{:T(128)} %constant.9.clone.1), kind=kCustom, calls=%fused_computation.27 | custom fusion | flops 262144 | bytes 2097664 | tf_op jit(solution)/shard_map/scatter-add | solution.py:79
  55.3 0.6 multiply_reduce_fusion
  55.9 0.6 fusion.26
  56.6 1.9 fusion.11
  58.4 1.5 copy.27
  60.2 1.6 div.29
  61.8 1.9 copy.28
  63.7 2.6 %divide_convert_fusion = bf16[4096,128]{1,0:T(8,128)(2,1)} fusion(f32[4096,128]{1,0:T(8,128)S(1)} %copy.28, bf16[4096,128]{1,0:T(8,128)(2,1)S(1)} %copy-done.1, bf16[4096,128]{1,0:T(8,128)(2,1)} %get-tuple-element.8), kind=kLoop, calls=%fused_computation.22 | loop fusion | flops 2621440 | bytes 5242880 | tf_op jit(solution)/shard_map/convert_element_type | solution.py:19
  66.3 0.7 collective-permute-start
  67.1 15.9 %all_to_all.42 = s32[16,1,480]{2,1,0:T(1,128)S(1)} all-to-all(s32[16,1,480]{2,1,0:T(1,128)S(1)} %all_to_all.31), channel_id=1, replica_groups=mesh['groups'=2,'shard'=16] {'shard'}, dimensions={0} | all-to-all | bytes 61440 | tf_op jit(solution)/shard_map/all_to_all | solution.py:89
  83.2 0.7 collective-permute-start.1
  83.9 1.0 collective-permute-done.1
  84.9 1.6 mul.32
  86.4 1.9 copy.29
  88.4 1.9 add_convert_fusion
  90.3 16.2 %gather_fusion = bf16[7680,128]{1,0:T(8,128)(2,1)} fusion(bf16[4096,128]{1,0:T(8,128)(2,1)S(1)} %add_convert_fusion, s32[8192]{0:T(1024)S(1)} %pad_clamp_fusion), kind=kCustom, calls=%fused_computation | custom fusion | bytes 3962880 | tf_op jit(solution)/shard_map/gather | solution.py:88
  106.5 9.5 %all-to-all-start.4 = ((bf16[16,480,128]{2,1,0:T(8,128)(2,1)}), bf16[16,480,128]{2,1,0:T(8,128)(2,1)S(1)}, u32[]{:S(2)}, u32[]{:S(2)}) async-start(bf16[16,480,128]{2,1,0:T(8,128)(2,1)} %bitcast.34), calls=%async_computation.4 | async-start | bytes 3932160 | tf_op jit(solution)/shard_map/all_to_all | solution.py:91
  116.2 0.4 reshape.157
  116.7 42.6 %all-to-all-done.4 = bf16[16,480,128]{2,1,0:T(8,128)(2,1)S(1)} async-done(((bf16[16,480,128]{2,1,0:T(8,128)(2,1)}), bf16[16,480,128]{2,1,0:T(8,128)(2,1)S(1)}, u32[]{:S(2)}, u32[]{:S(2)}) %all-to-all-start.4) | async-done | bytes 1966112 | tf_op jit(solution)/shard_map/all_to_all | solution.py:91
  159.3 15.1 %gather_fusion.1 = bf16[5120,128]{1,0:T(8,128)(2,1)S(1)} fusion(bf16[7680,128]{1,0:T(8,128)(2,1)S(1)} %bitcast.31, s32[5120]{0:T(1024)S(1)} %broadcast_clamp_fusion), kind=kCustom, calls=%fused_computation.1 | custom fusion | bytes 2641920 | tf_op jit(solution)/shard_map/gather | solution.py:94
  174.5 1.0 reshape.158
  175.5 2.6 %fusion.5 = bf16[1024,640]{1,0:T(8,128)(2,1)S(1)} fusion(bf16[1024,640]{1,0:T(8,128)(2,1)S(1)} %reshape.158, f32[640]{0:T(1024)S(1)} %get-tuple-element.5, bf16[3,640,640]{2,1,0:T(8,128)(2,1)} %param.21), kind=kOutput, calls=%fused_computation.14 | convolution fusion | flops 842137600 | bytes 4755456 | tf_op jit(solution)/shard_map/dot_general | solution.py:41
  178.1 1.3 fusion.17
  179.4 2.5 %fusion.9 = bf16[1024,640]{1,0:T(8,128)(2,1)} fusion(bf16[1024,640]{1,0:T(8,128)(2,1)S(1)} %reshape.158, bf16[1024,640]{1,0:T(8,128)(2,1)S(1)} %fusion.5, f32[1024,640]{1,0:T(8,128)S(1)} %fusion.17, f32[640]{0:T(1024)S(1)} %get-tuple-element.6, f32[640]{0:T(1024)S(1)} %get-tuple-element.4, bf16[3,640,640]{2,1,0:T(8,128)(2,1)S(1)} %copy-done.8), kind=kOutput, calls=%fused_computation.18 | convolution fusion | flops 850001920 | bytes 12627968 | tf_op jit(solution)/shard_map/dot_general | solution.py:41
  181.9 12.3 %fusion = f32[1,1024]{1,0:T(1,128)} fusion(bf16[4096,1]{0,1:T(2,128)(2,1)S(1)} %reshape.187, f32[4096]{0:T(1024)S(1)} %convert_element_type.91, bf16[1024,640]{1,0:T(8,128)(2,1)} %fusion.9, bf16[640,4096]{1,0:T(8,128)(2,1)} %param.23), kind=kOutput, calls=%fused_computation.4 | convolution fusion | flops 5389680640 | bytes 6582272 | tf_op jit(solution)/shard_map/dot_general | solution.py:48
  (36 shorter events, 1.0 us)
Async XLA Ops:
  22.2 19.4 %all-to-all-start.2 = ((bf16[16,128,128]{2,1,0:T(8,128)(2,1)}), bf16[16,128,128]{2,1,0:T(8,128)(2,1)S(1)}, u32[]{:S(2)}, u32[]{:S(2)}) async-start(bf16[16,128,128]{2,1,0:T(8,128)(2,1)} %param.16), calls=%async_computation.2 | async-start | bytes 1048576 | tf_op jit(solution)/shard_map/all_to_all | solution.py:70
  42.9 13.1 %copy-start.4 = (f32[4096]{0:T(1024)S(1)}, f32[4096]{0:T(1024)}, u32[]{:S(2)}) copy-start(f32[4096]{0:T(1024)} %param.14) | copy-start | bytes 49156
  42.9 13.7 %copy-start.1 = (bf16[4096,128]{1,0:T(8,128)(2,1)S(1)}, bf16[4096,128]{1,0:T(8,128)(2,1)}, u32[]{:S(2)}) copy-start(bf16[4096,128]{1,0:T(8,128)(2,1)} %param.13) | copy-start | bytes 3145732
  63.7 3.4 %copy-start.2 = (s32[16,480]{1,0:T(8,128)S(1)}, s32[16,480]{1,0:T(8,128)}, u32[]{:S(2)}) copy-start(s32[16,480]{1,0:T(8,128)} %param.19) | copy-start | bytes 92164
  66.3 22.1 %collective-permute-start = (bf16[4096,128]{1,0:T(8,128)(2,1)}, bf16[4096,128]{1,0:T(8,128)(2,1)}, u32[]{:S(2)}, u32[]{:S(2)}) collective-permute-start(bf16[4096,128]{1,0:T(8,128)(2,1)} %divide_convert_fusion), channel_id=1, source_target_pairs={{0,1},{1,2},{2,3},{3,4},{4,5},{5,6},{6,7},{7,8},{8,9},{9,10},{10,1... | collective-permute-start | bytes 3145736 | tf_op jit(solution)/shard_map/ppermute | solution.py:12
  83.2 1.7 collective-permute-start.1
  90.3 16.2 %copy-start = (bf16[4096,128]{1,0:T(8,128)(2,1)}, bf16[4096,128]{1,0:T(8,128)(2,1)S(1)}, u32[]{:S(2)}) copy-start(bf16[4096,128]{1,0:T(8,128)(2,1)S(1)} %add_convert_fusion) | copy-start | bytes 3145732
  106.5 9.5 %copy-start.3 = (s32[1024,5]{0,1:T(8,128)S(1)}, s32[1024,5]{0,1:T(8,128)}, u32[]{:S(2)}) copy-start(s32[1024,5]{0,1:T(8,128)} %param.20) | copy-start | bytes 61444
  106.5 10.1 %copy-start.6 = (bf16[4096]{0:T(1024)(128)(2,1)S(1)}, bf16[4096]{0:T(1024)(128)(2,1)}, u32[]{:S(2)}) copy-start(bf16[4096]{0:T(1024)(128)(2,1)} %param.24) | copy-start | bytes 24580
  106.5 10.1 %copy-start.7 = (bf16[4096]{0:T(1024)(128)(2,1)S(1)}, bf16[4096]{0:T(1024)(128)(2,1)}, u32[]{:S(2)}) copy-start(bf16[4096]{0:T(1024)(128)(2,1)} %param.25) | copy-start | bytes 24580
  106.5 10.2 %copy-start.5 = (bf16[3,640]{1,0:T(4,128)(2,1)S(1)}, bf16[3,640]{1,0:T(4,128)(2,1)}, u32[]{:S(2)}) copy-start(bf16[3,640]{1,0:T(4,128)(2,1)} %param.22) | copy-start | bytes 11524
  106.5 52.8 %all-to-all-start.4 = ((bf16[16,480,128]{2,1,0:T(8,128)(2,1)}), bf16[16,480,128]{2,1,0:T(8,128)(2,1)S(1)}, u32[]{:S(2)}, u32[]{:S(2)}) async-start(bf16[16,480,128]{2,1,0:T(8,128)(2,1)} %bitcast.34), calls=%async_computation.4 | async-start | bytes 3932160 | tf_op jit(solution)/shard_map/all_to_all | solution.py:91
  175.5 2.6 %copy-start.8 = (bf16[3,640,640]{2,1,0:T(8,128)(2,1)S(1)}, bf16[3,640,640]{2,1,0:T(8,128)(2,1)}, u32[]{:S(2)}) copy-start(bf16[3,640,640]{2,1,0:T(8,128)(2,1)} %param.21) | copy-start | bytes 7372804
where the time goes:
time: 196 us; the launch traced here: 194 us
  waiting for transfers between devices  57.3 us (29%)
  local copies, waits for them, and re-layouts  42.2 us (22%)
  blocking collectives  36.8 us (19%)
  other arithmetic  22.3 us (11%)
  matrix products  18.6 us (9%)
  starting transfers between devices  16 us (8%)
    all_to_all x1, waiting for transfers between devices, body(): lax.all_to_all(found_rows, 'shard', split_axis=0, concat_axis=0, tiled=True)  42.6 us
    gather x1, local copies, waits for them, and re-layouts, body(): new_serving[lax.all_to_all(routed, 'shard', split_axis=0, concat_axis=0,...  16.2 us
    all_to_all x1, blocking collectives, body(): lax.all_to_all(routed, 'shard', split_axis=0, concat_axis=0, tiled=True)  15.9 us
    gather x1, local copies, waits for them, and re-layouts, body(): fetched.reshape(-1, emb_width)[picked].reshape(request_slots.shape[0], -1)  15.1 us
    all_to_all x1, waiting for transfers between devices, body(): lax.all_to_all(grad_rows, 'shard', split_axis=0, concat_axis=0, tiled=True)  13.7 us
    scatter-add x1, other arithmetic, body(): jnp.zeros((row_count, emb_width), jnp.float32).at[flat_ids].add(values)  12.4 us
    dot_general x1, matrix products, tower_scores(): return jnp.dot(hidden, score_weight, preferred_element_type=jnp.float32)  12.3 us
    all_to_all x1, blocking collectives, body(): lax.all_to_all(grad_counts, 'shard', split_axis=0, concat_axis=0, tiled=T...  11.1 us
  transfers between devices with their start and end apart: 4, of which 3 were waited for; matrix products, arithmetic and copies ran while one was open for 2% of the time, Pallas kernels for 0%

commit v1 on v0

v1 whole, which is shorter than its diff:
```python
import functools
import jax
import jax.numpy as jnp
from jax import lax
from jax.experimental import pallas as pl
from jax.experimental.pallas import tpu as pltpu
from jax.sharding import PartitionSpec as P

LEARN_RATE = 0.5
SCALE_FLOOR = 0.25
LANES = 128
DIGIT = 64
TILE = 256
MIB = 1024 * 1024


def ceil_to(value, unit):
    return -(-value // unit) * unit


def pack_kernel(cap, meta_rows, req_rows, rows_ref, ids_ref, counts_ref, req_ref, out_ref, meta_ref):
    blocks = rows_ref.shape[0]
    f32 = jnp.float32
    out_ref[:, :cap, :] = rows_ref[...]
    meta_ref[...] = jnp.zeros_like(meta_ref)
    slot = lax.broadcasted_iota(jnp.int32, ids_ref.shape, 1)
    ids = ids_ref[...]
    valid = slot < counts_ref[...]
    high = jnp.where(valid, ids // TILE, TILE - 1).astype(f32)
    low = (ids % TILE).astype(f32)
    width = ids.shape[1]
    meta_ref[:, 0, :width] = high
    meta_ref[:, 1, :width] = low
    for row in range(req_rows):
        start = row * LANES
        stop = min(start + LANES, req_ref.shape[1])
        part = req_ref[:, start:stop]
        meta_ref[:, 2 + row, : stop - start] = (part // DIGIT).astype(f32)
        meta_ref[:, 2 + req_rows + row, : stop - start] = (part % DIGIT).astype(f32)
    out_ref[:, cap:, :] = meta_ref[...].astype(jnp.bfloat16)


def update_kernel(
    cap, req_at, req_rows, recv_ref, req_ref, accum_ref, item_ref, serving_ref,
    table_out, accum_out, serving_out, live_out, req_out,
):
    f32, bf16 = jnp.float32, jnp.bfloat16
    blocks = recv_ref.shape[0]
    row_count = item_ref.shape[0]
    req_high = req_ref[:, req_at : req_at + req_rows, :].astype(f32)
    req_low = req_ref[:, req_at + req_rows : req_at + 2 * req_rows, :].astype(f32)
    req_out[...] = (req_high * DIGIT + req_low).astype(jnp.int32)
    values = recv_ref[:, :cap, :].reshape(blocks * cap, LANES)
    row_in_tile = lax.broadcasted_iota(jnp.int32, (TILE, LANES), 0).astype(f32)
    lane = lax.broadcasted_iota(jnp.int32, (TILE, LANES), 1)
    eye = lax.broadcasted_iota(jnp.int32, (LANES, LANES), 0) == lax.broadcasted_iota(
        jnp.int32, (LANES, LANES), 1
    )
    source = lax.broadcasted_iota(jnp.int32, (LANES, LANES), 0)
    target = lax.broadcasted_iota(jnp.int32, (LANES, LANES), 1)
    spread = jnp.where(source == (target // 32) * 32 + 31, 1.0, 0.0).astype(bf16)
    high = [recv_ref[b, cap : cap + 1, :].astype(f32) for b in range(blocks)]
    low = [recv_ref[b, cap + 1 : cap + 2, :].astype(f32) for b in range(blocks)]

    def step(t, carry):
        here = t.astype(f32)
        marks = [
            jnp.where(row_in_tile == jnp.where(high[b] == here, low[b], -1.0), 1.0, 0.0).astype(bf16)
            for b in range(blocks)
        ]
        grad = jnp.dot(jnp.concatenate(marks, axis=1), values, preferred_element_type=f32)
        rows = pl.ds(pl.multiple_of(t * TILE, TILE), TILE)
        mean = jnp.sum(grad * grad, axis=1, keepdims=True) * (1.0 / LANES)
        columns = []
        for half in range(TILE // LANES):
            line = accum_ref[pl.ds(t * (TILE // LANES) + half, 1), :]
            column = jnp.sum(jnp.where(eye, line, 0.0), axis=1, keepdims=True)
            column = column + mean[half * LANES : (half + 1) * LANES]
            accum_out[pl.ds(t * (TILE // LANES) + half, 1), :] = jnp.sum(
                jnp.where(eye, column, 0.0), axis=0, keepdims=True
            )
            columns.append(column)
        accum = jnp.concatenate(columns, axis=0)
        item = item_ref[rows, :].astype(f32)
        fresh = (item - LEARN_RATE * grad / jnp.sqrt(accum)).astype(bf16)
        table_out[rows, :] = fresh
        delta = fresh.astype(f32) - item
        top = jnp.abs(delta)
        for shift in (1, 2, 4, 8, 16):
            top = jnp.maximum(top, pltpu.roll(top, shift, 1))
        scale = jnp.where(lane % 32 == 31, jnp.maximum(top, SCALE_FLOOR), 0.0).astype(bf16)
        scale = jnp.dot(scale, spread, preferred_element_type=f32)
        payload = (delta / scale).astype(bf16)
        serving = (serving_ref[rows, :].astype(f32) + payload.astype(f32) * scale).astype(bf16)
        serving_out[rows, :] = serving
        live_out[rows, :] = serving.astype(f32)
        return carry

    lax.fori_loop(0, row_count // TILE, step, 0)


def gather_kernel(width, pitch, ids_ref, live_ref, out_ref, line_ref):
    blocks = out_ref.shape[0]
    unroll = 8

    def block(b, carry):
        def rows(k, inner):
            for u in range(unroll):
                j = k * unroll + u
                line_ref[pl.ds(j, 1), :] = live_ref[pl.ds(ids_ref[b * pitch + j], 1), :]
            return inner

        lax.fori_loop(0, width // unroll, rows, 0)
        out_ref[b] = line_ref[...].astype(jnp.bfloat16)
        return carry

    lax.fori_loop(0, blocks, block, 0)


def tower_kernel(
    slots_ref, fetched_ref, cross_ref, cross_bias_ref, tower_ref, tower_bias_ref, score_ref,
    out_ref, wide_ref, base_ref, crossed_ref, sum_ref,
):
    f32, bf16 = jnp.float32, jnp.bfloat16
    feats, requests, _ = base_ref.shape
    hidden = tower_ref.shape[1]
    wide_ref[...] = fetched_ref[...].astype(f32)
    unroll = 8

    def collect(k, carry):
        for f in range(feats):
            for u in range(unroll):
                r = k * unroll + u
                base_ref[f, pl.ds(r, 1), :] = wide_ref[pl.ds(slots_ref[f, r], 1), :]
        return carry

    lax.fori_loop(0, requests // unroll, collect, 0)
    for f in range(feats):
        crossed_ref[:, f * LANES : (f + 1) * LANES] = base_ref[f].astype(bf16)
    chunk = 256
    for layer in range(cross_ref.shape[0]):
        def cross(k, carry):
            rows = pl.ds(pl.multiple_of(k * chunk, chunk), chunk)
            old = crossed_ref[rows, :]
            projected = jnp.dot(old, cross_ref[layer], preferred_element_type=f32)
            projected = projected + cross_bias_ref[layer : layer + 1, :].astype(f32)
            base = jnp.concatenate([base_ref[f, rows, :] for f in range(feats)], axis=1)
            crossed_ref[rows, :] = (base * projected + old.astype(f32)).astype(bf16)
            return carry

        lax.fori_loop(0, requests // chunk, cross, 0)
    sum_ref[...] = jnp.zeros_like(sum_ref)

    def tower(k, carry):
        cols = pl.ds(pl.multiple_of(k * chunk, chunk), chunk)
        raw = jnp.dot(crossed_ref[...], tower_ref[:, cols], preferred_element_type=f32)
        raw = jnp.maximum(raw + tower_bias_ref[:, cols].astype(f32), 0.0)
        raw = raw * score_ref[:, cols].astype(f32)
        sum_ref[...] += raw[:, :LANES] + raw[:, LANES:]
        return carry

    lax.fori_loop(0, hidden // chunk, tower, 0)
    eye = lax.broadcasted_iota(jnp.int32, (LANES, LANES), 0) == lax.broadcasted_iota(
        jnp.int32, (LANES, LANES), 1
    )
    for k in range(requests // LANES):
        column = jnp.sum(sum_ref[k * LANES : (k + 1) * LANES, :], axis=1, keepdims=True)
        out_ref[k : k + 1, :] = jnp.sum(jnp.where(eye, column, 0.0), axis=0, keepdims=True)


def body(
    item_table, row_accum, serving_table, grad_rows, grad_ids, grad_counts, request_ids,
    request_slots, cross_weight, cross_bias, tower_weight, tower_bias, score_weight,
):
    f32, bf16 = jnp.float32, jnp.bfloat16
    shards = lax.axis_size("shard")
    row_count, emb = item_table.shape
    cap, capr = grad_ids.shape[1], request_ids.shape[1]
    requests, feats = request_slots.shape
    req_rows = ceil_to(capr, LANES) // LANES
    meta_rows = ceil_to(2 + 2 * req_rows, 16)
    vmem = pl.BlockSpec(memory_space=pltpu.VMEM)
    smem = pl.BlockSpec(memory_space=pltpu.SMEM)
    params = functools.partial(pltpu.CompilerParams, vmem_limit_bytes=40 * MIB)

    behind = [(i, (i - 1) % shards) for i in range(shards)]
    ahead = [(i, (i + 1) % shards) for i in range(shards)]
    serving_here = lax.ppermute(serving_table, "shard", behind)

    packed = pl.pallas_call(
        functools.partial(pack_kernel, cap, meta_rows, req_rows),
        out_shape=jax.ShapeDtypeStruct((shards, cap + meta_rows, emb), bf16),
        in_specs=[vmem] * 4,
        out_specs=vmem,
        scratch_shapes=[pltpu.VMEM((shards, meta_rows, LANES), f32)],
        compiler_params=params(),
        name="pack",
    )(grad_rows, grad_ids, grad_counts.reshape(shards, 1), request_ids)
    recv = lax.all_to_all(packed, "shard", split_axis=0, concat_axis=0, tiled=True)

    joined = recv
    if cap < LANES:
        groups = shards * cap // LANES
        marks = recv[:, cap : cap + 2, :cap].reshape(groups, LANES // cap, 2, cap)
        marks = marks.transpose(0, 2, 1, 3).reshape(groups, 2, LANES)
        marks = jnp.pad(marks, ((0, 0), (0, 14), (0, 0)))
        joined = jnp.concatenate([recv[:, :cap, :].reshape(groups, LANES, emb), marks], axis=1)

    new_table, new_accum, serving_next, live, req = pl.pallas_call(
        functools.partial(update_kernel, LANES, cap + 2, req_rows),
        out_shape=(
            jax.ShapeDtypeStruct((row_count, emb), bf16),
            jax.ShapeDtypeStruct((row_count // LANES, LANES), f32),
            jax.ShapeDtypeStruct((row_count, emb), bf16),
            jax.ShapeDtypeStruct((row_count, emb), f32),
            jax.ShapeDtypeStruct((shards, req_rows, LANES), jnp.int32),
        ),
        in_specs=[vmem] * 5,
        out_specs=(vmem,) * 5,
        compiler_params=params(),
        name="update",
    )(joined, recv, row_accum.reshape(-1, LANES), item_table, serving_here)

    found = pl.pallas_call(
        functools.partial(gather_kernel, capr, req_rows * LANES),
        out_shape=jax.ShapeDtypeStruct((shards, capr, emb), bf16),
        in_specs=[smem, vmem],
        out_specs=vmem,
        scratch_shapes=[pltpu.VMEM((capr, emb), f32)],
        compiler_params=params(),
        name="gather",
    )(req.reshape(-1), live)
    fetched = lax.all_to_all(found, "shard", split_axis=0, concat_axis=0, tiled=True)
    new_serving = lax.ppermute(serving_next, "shard", ahead)

    scores = pl.pallas_call(
        tower_kernel,
        out_shape=jax.ShapeDtypeStruct((requests // LANES, LANES), f32),
        in_specs=[smem] + [vmem] * 6,
        out_specs=vmem,
        scratch_shapes=[
            pltpu.VMEM((shards * capr, emb), f32),
            pltpu.VMEM((feats, requests, emb), f32),
            pltpu.VMEM((requests, feats * emb), bf16),
            pltpu.VMEM((requests, LANES), f32),
        ],
        compiler_params=params(),
        name="tower",
    )(
        request_slots.T, fetched.reshape(shards * capr, emb), cross_weight, cross_bias, tower_weight,
        tower_bias.reshape(1, -1), score_weight.reshape(1, -1),
    )
    return (new_table, new_accum.reshape(row_count), new_serving, scores.reshape(requests))


def solution(mesh):
    both = ("groups", "shard")
    in_specs = (
        P("shard", None), P("shard"), P("shard", None), P(both, None, None), P(both, None), P(both),
        P(both, None), P(both, None), P(), P(), P(), P(), P(),
    )
    out_specs = (P(both, None), P(both), P(both, None), P(both))
    return jax.shard_map(body, mesh=mesh, in_specs=in_specs, out_specs=out_specs, check_vma=False)
```

time: 196 us -> 166 us (0.85)
  Pallas kernels: 0 us -> 58.5 us
  blocking collectives: 36.8 us -> 0 us
  local copies, waits for them, and re-layouts: 42.2 us -> 12.1 us
  other arithmetic: 22.3 us -> 0 us
  waiting for transfers between devices: 57.3 us -> 76.9 us
  matrix products: 18.6 us -> 0 us
    pallas_call x0 -> x4, Pallas kernels: none -> 58.5 us  [the longest x1 24.5 us: body(): pl.pallas_call(tower_kernel, out_shape=jax.ShapeDtypeStruct((requests //...]
    ppermute x2, waiting for transfers between devices: 1.01 us -> 43.1 us  [the longest x1 23.6 us: body(): new_serving = lax.ppermute(serving_next, 'shard', ahead)]
    all_to_all x3 -> x0, blocking collectives: 36.8 us -> none  [the longest x1 15.9 us: body(): lax.all_to_all(routed, 'shard', split_axis=0, concat_axis=0, tiled=True)]
    gather x2 -> x0, local copies, waits for them, and re-layouts: 31.3 us -> none  [the longest x1 16.2 us: body(): new_serving[lax.all_to_all(routed, 'shard', split_axis=0, concat_axis=0,...]
    all_to_all x2, waiting for transfers between devices: 56.3 us -> 33.8 us  [the longest x1 29.5 us: body(): lax.all_to_all(found, 'shard', split_axis=0, concat_axis=0, tiled=True)]
    dot_general x4 -> x0, matrix products: 18.6 us -> none  [the longest x1 12.3 us: tower_scores(): return jnp.dot(hidden, score_weight, preferred_element_type=jnp.float32)]
    scatter-add x1 -> x0, other arithmetic: 12.4 us -> none  [body(): jnp.zeros((row_count, emb_width), jnp.float32).at[flat_ids].add(values)]
    unnamed x19 -> x29, local copies, waits for them, and re-layouts: 0.06 us -> 11.2 us
  transfers between devices with their start and end apart: 4 -> 4, of which waited for: 3 -> 4; matrix products, arithmetic and copies ran while one was open for 2% -> 0% of each run, Pallas kernels for 0% -> 0%
where the time goes in v1:
time: 166 us; the launch traced here: 164 us
  waiting for transfers between devices  76.9 us (46%)
  Pallas kernels  58.5 us (35%)
  starting transfers between devices  15.6 us (9%)
  local copies, waits for them, and re-layouts  12.1 us (7%)
    all_to_all x1, waiting for transfers between devices, body(): lax.all_to_all(found, 'shard', split_axis=0, concat_axis=0, tiled=True)  29.5 us
    pallas_call x1, Pallas kernels, body(): pl.pallas_call(tower_kernel, out_shape=jax.ShapeDtypeStruct((requests //...  24.5 us
    ppermute x1, waiting for transfers between devices, body(): new_serving = lax.ppermute(serving_next, 'shard', ahead)  23.6 us
    ppermute x1, waiting for transfers between devices, body(): serving_here = lax.ppermute(serving_table, 'shard', behind)  19.5 us
    pallas_call x1, Pallas kernels, body(): pl.pallas_call(functools.partial(update_kernel, LANES, cap + 2, req_rows)...  18.6 us
    pallas_call x1, Pallas kernels, body(): pl.pallas_call(functools.partial(gather_kernel, capr, req_rows * LANES),...  14.4 us
    unnamed x29, local copies, waits for them, and re-layouts  11.2 us
    all_to_all x1, starting transfers between devices, body(): lax.all_to_all(found, 'shard', split_axis=0, concat_axis=0, tiled=True)  7.1 us
  transfers between devices with their start and end apart: 4, of which 4 were waited for; matrix products, arithmetic and copies ran while one was open for 0% of the time, Pallas kernels for 0%

profile of v1, /device:TPU:9, one launch (start us, length us, event | category | flops | bytes accessed | tf_op | source)
XLA Modules:
  0.0 163.8 jit_solution(14268124466048397966)
XLA Ops:
  0.6 0.0 copy-start.3
  0.6 0.8 copy.17.counts_ref
  1.5 0.0 copy-start.4
  1.5 1.0 copy-done.4
  2.5 0.8 copy-done.6
  3.3 0.7 copy-done.8
  4.0 0.9 pack.1
  4.9 6.6 %all-to-all-start = ((bf16[16,144,128]{2,1,0:T(8,128)(2,1)}), bf16[16,144,128]{2,1,0:T(8,128)(2,1)S(1)}, u32[]{:S(2)}, u32[]{:S(2)}) async-start(bf16[16,144,128]{2,1,0:T(8,128)(2,1)} %pack.1), calls=%async_computation | async-start | bytes 1179648 | tf_op jit(solution)/shard_map/all_to_all | solution.py:199
  11.5 0.4 collective-permute-start
  11.9 19.5 %collective-permute-done.serving_ref = bf16[4096,128]{1,0:T(8,128)(2,1)S(1)} collective-permute-done((bf16[4096,128]{1,0:T(8,128)(2,1)}, bf16[4096,128]{1,0:T(8,128)(2,1)S(1)}, u32[]{:S(2)}, u32[]{:S(2)}) %collective-permute-start) | collective-permute-done | bytes 1048608 | tf_op jit(solution)/shard_map/ppermute | solution.py:188
  31.4 4.4 %all-to-all-done.recv_ref.req_ref = bf16[16,144,128]{2,1,0:T(8,128)(2,1)S(1)} async-done(((bf16[16,144,128]{2,1,0:T(8,128)(2,1)}), bf16[16,144,128]{2,1,0:T(8,128)(2,1)S(1)}, u32[]{:S(2)}, u32[]{:S(2)}) %all-to-all-start) | async-done | bytes 589856 | tf_op jit(solution)/shard_map/all_to_all | solution.py:199
  35.8 0.0 copy-done.3
  35.8 0.0 copy-done.7
  35.8 18.6 %update.1 = (bf16[4096,128]{1,0:T(8,128)(2,1)}, f32[32,128]{1,0:T(8,128)}, bf16[4096,128]{1,0:T(8,128)(2,1)S(1)}, f32[4096,128]{1,0:T(8,128)S(1)}, s32[16,4,128]{2,1,0:T(4,128)S(1)}) custom-call(bf16[16,144,128]{2,1,0:T(8,128)(2,1)S(1)} %all-to-all-done.recv_ref.req_ref, bf16[16,144,128]{2,1,0:T(8,128)(2,1)S(1)} %all-to-all-done.recv_ref.req_ref, ...), custom_call_target="tpu_custom_call" | custom-call | tf_op jit(solution)/shard_map/update/pallas_call | solution.py:209
  54.4 1.0 copy-done.10
  55.3 14.4 %gather.1 = bf16[16,480,128]{2,1,0:T(8,128)(2,1)S(1)} custom-call(s32[8192]{0:T(1024)S(1)} %bitcast.9, f32[4096,128]{1,0:T(8,128)S(1)} %get-tuple-element.13.live_ref), custom_call_target="tpu_custom_call" | custom-call | tf_op jit(solution)/shard_map/gather/pallas_call | solution.py:224
  69.8 0.0 copy-start
  69.8 1.3 copy-done
  71.1 0.0 copy-start.9
  71.1 7.1 %all-to-all-start.1 = ((bf16[16,480,128]{2,1,0:T(8,128)(2,1)}), bf16[16,480,128]{2,1,0:T(8,128)(2,1)S(1)}, u32[]{:S(2)}, u32[]{:S(2)}) async-start(bf16[16,480,128]{2,1,0:T(8,128)(2,1)} %copy-done), calls=%async_computation.1 | async-start | bytes 3932160 | tf_op jit(solution)/shard_map/all_to_all | solution.py:233
  78.2 0.0 copy-done.11
  78.2 1.5 collective-permute-start.1
  79.7 0.0 copy-done.12
  79.7 0.0 copy-done.13
  79.7 23.6 %collective-permute-done.1 = bf16[4096,128]{1,0:T(8,128)(2,1)} collective-permute-done((bf16[4096,128]{1,0:T(8,128)(2,1)S(1)}, bf16[4096,128]{1,0:T(8,128)(2,1)}, u32[]{:S(2)}, u32[]{:S(2)}) %collective-permute-start.1) | collective-permute-done | bytes 1048608 | tf_op jit(solution)/shard_map/ppermute | solution.py:234
  103.3 29.5 %all-to-all-done.1 = bf16[16,480,128]{2,1,0:T(8,128)(2,1)S(1)} async-done(((bf16[16,480,128]{2,1,0:T(8,128)(2,1)}), bf16[16,480,128]{2,1,0:T(8,128)(2,1)S(1)}, u32[]{:S(2)}, u32[]{:S(2)}) %all-to-all-start.1) | async-done | bytes 1966112 | tf_op jit(solution)/shard_map/all_to_all | solution.py:233
  132.8 0.0 copy-done.5
  132.8 0.0 copy-done.9
  132.8 2.5 %copy-done.1 = bf16[640,4096]{1,0:T(8,128)(2,1)S(1)} copy-done((bf16[640,4096]{1,0:T(8,128)(2,1)S(1)}, bf16[640,4096]{1,0:T(8,128)(2,1)}, u32[]{:S(2)}) %copy-start.1) | copy-done | bytes 5242904
  135.3 1.7 %copy-done.2 = bf16[3,640,640]{2,1,0:T(8,128)(2,1)S(1)} copy-done((bf16[3,640,640]{2,1,0:T(8,128)(2,1)S(1)}, bf16[3,640,640]{2,1,0:T(8,128)(2,1)}, u32[]{:S(2)}) %copy-start.2) | copy-done | bytes 2457624
  137.0 24.5 %tower.1 = f32[8,128]{1,0:T(8,128)} custom-call(s32[5,1024]{1,0:T(8,128)S(1)} %bitcast.8, bf16[7680,128]{1,0:T(8,128)(2,1)S(1)} %bitcast.7, bf16[3,640,640]{2,1,0:T(8,128)(2,1)S(1)} %copy-done.2, bf16[3,640]{1,0:T(4,128)(2,1)S(1)} %copy-done.9, bf16[640,4096]{1,0:T(8,128)(2,1)S(1)} %copy-done.1, bf16[1,4096]{1,0:T(2,128)(2,1)S(1)} %reshape.37.tower_bias_ref, ...), custom_call_target="tpu_custom_call" | custom-call | tf_op jit(solution)/shard_map/tower/pallas_call | solution.py:236
  161.5 2.3 %copy.19 = bf16[4096,128]{1,0:T(8,128)(2,1)} copy(bf16[4096,128]{1,0:T(8,128)(2,1)} %collective-permute-done.1) | data formatting | bytes 2097152
  (12 shorter events, 0.0 us)
Async XLA Ops:
  0.6 35.1 %copy-start.3 = (bf16[4096,128]{1,0:T(8,128)(2,1)S(1)}, bf16[4096,128]{1,0:T(8,128)(2,1)}, u32[]{:S(2)}) copy-start(bf16[4096,128]{1,0:T(8,128)(2,1)} %item_ref.1) | copy-start | bytes 3145732
  1.5 1.0 copy-start.4
  2.5 0.8 copy-start.6
  3.3 0.7 copy-start.8
  4.0 31.8 %copy-start.7 = (f32[4096]{0:T(1024)S(1)}, f32[4096]{0:T(1024)}, u32[]{:S(2)}) copy-start(f32[4096]{0:T(1024)} %param.14) | copy-start | bytes 49156
  4.9 30.9 %all-to-all-start = ((bf16[16,144,128]{2,1,0:T(8,128)(2,1)}), bf16[16,144,128]{2,1,0:T(8,128)(2,1)S(1)}, u32[]{:S(2)}, u32[]{:S(2)}) async-start(bf16[16,144,128]{2,1,0:T(8,128)(2,1)} %pack.1), calls=%async_computation | async-start | bytes 1179648 | tf_op jit(solution)/shard_map/all_to_all | solution.py:199
  11.5 19.9 %collective-permute-start = (bf16[4096,128]{1,0:T(8,128)(2,1)}, bf16[4096,128]{1,0:T(8,128)(2,1)S(1)}, u32[]{:S(2)}, u32[]{:S(2)}) collective-permute-start(bf16[4096,128]{1,0:T(8,128)(2,1)} %param.15), channel_id=1, source_target_pairs={{0,15},{1,0},{2,1},{3,2},{4,3},{5,4},{6,5},{7,6},{8,7},{9,8},{10,9... | collective-permute-start | bytes 3145736 | tf_op jit(solution)/shard_map/ppermute | solution.py:188
  54.4 1.0 copy-start.10
  69.8 1.3 copy-start
  71.1 7.1 %copy-start.11 = (bf16[4096,128]{1,0:T(8,128)(2,1)S(1)}, bf16[4096,128]{1,0:T(8,128)(2,1)}, u32[]{:S(2)}) copy-start(bf16[4096,128]{1,0:T(8,128)(2,1)} %copy-done.10) | copy-start | bytes 3145732
  71.1 8.6 %copy-start.12 = (bf16[4096]{0:T(1024)(128)(2,1)S(1)}, bf16[4096]{0:T(1024)(128)(2,1)}, u32[]{:S(2)}) copy-start(bf16[4096]{0:T(1024)(128)(2,1)} %param.24) | copy-start | bytes 24580
  71.1 8.6 %copy-start.13 = (bf16[4096]{0:T(1024)(128)(2,1)S(1)}, bf16[4096]{0:T(1024)(128)(2,1)}, u32[]{:S(2)}) copy-start(bf16[4096]{0:T(1024)(128)(2,1)} %param.25) | copy-start | bytes 24580
  71.1 61.7 %copy-start.5 = (s32[1024,5]{0,1:T(8,128)S(1)}, s32[1024,5]{0,1:T(8,128)}, u32[]{:S(2)}) copy-start(s32[1024,5]{0,1:T(8,128)} %param.20) | copy-start | bytes 61444
  71.1 61.7 %copy-start.9 = (bf16[3,640]{1,0:T(4,128)(2,1)S(1)}, bf16[3,640]{1,0:T(4,128)(2,1)}, u32[]{:S(2)}) copy-start(bf16[3,640]{1,0:T(4,128)(2,1)} %cross_bias_ref.1) | copy-start | bytes 11524
  71.1 61.7 %all-to-all-start.1 = ((bf16[16,480,128]{2,1,0:T(8,128)(2,1)}), bf16[16,480,128]{2,1,0:T(8,128)(2,1)S(1)}, u32[]{:S(2)}, u32[]{:S(2)}) async-start(bf16[16,480,128]{2,1,0:T(8,128)(2,1)} %copy-done), calls=%async_computation.1 | async-start | bytes 3932160 | tf_op jit(solution)/shard_map/all_to_all | solution.py:233
  78.2 25.1 %collective-permute-start.1 = (bf16[4096,128]{1,0:T(8,128)(2,1)S(1)}, bf16[4096,128]{1,0:T(8,128)(2,1)}, u32[]{:S(2)}, u32[]{:S(2)}) collective-permute-start(bf16[4096,128]{1,0:T(8,128)(2,1)S(1)} %copy-done.11), channel_id=1, source_target_pairs={{0,1},{1,2},{2,3},{3,4},{4,5},{5,6},{6,7},{7,8},{8,9},{9,10},{10,1... | collective-permute-start | bytes 3145736 | tf_op jit(solution)/shard_map/ppermute | solution.py:234
  132.8 2.5 %copy-start.1 = (bf16[640,4096]{1,0:T(8,128)(2,1)S(1)}, bf16[640,4096]{1,0:T(8,128)(2,1)}, u32[]{:S(2)}) copy-start(bf16[640,4096]{1,0:T(8,128)(2,1)} %tower_ref.1) | copy-start | bytes 15728644
  135.3 1.7 %copy-start.2 = (bf16[3,640,640]{2,1,0:T(8,128)(2,1)S(1)}, bf16[3,640,640]{2,1,0:T(8,128)(2,1)}, u32[]{:S(2)}) copy-start(bf16[3,640,640]{2,1,0:T(8,128)(2,1)} %cross_ref.1) | copy-start | bytes 7372804

commit v2 on v1

v2 whole, which is shorter than its diff:
```python
import functools
import jax
import jax.numpy as jnp
from jax import lax
from jax.experimental import pallas as pl
from jax.experimental.pallas import tpu as pltpu
from jax.sharding import PartitionSpec as P

LEARN_RATE = 0.5
SCALE_FLOOR = 0.25
LANES = 128
DIGIT = 64
TILE = 256
BIG = 2048
MIB = 1024 * 1024


def ceil_to(value, unit):
    return -(-value // unit) * unit


SENDS = ((8,), (9, 1, 10), (2, 11, 3), (12, 4, 13), (5, 14, 6), (15, 7))
TAKES = ((8, 9, 1), (10, 2, 11), (3, 12, 4), (13, 5, 14))


def work(micros):
    return pl.CostEstimate(flops=0, transcendentals=0, bytes_accessed=int(micros * 3.0e6))


def pack_kernel(cap, req_rows, rows_hbm, ids_hbm, req_hbm, counts_ref, out_ref, ids_ref, req_ref, meta_ref, sems):
    f32 = jnp.float32
    loads = [
        pltpu.make_async_copy(ids_hbm, ids_ref, sems.at[0]),
        pltpu.make_async_copy(req_hbm, req_ref, sems.at[1]),
        pltpu.make_async_copy(rows_hbm, out_ref.at[:, :cap, :], sems.at[2]),
    ]
    for load in loads:
        load.start()
    meta_ref[...] = jnp.zeros_like(meta_ref)
    slot = lax.broadcasted_iota(jnp.int32, ids_ref.shape, 1)
    block = lax.broadcasted_iota(jnp.int32, ids_ref.shape, 0)
    count = jnp.zeros(ids_ref.shape, jnp.int32)
    for b in range(ids_ref.shape[0]):
        count = jnp.where(block == b, counts_ref[b], count)
    loads[0].wait()
    ids = ids_ref[...]
    width = ids.shape[1]
    meta_ref[:, 0, :width] = jnp.where(slot < count, ids // TILE, TILE - 1).astype(f32)
    meta_ref[:, 1, :width] = (ids % TILE).astype(f32)
    loads[1].wait()
    for row in range(req_rows):
        start = row * LANES
        stop = min(start + LANES, req_ref.shape[1])
        part = req_ref[:, start:stop]
        meta_ref[:, 2 + row, : stop - start] = (part // DIGIT).astype(f32)
        meta_ref[:, 2 + req_rows + row, : stop - start] = (part % DIGIT).astype(f32)
    out_ref[:, cap:, :] = meta_ref[...].astype(jnp.bfloat16)
    loads[2].wait()


def update_kernel(
    cap, req_at, req_rows, recv_ref, req_ref, accum_ref, item_hbm,
    table_hbm, accum_out, change_out, req_out, pair_ref, grad_ref, item_ref, table_out, sems,
):
    load_item = pltpu.make_async_copy(item_hbm, item_ref, sems.at[0])
    load_item.start()
    f32, bf16 = jnp.float32, jnp.bfloat16
    blocks = recv_ref.shape[0]
    row_count = item_hbm.shape[0]
    half_tiles = row_count // TILE // 2
    req_high = req_ref[:, req_at : req_at + req_rows, :].astype(f32)
    req_low = req_ref[:, req_at + req_rows : req_at + 2 * req_rows, :].astype(f32)
    req_out[...] = (req_high * DIGIT + req_low).astype(jnp.int32)
    eye = lax.broadcasted_iota(jnp.int32, (LANES, LANES), 0) == lax.broadcasted_iota(
        jnp.int32, (LANES, LANES), 1
    )
    eye_mark = jnp.where(eye, 1.0, 0.0).astype(bf16)
    ones = jnp.ones((LANES, LANES), bf16)
    keys = []
    for b in range(blocks):
        high = recv_ref[b, cap : cap + 1, :].astype(f32)
        low = recv_ref[b, cap + 1 : cap + 2, :].astype(f32)
        upper = high >= half_tiles
        keys.append((jnp.where(upper, high - half_tiles, high), low))
        spots = jnp.where(eye, jnp.where(upper, 1.0, 0.0), 0.0).astype(bf16)
        side = jnp.dot(spots, ones, preferred_element_type=f32)
        rows = recv_ref[b, :cap, :].astype(f32)
        pair_ref[b * cap : (b + 1) * cap, :LANES] = jnp.where(side > 0.5, 0.0, rows).astype(bf16)
        pair_ref[b * cap : (b + 1) * cap, LANES:] = jnp.where(side > 0.5, rows, 0.0).astype(bf16)
    row_in_tile = lax.broadcasted_iota(jnp.int32, (TILE, LANES), 0).astype(jnp.int16)
    mark, blank = jnp.ones((), bf16), jnp.zeros((), bf16)
    lines = lax.broadcasted_iota(jnp.int32, (8, LANES), 0)
    spread = jnp.where(lines == lax.broadcasted_iota(jnp.int32, (8, LANES), 1) // 32, 1.0, 0.0)
    spread = spread.astype(bf16)
    part = lax.broadcasted_iota(jnp.int32, (4 * LANES, LANES), 0)
    weigh = jnp.where(part < 2 * LANES, 1.0 / LANES, 1.0).astype(bf16)

    def scatter(t, carry):
        here = t.astype(f32)
        marks = []
        for high, low in keys:
            key = jnp.where(high == here, low, -1.0).astype(jnp.int16)
            marks.append(jnp.where(row_in_tile == jnp.broadcast_to(key, (TILE, LANES)), mark, blank))
        grad = jnp.dot(jnp.concatenate(marks, axis=1), pair_ref[...], preferred_element_type=f32)
        rows = pl.multiple_of(t * TILE, TILE)
        grad_ref[pl.ds(rows, TILE), :] = grad[:, :LANES]
        grad_ref[pl.ds(rows + row_count // 2, TILE), :] = grad[:, LANES:]
        return carry

    lax.fori_loop(0, half_tiles, scatter, 0, unroll=2)

    def adagrad(k, carry):
        rows = pl.ds(pl.multiple_of(k * BIG, BIG), BIG)
        grad = grad_ref[rows, :]
        square = grad * grad
        coarse = square.astype(bf16)
        rest = (square - coarse.astype(f32)).astype(bf16)
        lines = [accum_ref[pl.ds(k * (BIG // LANES) + q, 1), :] for q in range(BIG // LANES)]
        upper = [line.astype(bf16).astype(f32) for line in lines]
        olds = [
            jnp.concatenate([jnp.where(eye, line, 0.0) for line in part], axis=0).astype(bf16)
            for part in (upper, [line - high for line, high in zip(lines, upper)])
        ]
        accum = jnp.dot(
            jnp.concatenate([coarse, rest, *olds], axis=1), weigh, preferred_element_type=f32
        )
        for q in range(BIG // LANES):
            mine = jnp.where(eye, accum[q * LANES : (q + 1) * LANES], 0.0)
            accum_out[pl.ds(k * (BIG // LANES) + q, 1), :] = jnp.sum(mine, axis=0, keepdims=True)
        item = item_ref[rows, :].astype(f32)
        table_out[rows, :] = (item - LEARN_RATE * grad * lax.rsqrt(accum)).astype(bf16)
        return carry

    load_item.wait()
    lax.fori_loop(0, row_count // BIG, adagrad, 0)
    store_table = pltpu.make_async_copy(table_out, table_hbm, sems.at[1])
    store_table.start()

    def publish(k, carry):
        rows = pl.ds(pl.multiple_of(k * BIG, BIG), BIG)
        delta = table_out[rows, :].astype(f32) - item_ref[rows, :].astype(f32)
        turned = lax.dot_general(
            eye_mark, jnp.abs(delta).astype(bf16), (((1,), (1,)), ((), ())),
            preferred_element_type=f32,
        )
        top = jnp.max(turned.reshape(LANES // 32, 32, BIG), axis=1)
        top = jnp.concatenate([jnp.maximum(top, SCALE_FLOOR), jnp.zeros((4, BIG), f32)], axis=0)
        scale = lax.dot_general(
            top.astype(bf16), spread, (((0,), (0,)), ((), ())), preferred_element_type=f32
        )
        payload = (delta / scale).astype(bf16)
        change_out[rows, :] = payload.astype(f32) * scale
        return carry

    lax.fori_loop(0, row_count // BIG, publish, 0)
    store_table.wait()


def apply_kernel(change_ref, serving_ref, serving_out, live_out):
    f32 = jnp.float32
    serving = (serving_ref[...].astype(f32) + change_ref[...]).astype(jnp.bfloat16)
    serving_out[...] = serving
    live_out[...] = serving.astype(f32)


def unroll_of(width):
    for unroll in (64, 32, 16):
        if width % unroll == 0:
            return unroll
    return width


def copy_rows(from_ref, ids_ref, ids_at, to_ref, to_at, count):
    unroll = unroll_of(count)

    def some(k, carry):
        at = k * unroll
        rows = [from_ref[pl.ds(ids_ref[ids_at + at + u], 1), :] for u in range(unroll)]
        for u in range(unroll):
            to_ref[pl.ds(to_at + at + u, 1), :] = rows[u]
        return carry

    lax.fori_loop(0, count // unroll, some, 0)


def gather_kernel(moves, pitch, me_ref, ids_ref, live_ref, *outs):
    width = outs[0].shape[0]
    unroll = unroll_of(width)
    for move, out_ref in zip(moves, outs):
        start = lax.bitwise_xor(me_ref[0], move) * pitch

        def some(k, carry):
            at = start + k * unroll
            rows = [live_ref[pl.ds(ids_ref[at + u], 1), :] for u in range(unroll)]
            out_ref[pl.ds(pl.multiple_of(k * unroll, unroll), unroll), :] = jnp.concatenate(
                rows, axis=0
            ).astype(jnp.bfloat16)
            return carry

        lax.fori_loop(0, width // unroll, some, 0)


def gather_all_kernel(pitch, ids_ref, live_ref, out_ref):
    blocks, width, _ = out_ref.shape

    def block(b, carry):
        rows = [live_ref[pl.ds(ids_ref[b * pitch + u], 1), :] for u in range(width)]
        out_ref[b] = jnp.concatenate(rows, axis=0).astype(jnp.bfloat16)
        return carry

    lax.fori_loop(0, blocks, block, 0)


def token_kernel(token_ref, *refs):
    refs[-1][...] = token_ref[...]


def tower_kernel(
    moves, shape, pitch, token_ref, me_ref, ids_ref, slots_ref, live_ref, cross_hbm, cross_bias_ref, tower_hbm,
    tower_bias_ref, score_ref, serving_ref, *refs,
):
    f32, bf16 = jnp.float32, jnp.bfloat16
    feats, requests = shape
    pieces = refs[:-10]
    out_ref, serving_out, cross_ref, tower_ref, got_ref, served_ref = refs[-10:-4]
    wide_ref, plane_ref, crossed_ref, sems = refs[-4:]
    me = me_ref[0]
    loads = []
    for k, piece in enumerate(pieces):
        start, width = 0, piece.shape[0]
        if moves is not None:
            start = pl.multiple_of(lax.bitwise_xor(me, moves[k]) * width, width)
        loads.append(
            pltpu.make_async_copy(piece, got_ref.at[pl.ds(start, width), :], sems.at[4 + k])
        )
    load_cross = pltpu.make_async_copy(cross_hbm, cross_ref, sems.at[0])
    load_tower = pltpu.make_async_copy(tower_hbm, tower_ref, sems.at[1])
    load_serving = pltpu.make_async_copy(serving_ref, served_ref, sems.at[2])
    store_serving = pltpu.make_async_copy(served_ref, serving_out, sems.at[3])
    for load in loads:
        load.start()
    load_cross.start()
    load_serving.start()
    load_tower.start()
    for load in loads:
        load.wait()
    wide_ref[...] = got_ref[...].astype(f32)
    if moves is not None:
        width = pieces[0].shape[0]
        copy_rows(live_ref, ids_ref, me * pitch, wide_ref, me * width, width)
    load_serving.wait()
    store_serving.start()
    copy_rows(wide_ref, slots_ref, 0, plane_ref, 0, feats * requests)
    for f in range(feats):
        crossed_ref[:, f * LANES : (f + 1) * LANES] = plane_ref[
            f * requests : (f + 1) * requests, :
        ].astype(bf16)
    load_cross.wait()
    for layer in range(cross_ref.shape[0]):
        old = crossed_ref[...]
        projected = jnp.dot(old, cross_ref[layer], preferred_element_type=f32)
        projected = projected + cross_bias_ref[layer : layer + 1, :].astype(f32)
        for f in range(feats):
            cols = slice(f * LANES, (f + 1) * LANES)
            base = plane_ref[f * requests : (f + 1) * requests, :]
            crossed_ref[:, cols] = (base * projected[:, cols] + old[:, cols].astype(f32)).astype(bf16)
    load_tower.wait()
    hidden = tower_ref.shape[1]
    chunk = 1024
    total = jnp.zeros((requests, LANES), f32)
    for start in range(0, hidden, chunk):
        cols = slice(start, start + chunk)
        raw = jnp.dot(crossed_ref[...], tower_ref[:, cols], preferred_element_type=f32)
        raw = jnp.maximum(raw + tower_bias_ref[:, cols].astype(f32), 0.0)
        raw = raw * score_ref[:, cols].astype(f32)
        for q in range(chunk // LANES):
            total = total + raw[:, q * LANES : (q + 1) * LANES]
    eye = lax.broadcasted_iota(jnp.int32, (LANES, LANES), 0) == lax.broadcasted_iota(
        jnp.int32, (LANES, LANES), 1
    )
    for k in range(requests // LANES):
        column = jnp.sum(total[k * LANES : (k + 1) * LANES, :], axis=1, keepdims=True)
        out_ref[k : k + 1, :] = jnp.sum(jnp.where(eye, column, 0.0), axis=0, keepdims=True)
    store_serving.wait()


def body(
    item_table, row_accum, serving_table, grad_rows, grad_ids, grad_counts, request_ids,
    request_slots, cross_weight, cross_bias, tower_weight, tower_bias, score_weight,
):
    f32, bf16 = jnp.float32, jnp.bfloat16
    shards = lax.axis_size("shard")
    row_count, emb = item_table.shape
    cap, capr = grad_ids.shape[1], request_ids.shape[1]
    requests, feats = request_slots.shape
    req_rows = ceil_to(capr, LANES) // LANES
    meta_rows = ceil_to(2 + 2 * req_rows, 16)
    vmem = pl.BlockSpec(memory_space=pltpu.VMEM)
    smem = pl.BlockSpec(memory_space=pltpu.SMEM)
    hbm = pl.BlockSpec(memory_space=pltpu.HBM)

    def call(kernel, name, limit, **kwargs):
        params = pltpu.CompilerParams(vmem_limit_bytes=limit * MIB)
        return pl.pallas_call(kernel, name=name, compiler_params=params, **kwargs)

    packed = call(
        functools.partial(pack_kernel, cap, req_rows), "pack", 56,
        out_shape=jax.ShapeDtypeStruct((shards, cap + meta_rows, emb), bf16),
        in_specs=[hbm, hbm, hbm, smem],
        out_specs=vmem,
        scratch_shapes=[
            pltpu.VMEM((shards, cap), jnp.int32),
            pltpu.VMEM((shards, capr), jnp.int32),
            pltpu.VMEM((shards, meta_rows, LANES), f32),
            pltpu.SemaphoreType.DMA((3,)),
        ],
    )(grad_rows, grad_ids, request_ids, grad_counts)
    recv = lax.all_to_all(packed, "shard", split_axis=0, concat_axis=0, tiled=True)
    behind = [(i, (i - 1) % shards) for i in range(shards)]
    ahead = [(i, (i + 1) % shards) for i in range(shards)]
    serving_here = lax.ppermute(serving_table, "shard", behind)

    joined = recv
    if cap < LANES:
        groups = shards * cap // LANES
        marks = recv[:, cap : cap + 2, :cap].reshape(groups, LANES // cap, 2, cap)
        marks = marks.transpose(0, 2, 1, 3).reshape(groups, 2, LANES)
        marks = jnp.pad(marks, ((0, 0), (0, 14), (0, 0)))
        joined = jnp.concatenate([recv[:, :cap, :].reshape(groups, LANES, emb), marks], axis=1)

    new_table, new_accum, change, req = call(
        functools.partial(update_kernel, LANES, cap + 2, req_rows), "update", 32,
        out_shape=(
            jax.ShapeDtypeStruct((row_count, emb), bf16),
            jax.ShapeDtypeStruct((row_count // LANES, LANES), f32),
            jax.ShapeDtypeStruct((row_count, emb), f32),
            jax.ShapeDtypeStruct((shards, req_rows, LANES), jnp.int32),
        ),
        in_specs=[vmem, vmem, vmem, hbm],
        out_specs=(hbm, vmem, vmem, vmem),
        scratch_shapes=[
            pltpu.VMEM((shards * cap, 2 * LANES), bf16),
            pltpu.VMEM((row_count, LANES), f32),
            pltpu.VMEM((row_count, LANES), bf16),
            pltpu.VMEM((row_count, LANES), bf16),
            pltpu.SemaphoreType.DMA((2,)),
        ],
    )(joined, recv, row_accum.reshape(-1, LANES), item_table)
    serving_next, live = call(
        apply_kernel, "apply", 8,
        out_shape=(
            jax.ShapeDtypeStruct((row_count, emb), bf16),
            jax.ShapeDtypeStruct((row_count, emb), f32),
        ),
        in_specs=[vmem, vmem],
        out_specs=(vmem, vmem),
    )(change, serving_here)
    req = req.reshape(-1)

    me = lax.axis_index("shard").astype(jnp.int32).reshape(1)
    pitch = req_rows * LANES
    sent = lax.ppermute(serving_next, "shard", ahead)
    if shards == 16:
        moves, pieces = [], []
        for sends in SENDS:
            found = call(
                functools.partial(gather_kernel, sends, pitch), "gather", 4,
                out_shape=(jax.ShapeDtypeStruct((capr, emb), bf16),) * len(sends),
                in_specs=[smem, smem, vmem],
                out_specs=(vmem,) * len(sends),
                cost_estimate=work(0.6 * len(sends)),
            )(me, req, live)
            for move, rows in zip(sends, found):
                moves.append(move)
                pieces.append(lax.ppermute(rows, "shard", [(i, i ^ move) for i in range(shards)]))
        token = jnp.zeros((8, LANES), f32)
        for takes in TAKES:
            token = call(
                token_kernel, "token", 4,
                out_shape=jax.ShapeDtypeStruct((8, LANES), f32),
                in_specs=[vmem] + [hbm] * len(takes),
                out_specs=vmem,
                cost_estimate=work(0.6 * len(takes) + 0.6),
            )(token, *[pieces[moves.index(move)] for move in takes])
    else:
        found = call(
            functools.partial(gather_all_kernel, pitch), "gather", 8,
            out_shape=jax.ShapeDtypeStruct((shards, capr, emb), bf16),
            in_specs=[smem, vmem],
            out_specs=vmem,
        )(req, live)
        moves, token = None, jnp.zeros((8, LANES), f32)
        got = lax.all_to_all(found, "shard", split_axis=0, concat_axis=0, tiled=True)
        pieces = [got.reshape(shards * capr, emb)]
    scores, new_serving = call(
        functools.partial(tower_kernel, moves, (feats, requests), pitch), "tower", 58,
        out_shape=(
            jax.ShapeDtypeStruct((requests // LANES, LANES), f32),
            jax.ShapeDtypeStruct((row_count, emb), bf16),
        ),
        in_specs=[vmem] + [smem] * 3 + [vmem, hbm, vmem, hbm, vmem, vmem, hbm] + [hbm] * len(pieces),
        out_specs=(vmem, hbm),
        scratch_shapes=[
            pltpu.VMEM(cross_weight.shape, bf16),
            pltpu.VMEM(tower_weight.shape, bf16),
            pltpu.VMEM((shards * capr, emb), bf16),
            pltpu.VMEM((row_count, emb), bf16),
            pltpu.VMEM((shards * capr, emb), f32),
            pltpu.VMEM((feats * requests, emb), f32),
            pltpu.VMEM((requests, feats * emb), bf16),
            pltpu.SemaphoreType.DMA((4 + len(pieces),)),
        ],
    )(
        token, me, req, request_slots.T.reshape(-1), live, cross_weight, cross_bias, tower_weight,
        tower_bias.reshape(1, -1), score_weight.reshape(1, -1), sent, *pieces,
    )
    return (new_table, new_accum.reshape(row_count), new_serving, scores.reshape(requests))


def solution(mesh):
    both = ("groups", "shard")
    in_specs = (
        P("shard", None), P("shard"), P("shard", None), P(both, None, None), P(both, None), P(both),
        P(both, None), P(both, None), P(), P(), P(), P(), P(),
    )
    out_specs = (P(both, None), P(both), P(both, None), P(both))
    return jax.shard_map(body, mesh=mesh, in_specs=in_specs, out_specs=out_specs, check_vma=False)
```

time: 166 us -> 128 us (0.77); the launches traced: 164 us -> 128 us
  waiting for transfers between devices: 76.9 us -> 39.7 us
  starting transfers between devices: 15.6 us -> 36.4 us
  Pallas kernels: 58.5 us -> 46.6 us
  local copies, waits for them, and re-layouts: 12.1 us -> 3.89 us
    all_to_all x1 -> x0, waiting for transfers between devices: 29.5 us -> none  [body(): lax.all_to_all(found, 'shard', split_axis=0, concat_axis=0, tiled=True)]
    ppermute x1 -> x16, starting transfers between devices: 1.48 us -> 29.4 us  [the longest x15 29.4 us: body(): lax.ppermute(rows, 'shard', [(i, i ^ move) for i in range(shards)])]
    all_to_all x1, waiting for transfers between devices: 4.36 us -> 23.9 us  [body(): lax.all_to_all(packed, 'shard', split_axis=0, concat_axis=0, tiled=True)]
    ppermute x1, waiting for transfers between devices: 19.5 us -> 0.01 us  [body(): serving_here = lax.ppermute(serving_table, 'shard', behind)]
    pallas_call x4 -> x14, Pallas kernels: 58.5 us -> 46.6 us  [the longest x1 20.2 us: body(): call(functools.partial(tower_kernel, moves, (feats, requests), pitch), 't...]
    unnamed x29 -> x46, local copies, waits for them, and re-layouts: 11.2 us -> 2.03 us
    ppermute x1 -> x16, waiting for transfers between devices: 23.6 us -> 15.8 us  [the longest x15 15.8 us: body(): lax.ppermute(rows, 'shard', [(i, i ^ move) for i in range(shards)])]
    all_to_all x1 -> x0, starting transfers between devices: 7.1 us -> none  [body(): lax.all_to_all(found, 'shard', split_axis=0, concat_axis=0, tiled=True)]
  transfers between devices with their start and end apart: 4 -> 18, of which waited for: 4 -> 6; matrix products, arithmetic and copies ran while one was open for 0% -> 1% of each run, Pallas kernels for 0% -> 18%
where the time goes in v2:
time: 128 us
  Pallas kernels  46.6 us (36%)
  waiting for transfers between devices  39.7 us (31%)
  starting transfers between devices  36.4 us (28%)
  local copies, waits for them, and re-layouts  3.89 us (3%)
    ppermute x15, starting transfers between devices, body(): lax.ppermute(rows, 'shard', [(i, i ^ move) for i in range(shards)])  29.4 us
    all_to_all x1, waiting for transfers between devices, body(): lax.all_to_all(packed, 'shard', split_axis=0, concat_axis=0, tiled=True)  23.9 us
    pallas_call x1, Pallas kernels, body(): call(functools.partial(tower_kernel, moves, (feats, requests), pitch), 't...  20.2 us
    pallas_call x6, Pallas kernels, body(): call(functools.partial(gather_kernel, sends, pitch), 'gather', 4, out_sha...  15.8 us
    ppermute x15, waiting for transfers between devices, body(): lax.ppermute(rows, 'shard', [(i, i ^ move) for i in range(shards)])  15.8 us
    pallas_call x1, Pallas kernels, body(): call(functools.partial(update_kernel, LANES, cap + 2, req_rows), 'update'...  6.7 us
    all_to_all x1, starting transfers between devices, body(): lax.all_to_all(packed, 'shard', split_axis=0, concat_axis=0, tiled=True)  6.62 us
    pallas_call x1, Pallas kernels, body(): call(functools.partial(pack_kernel, cap, req_rows), 'pack', 56, out_shape...  2.71 us
  transfers between devices with their start and end apart: 18, of which 6 were waited for; matrix products, arithmetic and copies ran while one was open for 1% of the time, Pallas kernels for 18%

profile of v2, /device:TPU:9, one launch (start us, length us, event | category | flops | bytes accessed | tf_op | source)
XLA Modules:
  0.0 127.5 jit_solution(12805746389237551924)
XLA Ops:
  0.6 2.7 %pack.1 = bf16[16,144,128]{2,1,0:T(8,128)(2,1)} custom-call(bf16[16,128,128]{2,1,0:T(8,128)(2,1)} %rows_hbm.1, s32[16,128]{1,0:T(8,128)} %ids_hbm.1, s32[16,480]{1,0:T(8,128)} %req_hbm.1, s32[16]{0:T(128)} %counts_ref.1), custom_call_target="tpu_custom_call" | custom-call | tf_op jit(solution)/shard_map/pack/pallas_call | solution.py:306
  3.4 6.6 %all-to-all-start = ((bf16[16,144,128]{2,1,0:T(8,128)(2,1)}), bf16[16,144,128]{2,1,0:T(8,128)(2,1)S(1)}, u32[]{:S(2)}, u32[]{:S(2)}) async-start(bf16[16,144,128]{2,1,0:T(8,128)(2,1)} %pack.1), calls=%async_computation | async-start | bytes 1179648 | tf_op jit(solution)/shard_map/all_to_all | solution.py:318
  10.3 23.9 %all-to-all-done.recv_ref.req_ref = bf16[16,144,128]{2,1,0:T(8,128)(2,1)S(1)} async-done(((bf16[16,144,128]{2,1,0:T(8,128)(2,1)}), bf16[16,144,128]{2,1,0:T(8,128)(2,1)S(1)}, u32[]{:S(2)}, u32[]{:S(2)}) %all-to-all-start) | async-done | bytes 589856 | tf_op jit(solution)/shard_map/all_to_all | solution.py:318
  34.2 0.7 copy-done.16
  35.0 6.7 %update.1 = (bf16[4096,128]{1,0:T(8,128)(2,1)}, f32[32,128]{1,0:T(8,128)}, f32[4096,128]{1,0:T(8,128)S(1)}, s32[16,4,128]{2,1,0:T(4,128)S(1)}) custom-call(bf16[16,144,128]{2,1,0:T(8,128)(2,1)S(1)} %all-to-all-done.recv_ref.req_ref, bf16[16,144,128]{2,1,0:T(8,128)(2,1)S(1)} %all-to-all-done.recv_ref.req_ref, f32[32,128]{1,0:T(8,128)S(1)} %bitcast.13, ...), custom_call_target="tpu_custom_call" | custom-call | tf_op jit(solution)/shard_map/update/pallas_call | solution.py:331
  41.7 1.1 apply.1
  42.8 2.5 %gather.7 = (bf16[480,128]{1,0:T(8,128)(2,1)S(1)}, bf16[480,128]{1,0:T(8,128)(2,1)S(1)}, bf16[480,128]{1,0:T(8,128)(2,1)S(1)}) custom-call(s32[1]{0:T(128)} %bitcast.2.me_ref, s32[8192]{0:T(1024)S(1)} %bitcast.6, f32[4096,128]{1,0:T(8,128)S(1)} %get-tuple-element.30.live_ref), custom_call_target="tpu_custom_call" | custom-call | bytes 5399999 | tf_op jit(solution)/shard_map/gather/pallas_call | solution.py:366
  45.4 3.2 %collective-permute-start.2 = (bf16[480,128]{1,0:T(8,128)(2,1)S(1)}, bf16[480,128]{1,0:T(8,128)(2,1)S(1)}, u32[]{:S(2)}, u32[]{:S(2)}) collective-permute-start(bf16[480,128]{1,0:T(8,128)(2,1)S(1)} %get-tuple-element.31), channel_id=1, source_target_pairs={{0,9},{1,8},{2,11},{3,10},{4,13},{5,12},{6,15},{7,14},{8,1},{9,0},... | collective-permute-start | bytes 368648 | tf_op jit(solution)/shard_map/ppermute | solution.py:375
  48.6 1.7 %collective-permute-start.3 = (bf16[480,128]{1,0:T(8,128)(2,1)S(1)}, bf16[480,128]{1,0:T(8,128)(2,1)S(1)}, u32[]{:S(2)}, u32[]{:S(2)}) collective-permute-start(bf16[480,128]{1,0:T(8,128)(2,1)S(1)} %get-tuple-element.32), channel_id=1, source_target_pairs={{0,1},{1,0},{2,3},{3,2},{4,5},{5,4},{6,7},{7,6},{8,9},{9,8},{10,11... | collective-permute-start | bytes 368648 | tf_op jit(solution)/shard_map/ppermute | solution.py:375
  50.3 1.6 %gather.6 = bf16[480,128]{1,0:T(8,128)(2,1)S(1)} custom-call(s32[1]{0:T(128)} %bitcast.2.me_ref, s32[8192]{0:T(1024)S(1)} %bitcast.7, f32[4096,128]{1,0:T(8,128)S(1)} %get-tuple-element.30.live_ref), custom_call_target="tpu_custom_call" | custom-call | bytes 1800000 | tf_op jit(solution)/shard_map/gather/pallas_call | solution.py:366
  52.0 2.5 %gather.8 = (bf16[480,128]{1,0:T(8,128)(2,1)S(1)}, bf16[480,128]{1,0:T(8,128)(2,1)S(1)}, bf16[480,128]{1,0:T(8,128)(2,1)S(1)}) custom-call(s32[1]{0:T(128)} %bitcast.2.me_ref, s32[8192]{0:T(1024)S(1)} %bitcast.8, f32[4096,128]{1,0:T(8,128)S(1)} %get-tuple-element.30.live_ref), custom_call_target="tpu_custom_call" | custom-call | bytes 5399999 | tf_op jit(solution)/shard_map/gather/pallas_call | solution.py:366
  54.5 3.2 %gather.9 = (bf16[480,128]{1,0:T(8,128)(2,1)S(1)}, bf16[480,128]{1,0:T(8,128)(2,1)S(1)}, bf16[480,128]{1,0:T(8,128)(2,1)}) custom-call(s32[1]{0:T(128)} %bitcast.2.me_ref, s32[8192]{0:T(1024)S(1)} %bitcast.9, f32[4096,128]{1,0:T(8,128)S(1)} %get-tuple-element.30.live_ref), custom_call_target="tpu_custom_call" | custom-call | bytes 5399999 | tf_op jit(solution)/shard_map/gather/pallas_call | solution.py:366
  57.8 10.6 %collective-permute-start.6 = (bf16[480,128]{1,0:T(8,128)(2,1)S(1)}, bf16[480,128]{1,0:T(8,128)(2,1)S(1)}, u32[]{:S(2)}, u32[]{:S(2)}) collective-permute-start(bf16[480,128]{1,0:T(8,128)(2,1)S(1)} %get-tuple-element.35), channel_id=1, source_target_pairs={{0,11},{1,10},{2,9},{3,8},{4,15},{5,14},{6,13},{7,12},{8,3},{9,2},... | collective-permute-start | bytes 368648 | tf_op jit(solution)/shard_map/ppermute | solution.py:375
  68.5 3.0 %collective-permute-start.8 = (bf16[480,128]{1,0:T(8,128)(2,1)S(1)}, bf16[480,128]{1,0:T(8,128)(2,1)S(1)}, u32[]{:S(2)}, u32[]{:S(2)}) collective-permute-start(bf16[480,128]{1,0:T(8,128)(2,1)S(1)} %get-tuple-element.37), channel_id=1, source_target_pairs={{0,12},{1,13},{2,14},{3,15},{4,8},{5,9},{6,10},{7,11},{8,4},{9,5},... | collective-permute-start | bytes 368648 | tf_op jit(solution)/shard_map/ppermute | solution.py:375
  71.5 3.2 %gather.10 = (bf16[480,128]{1,0:T(8,128)(2,1)S(1)}, bf16[480,128]{1,0:T(8,128)(2,1)S(1)}, bf16[480,128]{1,0:T(8,128)(2,1)}) custom-call(s32[1]{0:T(128)} %bitcast.2.me_ref, s32[8192]{0:T(1024)S(1)} %bitcast.10, f32[4096,128]{1,0:T(8,128)S(1)} %get-tuple-element.30.live_ref), custom_call_target="tpu_custom_call" | custom-call | bytes 5399999 | tf_op jit(solution)/shard_map/gather/pallas_call | solution.py:366
  74.7 4.2 %collective-permute-done.6.refs_2_.refs_5_ = bf16[480,128]{1,0:T(8,128)(2,1)S(1)} collective-permute-done((bf16[480,128]{1,0:T(8,128)(2,1)S(1)}, bf16[480,128]{1,0:T(8,128)(2,1)S(1)}, u32[]{:S(2)}, u32[]{:S(2)}) %collective-permute-start.6) | collective-permute-done | bytes 122912 | tf_op jit(solution)/shard_map/ppermute | solution.py:375
  78.9 1.9 %collective-permute-start.7 = (bf16[480,128]{1,0:T(8,128)(2,1)S(1)}, bf16[480,128]{1,0:T(8,128)(2,1)S(1)}, u32[]{:S(2)}, u32[]{:S(2)}) collective-permute-start(bf16[480,128]{1,0:T(8,128)(2,1)S(1)} %get-tuple-element.36), channel_id=1, source_target_pairs={{0,3},{1,2},{2,1},{3,0},{4,7},{5,6},{6,5},{7,4},{8,11},{9,10},{10,... | collective-permute-start | bytes 368648 | tf_op jit(solution)/shard_map/ppermute | solution.py:375
  80.8 0.8 collective-permute-done.4.refs_0_.refs_3_
  81.5 3.4 %collective-permute-start.11 = (bf16[480,128]{1,0:T(8,128)(2,1)S(1)}, bf16[480,128]{1,0:T(8,128)(2,1)S(1)}, u32[]{:S(2)}, u32[]{:S(2)}) collective-permute-start(bf16[480,128]{1,0:T(8,128)(2,1)S(1)} %get-tuple-element.40), channel_id=1, source_target_pairs={{0,5},{1,4},{2,7},{3,6},{4,1},{5,0},{6,3},{7,2},{8,13},{9,12},{10,... | collective-permute-start | bytes 368648 | tf_op jit(solution)/shard_map/ppermute | solution.py:375
  85.2 2.8 %gather.11 = (bf16[480,128]{1,0:T(8,128)(2,1)}, bf16[480,128]{1,0:T(8,128)(2,1)}) custom-call(s32[1]{0:T(128)} %bitcast.2.me_ref, s32[8192]{0:T(1024)S(1)} %bitcast.11, f32[4096,128]{1,0:T(8,128)S(1)} %get-tuple-element.30.live_ref), custom_call_target="tpu_custom_call" | custom-call | bytes 3600000 | tf_op jit(solution)/shard_map/gather/pallas_call | solution.py:366
  87.9 2.9 %collective-permute-start.10 = (bf16[480,128]{1,0:T(8,128)(2,1)}, bf16[480,128]{1,0:T(8,128)(2,1)S(1)}, u32[]{:S(2)}, u32[]{:S(2)}) collective-permute-start(bf16[480,128]{1,0:T(8,128)(2,1)} %get-tuple-element.39), channel_id=1, source_target_pairs={{0,13},{1,12},{2,15},{3,14},{4,9},{5,8},{6,11},{7,10},{8,5},{9,4},... | collective-permute-start | bytes 368648 | tf_op jit(solution)/shard_map/ppermute | solution.py:375
  90.8 1.5 %collective-permute-start.14 = (bf16[480,128]{1,0:T(8,128)(2,1)}, bf16[480,128]{1,0:T(8,128)(2,1)S(1)}, u32[]{:S(2)}, u32[]{:S(2)}) collective-permute-start(bf16[480,128]{1,0:T(8,128)(2,1)} %get-tuple-element.43), channel_id=1, source_target_pairs={{0,6},{1,7},{2,4},{3,5},{4,2},{5,3},{6,0},{7,1},{8,14},{9,15},{10,... | collective-permute-start | bytes 368648 | tf_op jit(solution)/shard_map/ppermute | solution.py:375
  92.3 0.8 collective-permute-start.15
  93.1 3.1 %collective-permute-done.12.refs_2_.refs_11_ = bf16[480,128]{1,0:T(8,128)(2,1)S(1)} collective-permute-done((bf16[480,128]{1,0:T(8,128)(2,1)S(1)}, bf16[480,128]{1,0:T(8,128)(2,1)S(1)}, u32[]{:S(2)}, u32[]{:S(2)}) %collective-permute-start.12) | collective-permute-done | bytes 122912 | tf_op jit(solution)/shard_map/ppermute | solution.py:375
  96.2 0.6 reshape.36.slots_ref
  96.9 0.6 reshape.37.tower_bias_ref
  97.5 0.6 reshape.38.score_ref
  98.2 2.5 %collective-permute-done.10.refs_0_.refs_9_ = bf16[480,128]{1,0:T(8,128)(2,1)S(1)} collective-permute-done((bf16[480,128]{1,0:T(8,128)(2,1)}, bf16[480,128]{1,0:T(8,128)(2,1)S(1)}, u32[]{:S(2)}, u32[]{:S(2)}) %collective-permute-start.10) | collective-permute-done | bytes 122912 | tf_op jit(solution)/shard_map/ppermute | solution.py:375
  100.7 0.6 copy-done.15
  101.3 5.1 %collective-permute-done.15.refs_13_ = bf16[480,128]{1,0:T(8,128)(2,1)S(1)} collective-permute-done((bf16[480,128]{1,0:T(8,128)(2,1)}, bf16[480,128]{1,0:T(8,128)(2,1)S(1)}, u32[]{:S(2)}, u32[]{:S(2)}) %collective-permute-start.15) | collective-permute-done | bytes 122912 | tf_op jit(solution)/shard_map/ppermute | solution.py:375
  106.6 0.5 copy-done.18
  107.2 20.2 %tower.1 = (f32[8,128]{1,0:T(8,128)}, bf16[4096,128]{1,0:T(8,128)(2,1)}) custom-call(f32[8,128]{1,0:T(8,128)} %copy-done.15, s32[1]{0:T(128)} %bitcast.2.me_ref, s32[8192]{0:T(1024)} %bitcast.12, s32[5120]{0:T(1024)} %reshape.36.slots_ref, f32[4096,128]{1,0:T(8,128)} %copy-done, bf16[3,640,640]{2,1,0:T(8,128)(2,1)} %cross_hbm.1, ...), custom_call_target="tpu_custom_call" | custom-call | tf_op jit(solution)/shard_map/tower/pallas_call | solution.py:395
  (68 shorter events, 0.9 us)
Async XLA Ops:
  0.6 33.6 %copy-start.2 = (bf16[4096,128]{1,0:T(8,128)(2,1)S(1)}, bf16[4096,128]{1,0:T(8,128)(2,1)}, u32[]{:S(2)}) copy-start(bf16[4096,128]{1,0:T(8,128)(2,1)} %item_hbm.1) | copy-start | bytes 3145732
  3.4 30.9 %all-to-all-start = ((bf16[16,144,128]{2,1,0:T(8,128)(2,1)}), bf16[16,144,128]{2,1,0:T(8,128)(2,1)S(1)}, u32[]{:S(2)}, u32[]{:S(2)}) async-start(bf16[16,144,128]{2,1,0:T(8,128)(2,1)} %pack.1), calls=%async_computation | async-start | bytes 1179648 | tf_op jit(solution)/shard_map/all_to_all | solution.py:318
  10.0 31.7 %collective-permute-start = (bf16[4096,128]{1,0:T(8,128)(2,1)}, bf16[4096,128]{1,0:T(8,128)(2,1)S(1)}, u32[]{:S(2)}, u32[]{:S(2)}) collective-permute-start(bf16[4096,128]{1,0:T(8,128)(2,1)} %param.15), channel_id=1, source_target_pairs={{0,15},{1,0},{2,1},{3,2},{4,3},{5,4},{6,5},{7,6},{8,7},{9,8},{10,9... | collective-permute-start | bytes 3145736 | tf_op jit(solution)/shard_map/ppermute | solution.py:321
  41.7 43.5 %copy-start.1 = (s32[16,4,128]{2,1,0:T(4,128)}, s32[16,4,128]{2,1,0:T(4,128)S(1)}, u32[]{:S(2)}) copy-start(s32[16,4,128]{2,1,0:T(4,128)S(1)} %get-tuple-element.28) | copy-start | bytes 98308
  42.8 42.3 %copy-start = (f32[4096,128]{1,0:T(8,128)}, f32[4096,128]{1,0:T(8,128)S(1)}, u32[]{:S(2)}) copy-start(f32[4096,128]{1,0:T(8,128)S(1)} %get-tuple-element.30.live_ref) | copy-start | bytes 6291460
  42.8 63.6 %collective-permute-start.13 = (bf16[4096,128]{1,0:T(8,128)(2,1)}, bf16[4096,128]{1,0:T(8,128)(2,1)}, u32[]{:S(2)}, u32[]{:S(2)}) collective-permute-start(bf16[4096,128]{1,0:T(8,128)(2,1)} %get-tuple-element.42), channel_id=1, source_target_pairs={{0,1},{1,2},{2,3},{3,4},{4,5},{5,6},{6,7},{7,8},{8,9},{9,10},{10,1... | collective-permute-start | bytes 3145736 | tf_op jit(solution)/shard_map/ppermute | solution.py:362
  45.4 12.4 %collective-permute-start.2 = (bf16[480,128]{1,0:T(8,128)(2,1)S(1)}, bf16[480,128]{1,0:T(8,128)(2,1)S(1)}, u32[]{:S(2)}, u32[]{:S(2)}) collective-permute-start(bf16[480,128]{1,0:T(8,128)(2,1)S(1)} %get-tuple-element.31), channel_id=1, source_target_pairs={{0,9},{1,8},{2,11},{3,10},{4,13},{5,12},{6,15},{7,14},{8,1},{9,0},... | collective-permute-start | bytes 368648 | tf_op jit(solution)/shard_map/ppermute | solution.py:375
  48.6 19.8 %collective-permute-start.3 = (bf16[480,128]{1,0:T(8,128)(2,1)S(1)}, bf16[480,128]{1,0:T(8,128)(2,1)S(1)}, u32[]{:S(2)}, u32[]{:S(2)}) collective-permute-start(bf16[480,128]{1,0:T(8,128)(2,1)S(1)} %get-tuple-element.32), channel_id=1, source_target_pairs={{0,1},{1,0},{2,3},{3,2},{4,5},{5,4},{6,7},{7,6},{8,9},{9,8},{10,11... | collective-permute-start | bytes 368648 | tf_op jit(solution)/shard_map/ppermute | solution.py:375
  51.9 16.6 %collective-permute-start.1 = (bf16[480,128]{1,0:T(8,128)(2,1)S(1)}, bf16[480,128]{1,0:T(8,128)(2,1)S(1)}, u32[]{:S(2)}, u32[]{:S(2)}) collective-permute-start(bf16[480,128]{1,0:T(8,128)(2,1)S(1)} %gather.6), channel_id=1, source_target_pairs={{0,8},{1,9},{2,10},{3,11},{4,12},{5,13},{6,14},{7,15},{8,0},{9,1},... | collective-permute-start | bytes 368648 | tf_op jit(solution)/shard_map/ppermute | solution.py:375
  57.7 38.5 %copy-start.20 = (s32[1024,5]{0,1:T(8,128)S(1)}, s32[1024,5]{0,1:T(8,128)}, u32[]{:S(2)}) copy-start(s32[1024,5]{0,1:T(8,128)} %param.20) | copy-start | bytes 61444
  57.7 39.2 %copy-start.21 = (bf16[4096]{0:T(1024)(128)(2,1)S(1)}, bf16[4096]{0:T(1024)(128)(2,1)}, u32[]{:S(2)}) copy-start(bf16[4096]{0:T(1024)(128)(2,1)} %param.24) | copy-start | bytes 24580
  57.7 39.8 %copy-start.22 = (bf16[4096]{0:T(1024)(128)(2,1)S(1)}, bf16[4096]{0:T(1024)(128)(2,1)}, u32[]{:S(2)}) copy-start(bf16[4096]{0:T(1024)(128)(2,1)} %param.25) | copy-start | bytes 24580
  57.7 17.0 %collective-permute-start.5 = (bf16[480,128]{1,0:T(8,128)(2,1)S(1)}, bf16[480,128]{1,0:T(8,128)(2,1)S(1)}, u32[]{:S(2)}, u32[]{:S(2)}) collective-permute-start(bf16[480,128]{1,0:T(8,128)(2,1)S(1)} %get-tuple-element.34), channel_id=1, source_target_pairs={{0,2},{1,3},{2,0},{3,1},{4,6},{5,7},{6,4},{7,5},{8,10},{9,11},{10,... | collective-permute-start | bytes 368648 | tf_op jit(solution)/shard_map/ppermute | solution.py:375
  57.8 40.3 %copy-start.3 = (bf16[480,128]{1,0:T(8,128)(2,1)}, bf16[480,128]{1,0:T(8,128)(2,1)S(1)}, u32[]{:S(2)}) copy-start(bf16[480,128]{1,0:T(8,128)(2,1)S(1)} %collective-permute-done.2.refs_1_) | copy-start | bytes 368644
  57.8 21.1 %collective-permute-start.6 = (bf16[480,128]{1,0:T(8,128)(2,1)S(1)}, bf16[480,128]{1,0:T(8,128)(2,1)S(1)}, u32[]{:S(2)}, u32[]{:S(2)}) collective-permute-start(bf16[480,128]{1,0:T(8,128)(2,1)S(1)} %get-tuple-element.35), channel_id=1, source_target_pairs={{0,11},{1,10},{2,9},{3,8},{4,15},{5,14},{6,13},{7,12},{8,3},{9,2},... | collective-permute-start | bytes 368648 | tf_op jit(solution)/shard_map/ppermute | solution.py:375
  68.4 29.7 %copy-start.4 = (bf16[480,128]{1,0:T(8,128)(2,1)}, bf16[480,128]{1,0:T(8,128)(2,1)S(1)}, u32[]{:S(2)}) copy-start(bf16[480,128]{1,0:T(8,128)(2,1)S(1)} %collective-permute-done.3.refs_2_) | copy-start | bytes 368644
  68.4 13.1 %collective-permute-start.4 = (bf16[480,128]{1,0:T(8,128)(2,1)S(1)}, bf16[480,128]{1,0:T(8,128)(2,1)S(1)}, u32[]{:S(2)}, u32[]{:S(2)}) collective-permute-start(bf16[480,128]{1,0:T(8,128)(2,1)S(1)} %get-tuple-element.33), channel_id=1, source_target_pairs={{0,10},{1,11},{2,8},{3,9},{4,14},{5,15},{6,12},{7,13},{8,2},{9,3},... | collective-permute-start | bytes 368648 | tf_op jit(solution)/shard_map/ppermute | solution.py:375
  68.4 29.7 %copy-start.5 = (bf16[480,128]{1,0:T(8,128)(2,1)}, bf16[480,128]{1,0:T(8,128)(2,1)S(1)}, u32[]{:S(2)}) copy-start(bf16[480,128]{1,0:T(8,128)(2,1)S(1)} %collective-permute-done.1.refs_0_) | copy-start | bytes 368644
  68.5 16.5 %collective-permute-start.8 = (bf16[480,128]{1,0:T(8,128)(2,1)S(1)}, bf16[480,128]{1,0:T(8,128)(2,1)S(1)}, u32[]{:S(2)}, u32[]{:S(2)}) collective-permute-start(bf16[480,128]{1,0:T(8,128)(2,1)S(1)} %get-tuple-element.37), channel_id=1, source_target_pairs={{0,12},{1,13},{2,14},{3,15},{4,8},{5,9},{6,10},{7,11},{8,4},{9,5},... | collective-permute-start | bytes 368648 | tf_op jit(solution)/shard_map/ppermute | solution.py:375
  74.7 31.8 %copy-start.6 = (bf16[480,128]{1,0:T(8,128)(2,1)}, bf16[480,128]{1,0:T(8,128)(2,1)S(1)}, u32[]{:S(2)}) copy-start(bf16[480,128]{1,0:T(8,128)(2,1)S(1)} %collective-permute-done.5.refs_1_.refs_4_) | copy-start | bytes 368644
  74.7 13.2 %collective-permute-start.9 = (bf16[480,128]{1,0:T(8,128)(2,1)S(1)}, bf16[480,128]{1,0:T(8,128)(2,1)S(1)}, u32[]{:S(2)}, u32[]{:S(2)}) collective-permute-start(bf16[480,128]{1,0:T(8,128)(2,1)S(1)} %get-tuple-element.38), channel_id=1, source_target_pairs={{0,4},{1,5},{2,6},{3,7},{4,0},{5,1},{6,2},{7,3},{8,12},{9,13},{10,... | collective-permute-start | bytes 368648 | tf_op jit(solution)/shard_map/ppermute | solution.py:375
  78.9 27.6 %copy-start.7 = (bf16[480,128]{1,0:T(8,128)(2,1)}, bf16[480,128]{1,0:T(8,128)(2,1)S(1)}, u32[]{:S(2)}) copy-start(bf16[480,128]{1,0:T(8,128)(2,1)S(1)} %collective-permute-done.6.refs_2_.refs_5_) | copy-start | bytes 368644
  78.9 11.9 %collective-permute-start.7 = (bf16[480,128]{1,0:T(8,128)(2,1)S(1)}, bf16[480,128]{1,0:T(8,128)(2,1)S(1)}, u32[]{:S(2)}, u32[]{:S(2)}) collective-permute-start(bf16[480,128]{1,0:T(8,128)(2,1)S(1)} %get-tuple-element.36), channel_id=1, source_target_pairs={{0,3},{1,2},{2,1},{3,0},{4,7},{5,6},{6,5},{7,4},{8,11},{9,10},{10,... | collective-permute-start | bytes 368648 | tf_op jit(solution)/shard_map/ppermute | solution.py:375
  81.5 25.0 %copy-start.8 = (bf16[480,128]{1,0:T(8,128)(2,1)}, bf16[480,128]{1,0:T(8,128)(2,1)S(1)}, u32[]{:S(2)}) copy-start(bf16[480,128]{1,0:T(8,128)(2,1)S(1)} %collective-permute-done.4.refs_0_.refs_3_) | copy-start | bytes 368644
  81.5 10.7 %collective-permute-start.11 = (bf16[480,128]{1,0:T(8,128)(2,1)S(1)}, bf16[480,128]{1,0:T(8,128)(2,1)S(1)}, u32[]{:S(2)}, u32[]{:S(2)}) collective-permute-start(bf16[480,128]{1,0:T(8,128)(2,1)S(1)} %get-tuple-element.40), channel_id=1, source_target_pairs={{0,5},{1,4},{2,7},{3,6},{4,1},{5,0},{6,3},{7,2},{8,13},{9,12},{10,... | collective-permute-start | bytes 368648 | tf_op jit(solution)/shard_map/ppermute | solution.py:375
  85.0 21.5 %copy-start.9 = (bf16[480,128]{1,0:T(8,128)(2,1)}, bf16[480,128]{1,0:T(8,128)(2,1)S(1)}, u32[]{:S(2)}) copy-start(bf16[480,128]{1,0:T(8,128)(2,1)S(1)} %collective-permute-done.8.refs_1_.refs_7_) | copy-start | bytes 368644
  85.0 11.3 %collective-permute-start.12 = (bf16[480,128]{1,0:T(8,128)(2,1)S(1)}, bf16[480,128]{1,0:T(8,128)(2,1)S(1)}, u32[]{:S(2)}, u32[]{:S(2)}) collective-permute-start(bf16[480,128]{1,0:T(8,128)(2,1)S(1)} %get-tuple-element.41), channel_id=1, source_target_pairs={{0,14},{1,15},{2,12},{3,13},{4,10},{5,11},{6,8},{7,9},{8,6},{9,7},... | collective-permute-start | bytes 368648 | tf_op jit(solution)/shard_map/ppermute | solution.py:375
  87.9 18.6 %copy-start.10 = (bf16[480,128]{1,0:T(8,128)(2,1)}, bf16[480,128]{1,0:T(8,128)(2,1)S(1)}, u32[]{:S(2)}) copy-start(bf16[480,128]{1,0:T(8,128)(2,1)S(1)} %collective-permute-done.9.refs_2_.refs_8_) | copy-start | bytes 368644
  87.9 12.8 %collective-permute-start.10 = (bf16[480,128]{1,0:T(8,128)(2,1)}, bf16[480,128]{1,0:T(8,128)(2,1)S(1)}, u32[]{:S(2)}, u32[]{:S(2)}) collective-permute-start(bf16[480,128]{1,0:T(8,128)(2,1)} %get-tuple-element.39), channel_id=1, source_target_pairs={{0,13},{1,12},{2,15},{3,14},{4,9},{5,8},{6,11},{7,10},{8,5},{9,4},... | collective-permute-start | bytes 368648 | tf_op jit(solution)/shard_map/ppermute | solution.py:375
  90.8 10.6 %collective-permute-start.14 = (bf16[480,128]{1,0:T(8,128)(2,1)}, bf16[480,128]{1,0:T(8,128)(2,1)S(1)}, u32[]{:S(2)}, u32[]{:S(2)}) collective-permute-start(bf16[480,128]{1,0:T(8,128)(2,1)} %get-tuple-element.43), channel_id=1, source_target_pairs={{0,6},{1,7},{2,4},{3,5},{4,2},{5,3},{6,0},{7,1},{8,14},{9,15},{10,... | collective-permute-start | bytes 368648 | tf_op jit(solution)/shard_map/ppermute | solution.py:375
  92.3 14.2 %collective-permute-start.15 = (bf16[480,128]{1,0:T(8,128)(2,1)}, bf16[480,128]{1,0:T(8,128)(2,1)S(1)}, u32[]{:S(2)}, u32[]{:S(2)}) collective-permute-start(bf16[480,128]{1,0:T(8,128)(2,1)} %get-tuple-element.44), channel_id=1, source_target_pairs={{0,15},{1,14},{2,13},{3,12},{4,11},{5,10},{6,9},{7,8},{8,7},{9,6},... | collective-permute-start | bytes 368648 | tf_op jit(solution)/shard_map/ppermute | solution.py:375
  96.2 10.2 %collective-permute-start.16 = (bf16[480,128]{1,0:T(8,128)(2,1)}, bf16[480,128]{1,0:T(8,128)(2,1)S(1)}, u32[]{:S(2)}, u32[]{:S(2)}) collective-permute-start(bf16[480,128]{1,0:T(8,128)(2,1)} %get-tuple-element.45), channel_id=1, source_target_pairs={{0,7},{1,6},{2,5},{3,4},{4,3},{5,2},{6,1},{7,0},{8,15},{9,14},{10,... | collective-permute-start | bytes 368648 | tf_op jit(solution)/shard_map/ppermute | solution.py:375
  (9 other events, 54.1 us)

commit v3 on v2

--- a/solution.py
+++ b/solution.py
@@ -19,20 +19,26 @@
     return -(-value // unit) * unit
 
 
-SENDS = ((8,), (9, 1, 10), (2, 11, 3), (12, 4, 13), (5, 14, 6), (15, 7))
+SENDS = ((8,), (9, 1, 10), (2, 11, 3), (12, 4, 13), (5, 14, 6), (15, 7, 0))
 TAKES = ((8, 9, 1), (10, 2, 11), (3, 12, 4), (13, 5, 14))
+FAR = ((7, 8), (15, 0))
 
 
 def work(micros):
     return pl.CostEstimate(flops=0, transcendentals=0, bytes_accessed=int(micros * 3.0e6))
 
 
-def pack_kernel(cap, req_rows, rows_hbm, ids_hbm, req_hbm, counts_ref, out_ref, ids_ref, req_ref, meta_ref, sems):
+def pack_kernel(
+    cap, req_rows, rows_hbm, ids_hbm, req_hbm, serving_hbm, counts_ref, out_ref, aside_ref,
+    ids_ref, req_ref, meta_ref, sems,
+):
     f32 = jnp.float32
+    half = aside_ref.shape[0]
     loads = [
         pltpu.make_async_copy(ids_hbm, ids_ref, sems.at[0]),
         pltpu.make_async_copy(req_hbm, req_ref, sems.at[1]),
         pltpu.make_async_copy(rows_hbm, out_ref.at[:, :cap, :], sems.at[2]),
+        pltpu.make_async_copy(serving_hbm.at[pl.ds(half, half), :], aside_ref, sems.at[3]),
     ]
     for load in loads:
         load.start()
@@ -56,6 +62,7 @@
         meta_ref[:, 2 + req_rows + row, : stop - start] = (part % DIGIT).astype(f32)
     out_ref[:, cap:, :] = meta_ref[...].astype(jnp.bfloat16)
     loads[2].wait()
+    loads[3].wait()
 
 
 def update_kernel(
@@ -156,11 +163,22 @@
     store_table.wait()
 
 
-def apply_kernel(change_ref, serving_ref, serving_out, live_out):
+def stage_kernel(serving_hbm, *refs):
+    out_ref, sem = refs[-2:]
+    load = pltpu.make_async_copy(serving_hbm.at[pl.ds(0, out_ref.shape[0]), :], out_ref, sem)
+    load.start()
+    load.wait()
+
+
+def apply_kernel(me_ref, change_ref, upper_ref, lower_ref, around_ref, serving_out, live_out):
     f32 = jnp.float32
-    serving = (serving_ref[...].astype(f32) + change_ref[...]).astype(jnp.bfloat16)
-    serving_out[...] = serving
-    live_out[...] = serving.astype(f32)
+    half = upper_ref.shape[0]
+    turned = lax.rem(me_ref[0], 4) == 3
+    lower = jnp.where(turned, around_ref[...].astype(f32), lower_ref[...].astype(f32))
+    for start, old in ((0, upper_ref[...].astype(f32)), (half, lower)):
+        serving = (old + change_ref[start : start + half, :]).astype(jnp.bfloat16)
+        serving_out[start : start + half, :] = serving
+        live_out[start : start + half, :] = serving.astype(f32)
 
 
 def unroll_of(width):
@@ -168,19 +186,6 @@
         if width % unroll == 0:
             return unroll
     return width
-
-
-def copy_rows(from_ref, ids_ref, ids_at, to_ref, to_at, count):
-    unroll = unroll_of(count)
-
-    def some(k, carry):
-        at = k * unroll
-        rows = [from_ref[pl.ds(ids_ref[ids_at + at + u], 1), :] for u in range(unroll)]
-        for u in range(unroll):
-            to_ref[pl.ds(to_at + at + u, 1), :] = rows[u]
-        return carry
-
-    lax.fori_loop(0, count // unroll, some, 0)
 
 
 def gather_kernel(moves, pitch, me_ref, ids_ref, live_ref, *outs):
@@ -211,19 +216,32 @@
     lax.fori_loop(0, blocks, block, 0)
 
 
+def hold_kernel(live_ref, *refs):
+    refs[-1][...] = live_ref[...].astype(jnp.bfloat16)
+
+
+def deliver_kernel(every, me_ref, far_ref, near_hbm, out_hbm, sem):
+    @pl.when(lax.rem(me_ref[0], every) == 0)
+    def _():
+        store = pltpu.make_async_copy(far_ref, out_hbm, sem)
+        store.start()
+        store.wait()
+
+
 def token_kernel(token_ref, *refs):
     refs[-1][...] = token_ref[...]
 
 
 def tower_kernel(
-    moves, shape, pitch, token_ref, me_ref, ids_ref, slots_ref, live_ref, cross_hbm, cross_bias_ref, tower_hbm,
+    moves, shape, token_ref, me_ref, slots_ref, cross_hbm, cross_bias_ref, tower_hbm,
     tower_bias_ref, score_ref, serving_ref, *refs,
 ):
     f32, bf16 = jnp.float32, jnp.bfloat16
     feats, requests = shape
-    pieces = refs[:-10]
-    out_ref, serving_out, cross_ref, tower_ref, got_ref, served_ref = refs[-10:-4]
-    wide_ref, plane_ref, crossed_ref, sems = refs[-4:]
+    pieces = refs[:-11]
+    out_ref, serving_out, cross_ref, tower_ref, got_ref, served_ref = refs[-11:-5]
+    wide_ref, plane_a, plane_b, crossed_ref, sems = refs[-5:]
+    planes = (plane_a, plane_b)
     me = me_ref[0]
     loads = []
     for k, piece in enumerate(pieces):
@@ -245,25 +263,38 @@
     for load in loads:
         load.wait()
     wide_ref[...] = got_ref[...].astype(f32)
-    if moves is not None:
-        width = pieces[0].shape[0]
-        copy_rows(live_ref, ids_ref, me * pitch, wide_ref, me * width, width)
     load_serving.wait()
     store_serving.start()
-    copy_rows(wide_ref, slots_ref, 0, plane_ref, 0, feats * requests)
-    for f in range(feats):
-        crossed_ref[:, f * LANES : (f + 1) * LANES] = plane_ref[
-            f * requests : (f + 1) * requests, :
-        ].astype(bf16)
+    chunk = 256
+    batch = 64
+
+    def collect(c):
+        plane = planes[c % 2]
+        for f in range(feats):
+            for r in range(0, chunk, batch):
+                at = f * requests + c * chunk + r
+                rows = [wide_ref[pl.ds(slots_ref[at + u], 1), :] for u in range(batch)]
+                for u in range(batch):
+                    plane[f * chunk + r + u : f * chunk + r + u + 1, :] = rows[u]
+                yield
+
+    for _ in collect(0):
+        pass
     load_cross.wait()
-    for layer in range(cross_ref.shape[0]):
-        old = crossed_ref[...]
-        projected = jnp.dot(old, cross_ref[layer], preferred_element_type=f32)
-        projected = projected + cross_bias_ref[layer : layer + 1, :].astype(f32)
-        for f in range(feats):
-            cols = slice(f * LANES, (f + 1) * LANES)
-            base = plane_ref[f * requests : (f + 1) * requests, :]
-            crossed_ref[:, cols] = (base * projected[:, cols] + old[:, cols].astype(f32)).astype(bf16)
+    layers = cross_ref.shape[0]
+    for c in range(requests // chunk):
+        plane = planes[c % 2]
+        base = jnp.concatenate([plane[f * chunk : (f + 1) * chunk, :] for f in range(feats)], axis=1)
+        coming = list(range(feats * chunk // batch)) if (c + 1) * chunk < requests else []
+        batches = collect(c + 1) if coming else iter(())
+        old = base.astype(bf16)
+        for layer in range(layers):
+            projected = jnp.dot(old, cross_ref[layer], preferred_element_type=f32)
+            for _ in coming[layer::layers]:
+                next(batches)
+            projected = projected + cross_bias_ref[layer : layer + 1, :].astype(f32)
+            old = (base * projected + old.astype(f32)).astype(bf16)
+        crossed_ref[c * chunk : (c + 1) * chunk, :] = old
     load_tower.wait()
     hidden = tower_ref.shape[1]
     chunk = 1024
@@ -303,22 +334,46 @@
         params = pltpu.CompilerParams(vmem_limit_bytes=limit * MIB)
         return pl.pallas_call(kernel, name=name, compiler_params=params, **kwargs)
 
-    packed = call(
+    me = lax.axis_index("shard").astype(jnp.int32).reshape(1)
+
+    packed, aside = call(
         functools.partial(pack_kernel, cap, req_rows), "pack", 56,
-        out_shape=jax.ShapeDtypeStruct((shards, cap + meta_rows, emb), bf16),
-        in_specs=[hbm, hbm, hbm, smem],
-        out_specs=vmem,
+        out_shape=(
+            jax.ShapeDtypeStruct((shards, cap + meta_rows, emb), bf16),
+            jax.ShapeDtypeStruct((row_count // 2, emb), bf16),
+        ),
+        in_specs=[hbm] * 4 + [smem],
+        out_specs=(vmem, vmem),
         scratch_shapes=[
             pltpu.VMEM((shards, cap), jnp.int32),
             pltpu.VMEM((shards, capr), jnp.int32),
             pltpu.VMEM((shards, meta_rows, LANES), f32),
-            pltpu.SemaphoreType.DMA((3,)),
+            pltpu.SemaphoreType.DMA((4,)),
         ],
-    )(grad_rows, grad_ids, request_ids, grad_counts)
+    )(grad_rows, grad_ids, request_ids, serving_table, grad_counts)
     recv = lax.all_to_all(packed, "shard", split_axis=0, concat_axis=0, tiled=True)
     behind = [(i, (i - 1) % shards) for i in range(shards)]
     ahead = [(i, (i + 1) % shards) for i in range(shards)]
-    serving_here = lax.ppermute(serving_table, "shard", behind)
+    slots = request_slots.T.reshape(-1)
+    tower_bias, score_weight = tower_bias.reshape(1, -1), score_weight.reshape(1, -1)
+    half = row_count // 2
+    if shards == 16:
+        straight = [(i, i - 1) for i in range(shards) if i % 4]
+        lower = lax.ppermute(aside, "shard", straight + [(i, i + 3) for i in range(0, shards, 4)])
+        upper = call(
+            stage_kernel, "stage", 8,
+            out_shape=jax.ShapeDtypeStruct((half, emb), bf16),
+            in_specs=[hbm] * 5,
+            out_specs=vmem,
+            scratch_shapes=[pltpu.SemaphoreType.DMA],
+            cost_estimate=work(1.0),
+        )(serving_table, lower, slots, tower_bias, score_weight)
+        upper = lax.ppermute(upper, "shard", behind)
+        around = lax.ppermute(lower, "shard", [(3, 15), (7, 3), (11, 7), (15, 11)])
+        serving_parts = (upper, lower, around)
+    else:
+        serving_here = lax.ppermute(serving_table, "shard", behind)
+        serving_parts = (serving_here[:half], serving_here[half:], serving_here[half:])
 
     joined = recv
     if cap < LANES:
@@ -352,14 +407,14 @@
             jax.ShapeDtypeStruct((row_count, emb), bf16),
             jax.ShapeDtypeStruct((row_count, emb), f32),
         ),
-        in_specs=[vmem, vmem],
+        in_specs=[smem] + [vmem] * 4,
         out_specs=(vmem, vmem),
-    )(change, serving_here)
+    )(me, change, *serving_parts)
     req = req.reshape(-1)
 
-    me = lax.axis_index("shard").astype(jnp.int32).reshape(1)
     pitch = req_rows * LANES
-    sent = lax.ppermute(serving_next, "shard", ahead)
+    far = FAR if shards == 16 else ()
+    sent = lax.ppermute(serving_next, "shard", [pair for pair in ahead if pair not in far])
     if shards == 16:
         moves, pieces = [], []
         for sends in SENDS:
@@ -372,6 +427,9 @@
             )(me, req, live)
             for move, rows in zip(sends, found):
                 moves.append(move)
+                if move == 0:
+                    pieces.append(rows)
+                    continue
                 pieces.append(lax.ppermute(rows, "shard", [(i, i ^ move) for i in range(shards)]))
         token = jnp.zeros((8, LANES), f32)
         for takes in TAKES:
@@ -382,6 +440,14 @@
                 out_specs=vmem,
                 cost_estimate=work(0.6 * len(takes) + 0.6),
             )(token, *[pieces[moves.index(move)] for move in takes])
+        held = call(
+            hold_kernel, "hold", 8,
+            out_shape=jax.ShapeDtypeStruct((row_count, emb), bf16),
+            in_specs=[vmem] + [hbm] * len(pieces),
+            out_specs=vmem,
+            cost_estimate=work(0.5),
+        )(live, *pieces)
+        sent_far = lax.ppermute(held, "shard", far)
     else:
         found = call(
             functools.partial(gather_all_kernel, pitch), "gather", 8,
@@ -393,12 +459,12 @@
         got = lax.all_to_all(found, "shard", split_axis=0, concat_axis=0, tiled=True)
         pieces = [got.reshape(shards * capr, emb)]
     scores, new_serving = call(
-        functools.partial(tower_kernel, moves, (feats, requests), pitch), "tower", 58,
+        functools.partial(tower_kernel, moves, (feats, requests)), "tower", 58,
         out_shape=(
             jax.ShapeDtypeStruct((requests // LANES, LANES), f32),
             jax.ShapeDtypeStruct((row_count, emb), bf16),
         ),
-        in_specs=[vmem] + [smem] * 3 + [vmem, hbm, vmem, hbm, vmem, vmem, hbm] + [hbm] * len(pieces),
+        in_specs=[vmem] + [smem] * 2 + [hbm, vmem, hbm, vmem, vmem, hbm] + [hbm] * len(pieces),
         out_specs=(vmem, hbm),
         scratch_shapes=[
             pltpu.VMEM(cross_weight.shape, bf16),
@@ -406,14 +472,24 @@
             pltpu.VMEM((shards * capr, emb), bf16),
             pltpu.VMEM((row_count, emb), bf16),
             pltpu.VMEM((shards * capr, emb), f32),
-            pltpu.VMEM((feats * requests, emb), f32),
+            pltpu.VMEM((feats * 256, emb), f32),
+            pltpu.VMEM((feats * 256, emb), f32),
             pltpu.VMEM((requests, feats * emb), bf16),
             pltpu.SemaphoreType.DMA((4 + len(pieces),)),
         ],
     )(
-        token, me, req, request_slots.T.reshape(-1), live, cross_weight, cross_bias, tower_weight,
-        tower_bias.reshape(1, -1), score_weight.reshape(1, -1), sent, *pieces,
+        token, me, slots, cross_weight, cross_bias, tower_weight,
+        tower_bias, score_weight, sent, *pieces,
     )
+    if far:
+        new_serving = call(
+            functools.partial(deliver_kernel, shards // 2), "deliver", 8,
+            out_shape=jax.ShapeDtypeStruct((row_count, emb), bf16),
+            in_specs=[smem, vmem, hbm],
+            out_specs=hbm,
+            scratch_shapes=[pltpu.SemaphoreType.DMA],
+            input_output_aliases={2: 0},
+        )(me, sent_far, new_serving)
     return (new_table, new_accum.reshape(row_count), new_serving, scores.reshape(requests))
 
 

time: 128 us -> 116 us (0.906)
  waiting for transfers between devices: 39.7 us -> 35.9 us
  starting transfers between devices: 36.4 us -> 32.7 us
  Pallas kernels: 46.6 us -> 43.4 us
  local copies, waits for them, and re-layouts: 3.89 us -> 1.3 us
    all_to_all x1, waiting for transfers between devices: 23.9 us -> 0.11 us  [body(): lax.all_to_all(packed, 'shard', split_axis=0, concat_axis=0, tiled=True)]
    ppermute x2 -> x5, waiting for transfers between devices: 0.01 us -> 22.7 us  [the longest x1 13.3 us: body(): lax.ppermute(aside, 'shard', straight + [(i, i + 3) for i in range(0, sha...]
    ppermute x15, starting transfers between devices: 29.4 us -> 21.8 us  [body(): lax.ppermute(rows, 'shard', [(i, i ^ move) for i in range(shards)])]
    ppermute x2 -> x5, starting transfers between devices: 0.36 us -> 4.31 us  [the longest x1 2.3 us: body(): lax.ppermute(serving_next, 'shard', [pair for pair in ahead if pair not i...]
    ppermute x15, waiting for transfers between devices: 15.8 us -> 13.2 us  [body(): lax.ppermute(rows, 'shard', [(i, i ^ move) for i in range(shards)])]
    pallas_call x6, Pallas kernels: 15.8 us -> 14.3 us  [body(): call(functools.partial(gather_kernel, sends, pitch), 'gather', 4, out_sha...]
    pallas_call x1 -> x4, Pallas kernels: 20.2 us -> 19 us  [the longest x1 18 us: body(): call(functools.partial(tower_kernel, moves, (feats, requests)), 'tower',...]
  transfers between devices with their start and end apart: 18 -> 21, of which waited for: 6 -> 8; matrix products, arithmetic and copies ran while one was open for 1% -> 0% of each run, Pallas kernels for 18% -> 33%
where the time goes in v3:
time: 116 us; the launch traced here: 115 us
  Pallas kernels  43.4 us (37%)
  waiting for transfers between devices  35.9 us (31%)
  starting transfers between devices  32.7 us (28%)
  between operations  1.34 us (1%)
  local copies, waits for them, and re-layouts  1.3 us (1%)
    ppermute x15, starting transfers between devices, body(): lax.ppermute(rows, 'shard', [(i, i ^ move) for i in range(shards)])  21.8 us
    pallas_call x1, Pallas kernels, body(): call(functools.partial(tower_kernel, moves, (feats, requests)), 'tower',...  18 us
    pallas_call x6, Pallas kernels, body(): call(functools.partial(gather_kernel, sends, pitch), 'gather', 4, out_sha...  14.3 us
    ppermute x1, waiting for transfers between devices, body(): lax.ppermute(aside, 'shard', straight + [(i, i + 3) for i in range(0, sha...  13.3 us
    ppermute x15, waiting for transfers between devices, body(): lax.ppermute(rows, 'shard', [(i, i ^ move) for i in range(shards)])  13.2 us
    ppermute x1, waiting for transfers between devices, body(): lax.ppermute(serving_next, 'shard', [pair for pair in ahead if pair not i...  8.08 us
    pallas_call x1, Pallas kernels, body(): call(functools.partial(update_kernel, LANES, cap + 2, req_rows), 'update'...  6.71 us
    all_to_all x1, starting transfers between devices, body(): lax.all_to_all(packed, 'shard', split_axis=0, concat_axis=0, tiled=True)  6.62 us
  transfers between devices with their start and end apart: 21, of which 8 were waited for; matrix products, arithmetic and copies ran while one was open for 0% of the time, Pallas kernels for 33%

profile of v3, /device:TPU:9, one launch (start us, length us, event | category | flops | bytes accessed | tf_op | source)
XLA Modules:
  0.0 114.7 jit_solution(14985499971791296696)
XLA Ops:
  0.7 3.1 %pack.1 = (bf16[16,144,128]{2,1,0:T(8,128)(2,1)}, bf16[2048,128]{1,0:T(8,128)(2,1)}) custom-call(bf16[16,128,128]{2,1,0:T(8,128)(2,1)} %rows_hbm.1, s32[16,128]{1,0:T(8,128)} %ids_hbm.1, s32[16,480]{1,0:T(8,128)} %req_hbm.1, bf16[4096,128]{1,0:T(8,128)(2,1)} %serving_hbm.3, s32[16]{0:T(128)} %counts_ref.1), custom_call_target="tpu_custom_call" | custom-call | tf_op jit(solution)/shard_map/pack/pallas_call | solution.py:339
  3.8 6.6 %all-to-all-start = ((bf16[16,144,128]{2,1,0:T(8,128)(2,1)}), bf16[16,144,128]{2,1,0:T(8,128)(2,1)S(1)}, u32[]{:S(2)}, u32[]{:S(2)}) async-start(bf16[16,144,128]{2,1,0:T(8,128)(2,1)} %get-tuple-element.29), calls=%async_computation | async-start | bytes 1179648 | tf_op jit(solution)/shard_map/all_to_all | solution.py:354
  10.8 13.3 %collective-permute-done.refs_0_.lower_ref = bf16[2048,128]{1,0:T(8,128)(2,1)S(1)} collective-permute-done((bf16[2048,128]{1,0:T(8,128)(2,1)}, bf16[2048,128]{1,0:T(8,128)(2,1)S(1)}, u32[]{:S(2)}, u32[]{:S(2)}) %collective-permute-start) | collective-permute-done | bytes 524320 | tf_op jit(solution)/shard_map/ppermute | solution.py:362
  24.2 0.9 stage.1
  25.1 0.7 collective-permute-start.2
  25.9 6.7 %update.1 = (bf16[4096,128]{1,0:T(8,128)(2,1)}, f32[32,128]{1,0:T(8,128)}, f32[4096,128]{1,0:T(8,128)S(1)}, s32[16,4,128]{2,1,0:T(4,128)S(1)}) custom-call(bf16[16,144,128]{2,1,0:T(8,128)(2,1)S(1)} %all-to-all-done.recv_ref.req_ref, bf16[16,144,128]{2,1,0:T(8,128)(2,1)S(1)} %all-to-all-done.recv_ref.req_ref, f32[32,128]{1,0:T(8,128)S(1)} %bitcast.12, ...), custom_call_target="tpu_custom_call" | custom-call | tf_op jit(solution)/shard_map/update/pallas_call | solution.py:386
  32.6 1.3 %collective-permute-done.1.upper_ref = bf16[2048,128]{1,0:T(8,128)(2,1)S(1)} collective-permute-done((bf16[2048,128]{1,0:T(8,128)(2,1)}, bf16[2048,128]{1,0:T(8,128)(2,1)S(1)}, u32[]{:S(2)}, u32[]{:S(2)}) %collective-permute-start.1) | collective-permute-done | bytes 524320 | tf_op jit(solution)/shard_map/ppermute | solution.py:371
  34.3 2.5 %gather.7 = (bf16[480,128]{1,0:T(8,128)(2,1)S(1)}, bf16[480,128]{1,0:T(8,128)(2,1)S(1)}, bf16[480,128]{1,0:T(8,128)(2,1)S(1)}) custom-call(s32[1]{0:T(128)} %bitcast.2.me_ref, s32[8192]{0:T(1024)S(1)} %bitcast.6, f32[4096,128]{1,0:T(8,128)S(1)} %get-tuple-element.34.live_ref), custom_call_target="tpu_custom_call" | custom-call | bytes 5399999 | tf_op jit(solution)/shard_map/gather/pallas_call | solution.py:421
  36.9 1.8 %collective-permute-start.4 = (bf16[480,128]{1,0:T(8,128)(2,1)S(1)}, bf16[480,128]{1,0:T(8,128)(2,1)S(1)}, u32[]{:S(2)}, u32[]{:S(2)}) collective-permute-start(bf16[480,128]{1,0:T(8,128)(2,1)S(1)} %get-tuple-element.36), channel_id=1, source_target_pairs={{0,9},{1,8},{2,11},{3,10},{4,13},{5,12},{6,15},{7,14},{8,1},{9,0},... | collective-permute-start | bytes 368648 | tf_op jit(solution)/shard_map/ppermute | solution.py:433
  38.7 1.2 %collective-permute-start.5 = (bf16[480,128]{1,0:T(8,128)(2,1)S(1)}, bf16[480,128]{1,0:T(8,128)(2,1)S(1)}, u32[]{:S(2)}, u32[]{:S(2)}) collective-permute-start(bf16[480,128]{1,0:T(8,128)(2,1)S(1)} %get-tuple-element.37), channel_id=1, source_target_pairs={{0,1},{1,0},{2,3},{3,2},{4,5},{5,4},{6,7},{7,6},{8,9},{9,8},{10,11... | collective-permute-start | bytes 368648 | tf_op jit(solution)/shard_map/ppermute | solution.py:433
  39.9 1.6 %gather.6 = bf16[480,128]{1,0:T(8,128)(2,1)S(1)} custom-call(s32[1]{0:T(128)} %bitcast.2.me_ref, s32[8192]{0:T(1024)S(1)} %bitcast.7, f32[4096,128]{1,0:T(8,128)S(1)} %get-tuple-element.34.live_ref), custom_call_target="tpu_custom_call" | custom-call | bytes 1800000 | tf_op jit(solution)/shard_map/gather/pallas_call | solution.py:421
  41.5 2.5 %gather.8 = (bf16[480,128]{1,0:T(8,128)(2,1)S(1)}, bf16[480,128]{1,0:T(8,128)(2,1)S(1)}, bf16[480,128]{1,0:T(8,128)(2,1)S(1)}) custom-call(s32[1]{0:T(128)} %bitcast.2.me_ref, s32[8192]{0:T(1024)S(1)} %bitcast.8, f32[4096,128]{1,0:T(8,128)S(1)} %get-tuple-element.34.live_ref), custom_call_target="tpu_custom_call" | custom-call | bytes 5399999 | tf_op jit(solution)/shard_map/gather/pallas_call | solution.py:421
  44.1 3.0 %collective-permute-start.7 = (bf16[480,128]{1,0:T(8,128)(2,1)S(1)}, bf16[480,128]{1,0:T(8,128)(2,1)S(1)}, u32[]{:S(2)}, u32[]{:S(2)}) collective-permute-start(bf16[480,128]{1,0:T(8,128)(2,1)S(1)} %get-tuple-element.39), channel_id=1, source_target_pairs={{0,2},{1,3},{2,0},{3,1},{4,6},{5,7},{6,4},{7,5},{8,10},{9,11},{10,... | collective-permute-start | bytes 368648 | tf_op jit(solution)/shard_map/ppermute | solution.py:433
  47.1 2.3 %collective-permute-start.8 = (bf16[480,128]{1,0:T(8,128)(2,1)S(1)}, bf16[480,128]{1,0:T(8,128)(2,1)S(1)}, u32[]{:S(2)}, u32[]{:S(2)}) collective-permute-start(bf16[480,128]{1,0:T(8,128)(2,1)S(1)} %get-tuple-element.40), channel_id=1, source_target_pairs={{0,11},{1,10},{2,9},{3,8},{4,15},{5,14},{6,13},{7,12},{8,3},{9,2},... | collective-permute-start | bytes 368648 | tf_op jit(solution)/shard_map/ppermute | solution.py:433
  49.5 2.5 %gather.9 = (bf16[480,128]{1,0:T(8,128)(2,1)S(1)}, bf16[480,128]{1,0:T(8,128)(2,1)S(1)}, bf16[480,128]{1,0:T(8,128)(2,1)S(1)}) custom-call(s32[1]{0:T(128)} %bitcast.2.me_ref, s32[8192]{0:T(1024)S(1)} %bitcast.9, f32[4096,128]{1,0:T(8,128)S(1)} %get-tuple-element.34.live_ref), custom_call_target="tpu_custom_call" | custom-call | bytes 5399999 | tf_op jit(solution)/shard_map/gather/pallas_call | solution.py:421
  52.0 2.5 %gather.10 = (bf16[480,128]{1,0:T(8,128)(2,1)S(1)}, bf16[480,128]{1,0:T(8,128)(2,1)S(1)}, bf16[480,128]{1,0:T(8,128)(2,1)S(1)}) custom-call(s32[1]{0:T(128)} %bitcast.2.me_ref, s32[8192]{0:T(1024)S(1)} %bitcast.10, f32[4096,128]{1,0:T(8,128)S(1)} %get-tuple-element.34.live_ref), custom_call_target="tpu_custom_call" | custom-call | bytes 5399999 | tf_op jit(solution)/shard_map/gather/pallas_call | solution.py:421
  54.6 1.6 %collective-permute-start.6 = (bf16[480,128]{1,0:T(8,128)(2,1)S(1)}, bf16[480,128]{1,0:T(8,128)(2,1)S(1)}, u32[]{:S(2)}, u32[]{:S(2)}) collective-permute-start(bf16[480,128]{1,0:T(8,128)(2,1)S(1)} %get-tuple-element.38), channel_id=1, source_target_pairs={{0,10},{1,11},{2,8},{3,9},{4,14},{5,15},{6,12},{7,13},{8,2},{9,3},... | collective-permute-start | bytes 368648 | tf_op jit(solution)/shard_map/ppermute | solution.py:433
  56.3 3.3 %collective-permute-start.11 = (bf16[480,128]{1,0:T(8,128)(2,1)S(1)}, bf16[480,128]{1,0:T(8,128)(2,1)S(1)}, u32[]{:S(2)}, u32[]{:S(2)}) collective-permute-start(bf16[480,128]{1,0:T(8,128)(2,1)S(1)} %get-tuple-element.43), channel_id=1, source_target_pairs={{0,4},{1,5},{2,6},{3,7},{4,0},{5,1},{6,2},{7,3},{8,12},{9,13},{10,... | collective-permute-start | bytes 368648 | tf_op jit(solution)/shard_map/ppermute | solution.py:433
  59.6 0.8 collective-permute-start.9
  60.4 2.5 %gather.11 = (bf16[480,128]{1,0:T(8,128)(2,1)S(1)}, bf16[480,128]{1,0:T(8,128)(2,1)S(1)}, bf16[480,128]{1,0:T(8,128)(2,1)S(1)}) custom-call(s32[1]{0:T(128)} %bitcast.2.me_ref, s32[8192]{0:T(1024)S(1)} %bitcast.11, f32[4096,128]{1,0:T(8,128)S(1)} %get-tuple-element.34.live_ref), custom_call_target="tpu_custom_call" | custom-call | bytes 5399999 | tf_op jit(solution)/shard_map/gather/pallas_call | solution.py:421
  62.9 1.6 %collective-permute-done.6.refs_3_.refs_0_ = bf16[480,128]{1,0:T(8,128)(2,1)S(1)} collective-permute-done((bf16[480,128]{1,0:T(8,128)(2,1)S(1)}, bf16[480,128]{1,0:T(8,128)(2,1)S(1)}, u32[]{:S(2)}, u32[]{:S(2)}) %collective-permute-start.6) | collective-permute-done | bytes 122912 | tf_op jit(solution)/shard_map/ppermute | solution.py:433
  64.5 2.9 %collective-permute-done.10.refs_7_.refs_1_ = bf16[480,128]{1,0:T(8,128)(2,1)S(1)} collective-permute-done((bf16[480,128]{1,0:T(8,128)(2,1)S(1)}, bf16[480,128]{1,0:T(8,128)(2,1)S(1)}, u32[]{:S(2)}, u32[]{:S(2)}) %collective-permute-start.10) | collective-permute-done | bytes 122912 | tf_op jit(solution)/shard_map/ppermute | solution.py:433
  67.4 2.5 %collective-permute-start.12 = (bf16[480,128]{1,0:T(8,128)(2,1)S(1)}, bf16[480,128]{1,0:T(8,128)(2,1)S(1)}, u32[]{:S(2)}, u32[]{:S(2)}) collective-permute-start(bf16[480,128]{1,0:T(8,128)(2,1)S(1)} %get-tuple-element.44), channel_id=1, source_target_pairs={{0,13},{1,12},{2,15},{3,14},{4,9},{5,8},{6,11},{7,10},{8,5},{9,4},... | collective-permute-start | bytes 368648 | tf_op jit(solution)/shard_map/ppermute | solution.py:433
  70.0 5.1 %collective-permute-start.17 = (bf16[480,128]{1,0:T(8,128)(2,1)S(1)}, bf16[480,128]{1,0:T(8,128)(2,1)S(1)}, u32[]{:S(2)}, u32[]{:S(2)}) collective-permute-start(bf16[480,128]{1,0:T(8,128)(2,1)S(1)} %get-tuple-element.49), channel_id=1, source_target_pairs={{0,7},{1,6},{2,5},{3,4},{4,3},{5,2},{6,1},{7,0},{8,15},{9,14},{10,... | collective-permute-start | bytes 368648 | tf_op jit(solution)/shard_map/ppermute | solution.py:433
  75.1 2.3 %collective-permute-start.19 = (bf16[4096,128]{1,0:T(8,128)(2,1)S(1)}, bf16[4096,128]{1,0:T(8,128)(2,1)}, u32[]{:S(2)}, u32[]{:S(2)}) collective-permute-start(bf16[4096,128]{1,0:T(8,128)(2,1)S(1)} %get-tuple-element.51), channel_id=1, source_target_pairs={{0,1},{1,2},{2,3},{3,4},{4,5},{5,6},{6,7},{8,9},{9,10},{10,11},{11... | collective-permute-start | bytes 3145736 | tf_op jit(solution)/shard_map/ppermute | solution.py:417
  77.4 3.5 %collective-permute-done.12.refs_9_.refs_0_ = bf16[480,128]{1,0:T(8,128)(2,1)S(1)} collective-permute-done((bf16[480,128]{1,0:T(8,128)(2,1)S(1)}, bf16[480,128]{1,0:T(8,128)(2,1)S(1)}, u32[]{:S(2)}, u32[]{:S(2)}) %collective-permute-start.12) | collective-permute-done | bytes 122912 | tf_op jit(solution)/shard_map/ppermute | solution.py:433
  80.8 5.2 %collective-permute-done.16.refs_13_ = bf16[480,128]{1,0:T(8,128)(2,1)S(1)} collective-permute-done((bf16[480,128]{1,0:T(8,128)(2,1)S(1)}, bf16[480,128]{1,0:T(8,128)(2,1)S(1)}, u32[]{:S(2)}, u32[]{:S(2)}) %collective-permute-start.16) | collective-permute-done | bytes 122912 | tf_op jit(solution)/shard_map/ppermute | solution.py:433
  86.2 0.5 copy-done.15
  86.8 0.9 collective-permute-start.18
  87.9 0.6 copy-done.22
  88.4 8.1 %collective-permute-done.19.serving_ref = bf16[4096,128]{1,0:T(8,128)(2,1)} collective-permute-done((bf16[4096,128]{1,0:T(8,128)(2,1)S(1)}, bf16[4096,128]{1,0:T(8,128)(2,1)}, u32[]{:S(2)}, u32[]{:S(2)}) %collective-permute-start.19) | collective-permute-done | bytes 1048608 | tf_op jit(solution)/shard_map/ppermute | solution.py:417
  96.5 18.0 %tower.1 = (f32[8,128]{1,0:T(8,128)}, bf16[4096,128]{1,0:T(8,128)(2,1)}) custom-call(f32[8,128]{1,0:T(8,128)} %copy-done.22, s32[1]{0:T(128)} %bitcast.2.me_ref, s32[5120]{0:T(1024)} %copy-done.18, bf16[3,640,640]{2,1,0:T(8,128)(2,1)} %cross_hbm.1, bf16[3,640]{1,0:T(4,128)(2,1)} %cross_bias_ref.1, bf16[640,4096]{1,0:T(8,128)(2,1)} %tower_hbm.1, ...), custom_call_target="tpu_custom_call" | custom-call | tf_op jit(solution)/shard_map/tower/pallas_call | solution.py:461
  (83 shorter events, 1.4 us)
Async XLA Ops:
  0.6 23.5 %copy-start = (bf16[4096,128]{1,0:T(8,128)(2,1)S(1)}, bf16[4096,128]{1,0:T(8,128)(2,1)}, u32[]{:S(2)}) copy-start(bf16[4096,128]{1,0:T(8,128)(2,1)} %serving_hbm.3) | copy-start | bytes 3145732
  0.7 25.2 %copy-start.21 = (f32[4096]{0:T(1024)S(1)}, f32[4096]{0:T(1024)}, u32[]{:S(2)}) copy-start(f32[4096]{0:T(1024)} %param.14) | copy-start | bytes 49156
  0.7 25.2 %copy-start.13 = (bf16[4096,128]{1,0:T(8,128)(2,1)S(1)}, bf16[4096,128]{1,0:T(8,128)(2,1)}, u32[]{:S(2)}) copy-start(bf16[4096,128]{1,0:T(8,128)(2,1)} %item_hbm.1) | copy-start | bytes 3145732
  3.8 22.2 %all-to-all-start = ((bf16[16,144,128]{2,1,0:T(8,128)(2,1)}), bf16[16,144,128]{2,1,0:T(8,128)(2,1)S(1)}, u32[]{:S(2)}, u32[]{:S(2)}) async-start(bf16[16,144,128]{2,1,0:T(8,128)(2,1)} %get-tuple-element.29), calls=%async_computation | async-start | bytes 1179648 | tf_op jit(solution)/shard_map/all_to_all | solution.py:354
  10.4 13.8 %collective-permute-start = (bf16[2048,128]{1,0:T(8,128)(2,1)}, bf16[2048,128]{1,0:T(8,128)(2,1)S(1)}, u32[]{:S(2)}, u32[]{:S(2)}) collective-permute-start(bf16[2048,128]{1,0:T(8,128)(2,1)} %get-tuple-element.33), channel_id=1, source_target_pairs={{1,0},{2,1},{3,2},{5,4},{6,5},{7,6},{9,8},{10,9},{11,10},{13,12},{... | collective-permute-start | bytes 1572872 | tf_op jit(solution)/shard_map/ppermute | solution.py:362
  10.8 23.5 %copy-start.18 = (s32[5120]{0:T(1024)}, s32[5120]{0:T(1024)S(1)}, u32[]{:S(2)}) copy-start(s32[5120]{0:T(1024)S(1)} %reshape.35.refs_1_.slots_ref) | copy-start | bytes 61444
  10.8 23.5 %copy-start.19 = (bf16[1,4096]{1,0:T(2,128)(2,1)}, bf16[1,4096]{1,0:T(2,128)(2,1)S(1)}, u32[]{:S(2)}) copy-start(bf16[1,4096]{1,0:T(2,128)(2,1)S(1)} %reshape.36.refs_2_.tower_bias_ref) | copy-start | bytes 24580
  10.8 23.5 %copy-start.20 = (bf16[1,4096]{1,0:T(2,128)(2,1)}, bf16[1,4096]{1,0:T(2,128)(2,1)S(1)}, u32[]{:S(2)}) copy-start(bf16[1,4096]{1,0:T(2,128)(2,1)S(1)} %reshape.37.refs_3_.score_ref) | copy-start | bytes 24580
  25.0 8.9 %collective-permute-start.1 = (bf16[2048,128]{1,0:T(8,128)(2,1)}, bf16[2048,128]{1,0:T(8,128)(2,1)S(1)}, u32[]{:S(2)}, u32[]{:S(2)}) collective-permute-start(bf16[2048,128]{1,0:T(8,128)(2,1)} %stage.1), channel_id=1, source_target_pairs={{0,15},{1,0},{2,1},{3,2},{4,3},{5,4},{6,5},{7,6},{8,7},{9,8},{10,9... | collective-permute-start | bytes 1572872 | tf_op jit(solution)/shard_map/ppermute | solution.py:371
  25.1 8.8 %collective-permute-start.2 = (bf16[2048,128]{1,0:T(8,128)(2,1)S(1)}, bf16[2048,128]{1,0:T(8,128)(2,1)S(1)}, u32[]{:S(2)}, u32[]{:S(2)}) collective-permute-start(bf16[2048,128]{1,0:T(8,128)(2,1)S(1)} %collective-permute-done.refs_0_.lower_ref), channel_id=1, source_target_pairs={{3,15},{7,3},{11,7},{15,11},{19,31},{23,19},{27,23},{31,27}} | collective-permute-start | bytes 1572872 | tf_op jit(solution)/shard_map/ppermute | solution.py:372
  36.9 17.7 %collective-permute-start.4 = (bf16[480,128]{1,0:T(8,128)(2,1)S(1)}, bf16[480,128]{1,0:T(8,128)(2,1)S(1)}, u32[]{:S(2)}, u32[]{:S(2)}) collective-permute-start(bf16[480,128]{1,0:T(8,128)(2,1)S(1)} %get-tuple-element.36), channel_id=1, source_target_pairs={{0,9},{1,8},{2,11},{3,10},{4,13},{5,12},{6,15},{7,14},{8,1},{9,0},... | collective-permute-start | bytes 368648 | tf_op jit(solution)/shard_map/ppermute | solution.py:433
  38.7 17.5 %collective-permute-start.5 = (bf16[480,128]{1,0:T(8,128)(2,1)S(1)}, bf16[480,128]{1,0:T(8,128)(2,1)S(1)}, u32[]{:S(2)}, u32[]{:S(2)}) collective-permute-start(bf16[480,128]{1,0:T(8,128)(2,1)S(1)} %get-tuple-element.37), channel_id=1, source_target_pairs={{0,1},{1,0},{2,3},{3,2},{4,5},{5,4},{6,7},{7,6},{8,9},{9,8},{10,11... | collective-permute-start | bytes 368648 | tf_op jit(solution)/shard_map/ppermute | solution.py:433
  41.5 14.8 %collective-permute-start.3 = (bf16[480,128]{1,0:T(8,128)(2,1)S(1)}, bf16[480,128]{1,0:T(8,128)(2,1)S(1)}, u32[]{:S(2)}, u32[]{:S(2)}) collective-permute-start(bf16[480,128]{1,0:T(8,128)(2,1)S(1)} %gather.6), channel_id=1, source_target_pairs={{0,8},{1,9},{2,10},{3,11},{4,12},{5,13},{6,14},{7,15},{8,0},{9,1},... | collective-permute-start | bytes 368648 | tf_op jit(solution)/shard_map/ppermute | solution.py:433
  44.1 15.5 %collective-permute-start.7 = (bf16[480,128]{1,0:T(8,128)(2,1)S(1)}, bf16[480,128]{1,0:T(8,128)(2,1)S(1)}, u32[]{:S(2)}, u32[]{:S(2)}) collective-permute-start(bf16[480,128]{1,0:T(8,128)(2,1)S(1)} %get-tuple-element.39), channel_id=1, source_target_pairs={{0,2},{1,3},{2,0},{3,1},{4,6},{5,7},{6,4},{7,5},{8,10},{9,11},{10,... | collective-permute-start | bytes 368648 | tf_op jit(solution)/shard_map/ppermute | solution.py:433
  47.1 13.2 %collective-permute-start.8 = (bf16[480,128]{1,0:T(8,128)(2,1)S(1)}, bf16[480,128]{1,0:T(8,128)(2,1)S(1)}, u32[]{:S(2)}, u32[]{:S(2)}) collective-permute-start(bf16[480,128]{1,0:T(8,128)(2,1)S(1)} %get-tuple-element.40), channel_id=1, source_target_pairs={{0,11},{1,10},{2,9},{3,8},{4,15},{5,14},{6,13},{7,12},{8,3},{9,2},... | collective-permute-start | bytes 368648 | tf_op jit(solution)/shard_map/ppermute | solution.py:433
  54.6 33.1 %copy-start.1 = (bf16[480,128]{1,0:T(8,128)(2,1)}, bf16[480,128]{1,0:T(8,128)(2,1)S(1)}, u32[]{:S(2)}) copy-start(bf16[480,128]{1,0:T(8,128)(2,1)S(1)} %collective-permute-done.4.refs_1_) | copy-start | bytes 368644
  54.6 9.9 %collective-permute-start.6 = (bf16[480,128]{1,0:T(8,128)(2,1)S(1)}, bf16[480,128]{1,0:T(8,128)(2,1)S(1)}, u32[]{:S(2)}, u32[]{:S(2)}) collective-permute-start(bf16[480,128]{1,0:T(8,128)(2,1)S(1)} %get-tuple-element.38), channel_id=1, source_target_pairs={{0,10},{1,11},{2,8},{3,9},{4,14},{5,15},{6,12},{7,13},{8,2},{9,3},... | collective-permute-start | bytes 368648 | tf_op jit(solution)/shard_map/ppermute | solution.py:433
  56.2 31.5 %copy-start.2 = (bf16[480,128]{1,0:T(8,128)(2,1)}, bf16[480,128]{1,0:T(8,128)(2,1)S(1)}, u32[]{:S(2)}) copy-start(bf16[480,128]{1,0:T(8,128)(2,1)S(1)} %collective-permute-done.5.refs_2_) | copy-start | bytes 368644
  56.2 11.2 %collective-permute-start.10 = (bf16[480,128]{1,0:T(8,128)(2,1)S(1)}, bf16[480,128]{1,0:T(8,128)(2,1)S(1)}, u32[]{:S(2)}, u32[]{:S(2)}) collective-permute-start(bf16[480,128]{1,0:T(8,128)(2,1)S(1)} %get-tuple-element.42), channel_id=1, source_target_pairs={{0,12},{1,13},{2,14},{3,15},{4,8},{5,9},{6,10},{7,11},{8,4},{9,5},... | collective-permute-start | bytes 368648 | tf_op jit(solution)/shard_map/ppermute | solution.py:433
  56.2 31.5 %copy-start.3 = (bf16[480,128]{1,0:T(8,128)(2,1)}, bf16[480,128]{1,0:T(8,128)(2,1)S(1)}, u32[]{:S(2)}) copy-start(bf16[480,128]{1,0:T(8,128)(2,1)S(1)} %collective-permute-done.3.refs_0_) | copy-start | bytes 368644
  56.3 13.7 %collective-permute-start.11 = (bf16[480,128]{1,0:T(8,128)(2,1)S(1)}, bf16[480,128]{1,0:T(8,128)(2,1)S(1)}, u32[]{:S(2)}, u32[]{:S(2)}) collective-permute-start(bf16[480,128]{1,0:T(8,128)(2,1)S(1)} %get-tuple-element.43), channel_id=1, source_target_pairs={{0,4},{1,5},{2,6},{3,7},{4,0},{5,1},{6,2},{7,3},{8,12},{9,13},{10,... | collective-permute-start | bytes 368648 | tf_op jit(solution)/shard_map/ppermute | solution.py:433
  59.6 28.1 %copy-start.4 = (bf16[480,128]{1,0:T(8,128)(2,1)}, bf16[480,128]{1,0:T(8,128)(2,1)S(1)}, u32[]{:S(2)}) copy-start(bf16[480,128]{1,0:T(8,128)(2,1)S(1)} %collective-permute-done.7.refs_4_.refs_1_) | copy-start | bytes 368644
  59.6 10.4 %collective-permute-start.9 = (bf16[480,128]{1,0:T(8,128)(2,1)S(1)}, bf16[480,128]{1,0:T(8,128)(2,1)S(1)}, u32[]{:S(2)}, u32[]{:S(2)}) collective-permute-start(bf16[480,128]{1,0:T(8,128)(2,1)S(1)} %get-tuple-element.41), channel_id=1, source_target_pairs={{0,3},{1,2},{2,1},{3,0},{4,7},{5,6},{6,5},{7,4},{8,11},{9,10},{10,... | collective-permute-start | bytes 368648 | tf_op jit(solution)/shard_map/ppermute | solution.py:433
  60.4 27.4 %copy-start.5 = (bf16[480,128]{1,0:T(8,128)(2,1)}, bf16[480,128]{1,0:T(8,128)(2,1)S(1)}, u32[]{:S(2)}) copy-start(bf16[480,128]{1,0:T(8,128)(2,1)S(1)} %collective-permute-done.8.refs_5_.refs_2_) | copy-start | bytes 368644
  60.4 14.7 %collective-permute-start.13 = (bf16[480,128]{1,0:T(8,128)(2,1)S(1)}, bf16[480,128]{1,0:T(8,128)(2,1)S(1)}, u32[]{:S(2)}, u32[]{:S(2)}) collective-permute-start(bf16[480,128]{1,0:T(8,128)(2,1)S(1)} %get-tuple-element.45), channel_id=1, source_target_pairs={{0,5},{1,4},{2,7},{3,6},{4,1},{5,0},{6,3},{7,2},{8,13},{9,12},{10,... | collective-permute-start | bytes 368648 | tf_op jit(solution)/shard_map/ppermute | solution.py:433
  64.5 10.5 %collective-permute-start.14 = (bf16[480,128]{1,0:T(8,128)(2,1)S(1)}, bf16[480,128]{1,0:T(8,128)(2,1)S(1)}, u32[]{:S(2)}, u32[]{:S(2)}) collective-permute-start(bf16[480,128]{1,0:T(8,128)(2,1)S(1)} %get-tuple-element.46), channel_id=1, source_target_pairs={{0,14},{1,15},{2,12},{3,13},{4,10},{5,11},{6,8},{7,9},{8,6},{9,7},... | collective-permute-start | bytes 368648 | tf_op jit(solution)/shard_map/ppermute | solution.py:433
  67.4 13.4 %collective-permute-start.12 = (bf16[480,128]{1,0:T(8,128)(2,1)S(1)}, bf16[480,128]{1,0:T(8,128)(2,1)S(1)}, u32[]{:S(2)}, u32[]{:S(2)}) collective-permute-start(bf16[480,128]{1,0:T(8,128)(2,1)S(1)} %get-tuple-element.44), channel_id=1, source_target_pairs={{0,13},{1,12},{2,15},{3,14},{4,9},{5,8},{6,11},{7,10},{8,5},{9,4},... | collective-permute-start | bytes 368648 | tf_op jit(solution)/shard_map/ppermute | solution.py:433
  69.9 16.1 %collective-permute-start.16 = (bf16[480,128]{1,0:T(8,128)(2,1)S(1)}, bf16[480,128]{1,0:T(8,128)(2,1)S(1)}, u32[]{:S(2)}, u32[]{:S(2)}) collective-permute-start(bf16[480,128]{1,0:T(8,128)(2,1)S(1)} %get-tuple-element.48), channel_id=1, source_target_pairs={{0,15},{1,14},{2,13},{3,12},{4,11},{5,10},{6,9},{7,8},{8,7},{9,6},... | collective-permute-start | bytes 368648 | tf_op jit(solution)/shard_map/ppermute | solution.py:433
  70.0 16.1 %collective-permute-start.17 = (bf16[480,128]{1,0:T(8,128)(2,1)S(1)}, bf16[480,128]{1,0:T(8,128)(2,1)S(1)}, u32[]{:S(2)}, u32[]{:S(2)}) collective-permute-start(bf16[480,128]{1,0:T(8,128)(2,1)S(1)} %get-tuple-element.49), channel_id=1, source_target_pairs={{0,7},{1,6},{2,5},{3,4},{4,3},{5,2},{6,1},{7,0},{8,15},{9,14},{10,... | collective-permute-start | bytes 368648 | tf_op jit(solution)/shard_map/ppermute | solution.py:433
  75.0 11.0 %collective-permute-start.15 = (bf16[480,128]{1,0:T(8,128)(2,1)S(1)}, bf16[480,128]{1,0:T(8,128)(2,1)S(1)}, u32[]{:S(2)}, u32[]{:S(2)}) collective-permute-start(bf16[480,128]{1,0:T(8,128)(2,1)S(1)} %get-tuple-element.47), channel_id=1, source_target_pairs={{0,6},{1,7},{2,4},{3,5},{4,2},{5,3},{6,0},{7,1},{8,14},{9,15},{10,... | collective-permute-start | bytes 368648 | tf_op jit(solution)/shard_map/ppermute | solution.py:433
  75.1 21.5 %collective-permute-start.19 = (bf16[4096,128]{1,0:T(8,128)(2,1)S(1)}, bf16[4096,128]{1,0:T(8,128)(2,1)}, u32[]{:S(2)}, u32[]{:S(2)}) collective-permute-start(bf16[4096,128]{1,0:T(8,128)(2,1)S(1)} %get-tuple-element.51), channel_id=1, source_target_pairs={{0,1},{1,2},{2,3},{3,4},{4,5},{5,6},{6,7},{8,9},{9,10},{10,11},{11... | collective-permute-start | bytes 3145736 | tf_op jit(solution)/shard_map/ppermute | solution.py:417
  86.8 27.7 %collective-permute-start.18 = (bf16[4096,128]{1,0:T(8,128)(2,1)S(1)}, bf16[4096,128]{1,0:T(8,128)(2,1)S(1)}, u32[]{:S(2)}, u32[]{:S(2)}) collective-permute-start(bf16[4096,128]{1,0:T(8,128)(2,1)S(1)} %hold.1), channel_id=1, source_target_pairs={{7,8},{15,0},{23,24},{31,16}} | collective-permute-start | bytes 3145736 | tf_op jit(solution)/shard_map/ppermute | solution.py:450
  (15 other events, 168.0 us)

commit v4 on v3

--- a/solution.py
+++ b/solution.py
@@ -21,7 +21,6 @@
 
 SENDS = ((8,), (9, 1, 10), (2, 11, 3), (12, 4, 13), (5, 14, 6), (15, 7, 0))
 TAKES = ((8, 9, 1), (10, 2, 11), (3, 12, 4), (13, 5, 14))
-FAR = ((7, 8), (15, 0))
 
 
 def work(micros):
@@ -220,12 +219,10 @@
     refs[-1][...] = live_ref[...].astype(jnp.bfloat16)
 
 
-def deliver_kernel(every, me_ref, far_ref, near_hbm, out_hbm, sem):
-    @pl.when(lax.rem(me_ref[0], every) == 0)
-    def _():
-        store = pltpu.make_async_copy(far_ref, out_hbm, sem)
-        store.start()
-        store.wait()
+def deliver_kernel(from_ref, out_hbm, sem):
+    store = pltpu.make_async_copy(from_ref, out_hbm, sem)
+    store.start()
+    store.wait()
 
 
 def token_kernel(token_ref, *refs):
@@ -234,12 +231,12 @@
 
 def tower_kernel(
     moves, shape, token_ref, me_ref, slots_ref, cross_hbm, cross_bias_ref, tower_hbm,
-    tower_bias_ref, score_ref, serving_ref, *refs,
+    tower_bias_ref, score_ref, *refs,
 ):
     f32, bf16 = jnp.float32, jnp.bfloat16
     feats, requests = shape
-    pieces = refs[:-11]
-    out_ref, serving_out, cross_ref, tower_ref, got_ref, served_ref = refs[-11:-5]
+    pieces = refs[:-9]
+    out_ref, cross_ref, tower_ref, got_ref = refs[-9:-5]
     wide_ref, plane_a, plane_b, crossed_ref, sems = refs[-5:]
     planes = (plane_a, plane_b)
     me = me_ref[0]
@@ -249,22 +246,17 @@
         if moves is not None:
             start = pl.multiple_of(lax.bitwise_xor(me, moves[k]) * width, width)
         loads.append(
-            pltpu.make_async_copy(piece, got_ref.at[pl.ds(start, width), :], sems.at[4 + k])
+            pltpu.make_async_copy(piece, got_ref.at[pl.ds(start, width), :], sems.at[2 + k])
         )
     load_cross = pltpu.make_async_copy(cross_hbm, cross_ref, sems.at[0])
     load_tower = pltpu.make_async_copy(tower_hbm, tower_ref, sems.at[1])
-    load_serving = pltpu.make_async_copy(serving_ref, served_ref, sems.at[2])
-    store_serving = pltpu.make_async_copy(served_ref, serving_out, sems.at[3])
     for load in loads:
         load.start()
     load_cross.start()
-    load_serving.start()
     load_tower.start()
     for load in loads:
         load.wait()
     wide_ref[...] = got_ref[...].astype(f32)
-    load_serving.wait()
-    store_serving.start()
     chunk = 256
     batch = 64
 
@@ -312,7 +304,6 @@
     for k in range(requests // LANES):
         column = jnp.sum(total[k * LANES : (k + 1) * LANES, :], axis=1, keepdims=True)
         out_ref[k : k + 1, :] = jnp.sum(jnp.where(eye, column, 0.0), axis=0, keepdims=True)
-    store_serving.wait()
 
 
 def body(
@@ -413,8 +404,7 @@
     req = req.reshape(-1)
 
     pitch = req_rows * LANES
-    far = FAR if shards == 16 else ()
-    sent = lax.ppermute(serving_next, "shard", [pair for pair in ahead if pair not in far])
+    serving_next = live
     if shards == 16:
         moves, pieces = [], []
         for sends in SENDS:
@@ -440,14 +430,6 @@
                 out_specs=vmem,
                 cost_estimate=work(0.6 * len(takes) + 0.6),
             )(token, *[pieces[moves.index(move)] for move in takes])
-        held = call(
-            hold_kernel, "hold", 8,
-            out_shape=jax.ShapeDtypeStruct((row_count, emb), bf16),
-            in_specs=[vmem] + [hbm] * len(pieces),
-            out_specs=vmem,
-            cost_estimate=work(0.5),
-        )(live, *pieces)
-        sent_far = lax.ppermute(held, "shard", far)
     else:
         found = call(
             functools.partial(gather_all_kernel, pitch), "gather", 8,
@@ -458,38 +440,40 @@
         moves, token = None, jnp.zeros((8, LANES), f32)
         got = lax.all_to_all(found, "shard", split_axis=0, concat_axis=0, tiled=True)
         pieces = [got.reshape(shards * capr, emb)]
-    scores, new_serving = call(
+    held = call(
+        hold_kernel, "hold", 8,
+        out_shape=jax.ShapeDtypeStruct((row_count, emb), bf16),
+        in_specs=[vmem] + [hbm] * len(pieces),
+        out_specs=vmem,
+        cost_estimate=work(0.5),
+    )(live, *pieces)
+    sent = lax.ppermute(held, "shard", ahead)
+    scores = call(
         functools.partial(tower_kernel, moves, (feats, requests)), "tower", 58,
-        out_shape=(
-            jax.ShapeDtypeStruct((requests // LANES, LANES), f32),
-            jax.ShapeDtypeStruct((row_count, emb), bf16),
-        ),
-        in_specs=[vmem] + [smem] * 2 + [hbm, vmem, hbm, vmem, vmem, hbm] + [hbm] * len(pieces),
-        out_specs=(vmem, hbm),
+        out_shape=jax.ShapeDtypeStruct((requests // LANES, LANES), f32),
+        in_specs=[vmem] + [smem] * 2 + [hbm, vmem, hbm, vmem, vmem] + [hbm] * len(pieces),
+        out_specs=vmem,
         scratch_shapes=[
             pltpu.VMEM(cross_weight.shape, bf16),
             pltpu.VMEM(tower_weight.shape, bf16),
             pltpu.VMEM((shards * capr, emb), bf16),
-            pltpu.VMEM((row_count, emb), bf16),
             pltpu.VMEM((shards * capr, emb), f32),
             pltpu.VMEM((feats * 256, emb), f32),
             pltpu.VMEM((feats * 256, emb), f32),
             pltpu.VMEM((requests, feats * emb), bf16),
-            pltpu.SemaphoreType.DMA((4 + len(pieces),)),
+            pltpu.SemaphoreType.DMA((2 + len(pieces),)),
         ],
     )(
         token, me, slots, cross_weight, cross_bias, tower_weight,
-        tower_bias, score_weight, sent, *pieces,
+        tower_bias, score_weight, *pieces,
     )
-    if far:
-        new_serving = call(
-            functools.partial(deliver_kernel, shards // 2), "deliver", 8,
-            out_shape=jax.ShapeDtypeStruct((row_count, emb), bf16),
-            in_specs=[smem, vmem, hbm],
-            out_specs=hbm,
-            scratch_shapes=[pltpu.SemaphoreType.DMA],
-            input_output_aliases={2: 0},
-        )(me, sent_far, new_serving)
+    new_serving = call(
+        deliver_kernel, "deliver", 8,
+        out_shape=jax.ShapeDtypeStruct((row_count, emb), bf16),
+        in_specs=[vmem],
+        out_specs=hbm,
+        scratch_shapes=[pltpu.SemaphoreType.DMA],
+    )(sent)
     return (new_table, new_accum.reshape(row_count), new_serving, scores.reshape(requests))
 
 

time: 116 us -> 109 us (0.940)
  waiting for transfers between devices: 35.9 us -> 30.2 us
    ppermute x2 -> x1, waiting for transfers between devices: 8.08 us -> 0.01 us  [body(): sent = lax.ppermute(held, 'shard', ahead)]
    ppermute x15, waiting for transfers between devices: 13.2 us -> 15.5 us  [body(): lax.ppermute(rows, 'shard', [(i, i ^ move) for i in range(shards)])]
    ppermute x2 -> x1, starting transfers between devices: 3.2 us -> 2.2 us  [body(): sent = lax.ppermute(held, 'shard', ahead)]
  transfers between devices with their start and end apart: 21 -> 20, of which waited for: 8 -> 7; matrix products, arithmetic and copies ran while one was open for 0% -> 0% of each run, Pallas kernels for 33% -> 33%
where the time goes in v4:
time: 109 us
  Pallas kernels  44.3 us (41%)
  starting transfers between devices  31.7 us (29%)
  waiting for transfers between devices  30.2 us (28%)
  local copies, waits for them, and re-layouts  1.3 us (1%)
  between operations  1.27 us (1%)
    ppermute x15, starting transfers between devices, body(): lax.ppermute(rows, 'shard', [(i, i ^ move) for i in range(shards)])  21.8 us
    pallas_call x1, Pallas kernels, body(): call(functools.partial(tower_kernel, moves, (feats, requests)), 'tower',...  17.1 us
    ppermute x15, waiting for transfers between devices, body(): lax.ppermute(rows, 'shard', [(i, i ^ move) for i in range(shards)])  15.5 us
    pallas_call x6, Pallas kernels, body(): call(functools.partial(gather_kernel, sends, pitch), 'gather', 4, out_sha...  14.3 us
    ppermute x1, waiting for transfers between devices, body(): lax.ppermute(aside, 'shard', straight + [(i, i + 3) for i in range(0, sha...  13.3 us
    pallas_call x1, Pallas kernels, body(): call(functools.partial(update_kernel, LANES, cap + 2, req_rows), 'update'...  6.71 us
    all_to_all x1, starting transfers between devices, body(): lax.all_to_all(packed, 'shard', split_axis=0, concat_axis=0, tiled=True)  6.62 us
    pallas_call x1, Pallas kernels, body(): call(functools.partial(pack_kernel, cap, req_rows), 'pack', 56, out_shape...  3.05 us
  transfers between devices with their start and end apart: 20, of which 7 were waited for; matrix products, arithmetic and copies ran while one was open for 0% of the time, Pallas kernels for 33%

profile of v4, /device:TPU:9, one launch (start us, length us, event | category | flops | bytes accessed | tf_op | source)
XLA Modules:
  0.0 108.8 jit_solution(7022251252312117210)
XLA Ops:
  0.7 3.1 %pack.1 = (bf16[16,144,128]{2,1,0:T(8,128)(2,1)}, bf16[2048,128]{1,0:T(8,128)(2,1)}) custom-call(bf16[16,128,128]{2,1,0:T(8,128)(2,1)} %rows_hbm.1, s32[16,128]{1,0:T(8,128)} %ids_hbm.1, s32[16,480]{1,0:T(8,128)} %req_hbm.1, bf16[4096,128]{1,0:T(8,128)(2,1)} %serving_hbm.3, s32[16]{0:T(128)} %counts_ref.1), custom_call_target="tpu_custom_call" | custom-call | tf_op jit(solution)/shard_map/pack/pallas_call | solution.py:330
  3.8 6.6 %all-to-all-start = ((bf16[16,144,128]{2,1,0:T(8,128)(2,1)}), bf16[16,144,128]{2,1,0:T(8,128)(2,1)S(1)}, u32[]{:S(2)}, u32[]{:S(2)}) async-start(bf16[16,144,128]{2,1,0:T(8,128)(2,1)} %get-tuple-element.26), calls=%async_computation | async-start | bytes 1179648 | tf_op jit(solution)/shard_map/all_to_all | solution.py:345
  10.8 13.3 %collective-permute-done.refs_0_.lower_ref = bf16[2048,128]{1,0:T(8,128)(2,1)S(1)} collective-permute-done((bf16[2048,128]{1,0:T(8,128)(2,1)}, bf16[2048,128]{1,0:T(8,128)(2,1)S(1)}, u32[]{:S(2)}, u32[]{:S(2)}) %collective-permute-start) | collective-permute-done | bytes 524320 | tf_op jit(solution)/shard_map/ppermute | solution.py:353
  24.2 0.8 stage.1
  25.1 0.7 collective-permute-start.2
  25.9 6.7 %update.1 = (bf16[4096,128]{1,0:T(8,128)(2,1)}, f32[32,128]{1,0:T(8,128)}, f32[4096,128]{1,0:T(8,128)S(1)}, s32[16,4,128]{2,1,0:T(4,128)S(1)}) custom-call(bf16[16,144,128]{2,1,0:T(8,128)(2,1)S(1)} %all-to-all-done.recv_ref.req_ref, bf16[16,144,128]{2,1,0:T(8,128)(2,1)S(1)} %all-to-all-done.recv_ref.req_ref, f32[32,128]{1,0:T(8,128)S(1)} %bitcast.12, ...), custom_call_target="tpu_custom_call" | custom-call | tf_op jit(solution)/shard_map/update/pallas_call | solution.py:377
  32.6 1.3 %collective-permute-done.1.upper_ref = bf16[2048,128]{1,0:T(8,128)(2,1)S(1)} collective-permute-done((bf16[2048,128]{1,0:T(8,128)(2,1)}, bf16[2048,128]{1,0:T(8,128)(2,1)S(1)}, u32[]{:S(2)}, u32[]{:S(2)}) %collective-permute-start.1) | collective-permute-done | bytes 524320 | tf_op jit(solution)/shard_map/ppermute | solution.py:362
  33.9 1.2 %apply.1 = (bf16[4096,128]{1,0:T(8,128)(2,1)}, f32[4096,128]{1,0:T(8,128)S(1)}) custom-call(s32[1]{0:T(128)} %bitcast.2.me_ref, f32[4096,128]{1,0:T(8,128)S(1)} %get-tuple-element.29.change_ref, bf16[2048,128]{1,0:T(8,128)(2,1)S(1)} %collective-permute-done.1.upper_ref, bf16[2048,128]{1,0:T(8,128)(2,1)S(1)} %collective-permute-done.refs_0_.lower_ref, ...), custom_call_target="tpu_custom_call" | custom-call | tf_op jit(solution)/shard_map/apply/pallas_call | solution.py:395
  35.1 2.5 %gather.7 = (bf16[480,128]{1,0:T(8,128)(2,1)S(1)}, bf16[480,128]{1,0:T(8,128)(2,1)S(1)}, bf16[480,128]{1,0:T(8,128)(2,1)S(1)}) custom-call(s32[1]{0:T(128)} %bitcast.2.me_ref, s32[8192]{0:T(1024)S(1)} %bitcast.6, f32[4096,128]{1,0:T(8,128)S(1)} %get-tuple-element.31.live_ref), custom_call_target="tpu_custom_call" | custom-call | bytes 5399999 | tf_op jit(solution)/shard_map/gather/pallas_call | solution.py:411
  37.7 1.8 %collective-permute-start.4 = (bf16[480,128]{1,0:T(8,128)(2,1)S(1)}, bf16[480,128]{1,0:T(8,128)(2,1)S(1)}, u32[]{:S(2)}, u32[]{:S(2)}) collective-permute-start(bf16[480,128]{1,0:T(8,128)(2,1)S(1)} %get-tuple-element.33), channel_id=1, source_target_pairs={{0,9},{1,8},{2,11},{3,10},{4,13},{5,12},{6,15},{7,14},{8,1},{9,0},... | collective-permute-start | bytes 368648 | tf_op jit(solution)/shard_map/ppermute | solution.py:423
  39.5 1.2 %collective-permute-start.5 = (bf16[480,128]{1,0:T(8,128)(2,1)S(1)}, bf16[480,128]{1,0:T(8,128)(2,1)S(1)}, u32[]{:S(2)}, u32[]{:S(2)}) collective-permute-start(bf16[480,128]{1,0:T(8,128)(2,1)S(1)} %get-tuple-element.34), channel_id=1, source_target_pairs={{0,1},{1,0},{2,3},{3,2},{4,5},{5,4},{6,7},{7,6},{8,9},{9,8},{10,11... | collective-permute-start | bytes 368648 | tf_op jit(solution)/shard_map/ppermute | solution.py:423
  40.7 1.6 %gather.6 = bf16[480,128]{1,0:T(8,128)(2,1)S(1)} custom-call(s32[1]{0:T(128)} %bitcast.2.me_ref, s32[8192]{0:T(1024)S(1)} %bitcast.7, f32[4096,128]{1,0:T(8,128)S(1)} %get-tuple-element.31.live_ref), custom_call_target="tpu_custom_call" | custom-call | bytes 1800000 | tf_op jit(solution)/shard_map/gather/pallas_call | solution.py:411
  42.3 2.5 %gather.8 = (bf16[480,128]{1,0:T(8,128)(2,1)S(1)}, bf16[480,128]{1,0:T(8,128)(2,1)S(1)}, bf16[480,128]{1,0:T(8,128)(2,1)S(1)}) custom-call(s32[1]{0:T(128)} %bitcast.2.me_ref, s32[8192]{0:T(1024)S(1)} %bitcast.8, f32[4096,128]{1,0:T(8,128)S(1)} %get-tuple-element.31.live_ref), custom_call_target="tpu_custom_call" | custom-call | bytes 5399999 | tf_op jit(solution)/shard_map/gather/pallas_call | solution.py:411
  44.9 3.0 %collective-permute-start.7 = (bf16[480,128]{1,0:T(8,128)(2,1)S(1)}, bf16[480,128]{1,0:T(8,128)(2,1)S(1)}, u32[]{:S(2)}, u32[]{:S(2)}) collective-permute-start(bf16[480,128]{1,0:T(8,128)(2,1)S(1)} %get-tuple-element.36), channel_id=1, source_target_pairs={{0,2},{1,3},{2,0},{3,1},{4,6},{5,7},{6,4},{7,5},{8,10},{9,11},{10,... | collective-permute-start | bytes 368648 | tf_op jit(solution)/shard_map/ppermute | solution.py:423
  48.0 2.3 %collective-permute-start.8 = (bf16[480,128]{1,0:T(8,128)(2,1)S(1)}, bf16[480,128]{1,0:T(8,128)(2,1)S(1)}, u32[]{:S(2)}, u32[]{:S(2)}) collective-permute-start(bf16[480,128]{1,0:T(8,128)(2,1)S(1)} %get-tuple-element.37), channel_id=1, source_target_pairs={{0,11},{1,10},{2,9},{3,8},{4,15},{5,14},{6,13},{7,12},{8,3},{9,2},... | collective-permute-start | bytes 368648 | tf_op jit(solution)/shard_map/ppermute | solution.py:423
  50.3 2.5 %gather.9 = (bf16[480,128]{1,0:T(8,128)(2,1)S(1)}, bf16[480,128]{1,0:T(8,128)(2,1)S(1)}, bf16[480,128]{1,0:T(8,128)(2,1)S(1)}) custom-call(s32[1]{0:T(128)} %bitcast.2.me_ref, s32[8192]{0:T(1024)S(1)} %bitcast.9, f32[4096,128]{1,0:T(8,128)S(1)} %get-tuple-element.31.live_ref), custom_call_target="tpu_custom_call" | custom-call | bytes 5399999 | tf_op jit(solution)/shard_map/gather/pallas_call | solution.py:411
  52.8 2.5 %gather.10 = (bf16[480,128]{1,0:T(8,128)(2,1)S(1)}, bf16[480,128]{1,0:T(8,128)(2,1)S(1)}, bf16[480,128]{1,0:T(8,128)(2,1)S(1)}) custom-call(s32[1]{0:T(128)} %bitcast.2.me_ref, s32[8192]{0:T(1024)S(1)} %bitcast.10, f32[4096,128]{1,0:T(8,128)S(1)} %get-tuple-element.31.live_ref), custom_call_target="tpu_custom_call" | custom-call | bytes 5399999 | tf_op jit(solution)/shard_map/gather/pallas_call | solution.py:411
  55.4 1.6 %collective-permute-start.6 = (bf16[480,128]{1,0:T(8,128)(2,1)S(1)}, bf16[480,128]{1,0:T(8,128)(2,1)S(1)}, u32[]{:S(2)}, u32[]{:S(2)}) collective-permute-start(bf16[480,128]{1,0:T(8,128)(2,1)S(1)} %get-tuple-element.35), channel_id=1, source_target_pairs={{0,10},{1,11},{2,8},{3,9},{4,14},{5,15},{6,12},{7,13},{8,2},{9,3},... | collective-permute-start | bytes 368648 | tf_op jit(solution)/shard_map/ppermute | solution.py:423
  57.1 3.3 %collective-permute-start.11 = (bf16[480,128]{1,0:T(8,128)(2,1)S(1)}, bf16[480,128]{1,0:T(8,128)(2,1)S(1)}, u32[]{:S(2)}, u32[]{:S(2)}) collective-permute-start(bf16[480,128]{1,0:T(8,128)(2,1)S(1)} %get-tuple-element.40), channel_id=1, source_target_pairs={{0,4},{1,5},{2,6},{3,7},{4,0},{5,1},{6,2},{7,3},{8,12},{9,13},{10,... | collective-permute-start | bytes 368648 | tf_op jit(solution)/shard_map/ppermute | solution.py:423
  60.4 0.8 collective-permute-start.9
  61.2 2.5 %gather.11 = (bf16[480,128]{1,0:T(8,128)(2,1)S(1)}, bf16[480,128]{1,0:T(8,128)(2,1)S(1)}, bf16[480,128]{1,0:T(8,128)(2,1)S(1)}) custom-call(s32[1]{0:T(128)} %bitcast.2.me_ref, s32[8192]{0:T(1024)S(1)} %bitcast.11, f32[4096,128]{1,0:T(8,128)S(1)} %get-tuple-element.31.live_ref), custom_call_target="tpu_custom_call" | custom-call | bytes 5399999 | tf_op jit(solution)/shard_map/gather/pallas_call | solution.py:411
  63.7 1.6 %collective-permute-done.6.refs_3_.refs_0_ = bf16[480,128]{1,0:T(8,128)(2,1)S(1)} collective-permute-done((bf16[480,128]{1,0:T(8,128)(2,1)S(1)}, bf16[480,128]{1,0:T(8,128)(2,1)S(1)}, u32[]{:S(2)}, u32[]{:S(2)}) %collective-permute-start.6) | collective-permute-done | bytes 122912 | tf_op jit(solution)/shard_map/ppermute | solution.py:423
  65.3 2.9 %collective-permute-done.10.refs_7_.refs_1_ = bf16[480,128]{1,0:T(8,128)(2,1)S(1)} collective-permute-done((bf16[480,128]{1,0:T(8,128)(2,1)S(1)}, bf16[480,128]{1,0:T(8,128)(2,1)S(1)}, u32[]{:S(2)}, u32[]{:S(2)}) %collective-permute-start.10) | collective-permute-done | bytes 122912 | tf_op jit(solution)/shard_map/ppermute | solution.py:423
  68.2 2.5 %collective-permute-start.12 = (bf16[480,128]{1,0:T(8,128)(2,1)S(1)}, bf16[480,128]{1,0:T(8,128)(2,1)S(1)}, u32[]{:S(2)}, u32[]{:S(2)}) collective-permute-start(bf16[480,128]{1,0:T(8,128)(2,1)S(1)} %get-tuple-element.41), channel_id=1, source_target_pairs={{0,13},{1,12},{2,15},{3,14},{4,9},{5,8},{6,11},{7,10},{8,5},{9,4},... | collective-permute-start | bytes 368648 | tf_op jit(solution)/shard_map/ppermute | solution.py:423
  70.8 5.1 %collective-permute-start.17 = (bf16[480,128]{1,0:T(8,128)(2,1)S(1)}, bf16[480,128]{1,0:T(8,128)(2,1)S(1)}, u32[]{:S(2)}, u32[]{:S(2)}) collective-permute-start(bf16[480,128]{1,0:T(8,128)(2,1)S(1)} %get-tuple-element.46), channel_id=1, source_target_pairs={{0,7},{1,6},{2,5},{3,4},{4,3},{5,2},{6,1},{7,0},{8,15},{9,14},{10,... | collective-permute-start | bytes 368648 | tf_op jit(solution)/shard_map/ppermute | solution.py:423
  75.9 5.8 %collective-permute-done.12.refs_9_.refs_0_ = bf16[480,128]{1,0:T(8,128)(2,1)S(1)} collective-permute-done((bf16[480,128]{1,0:T(8,128)(2,1)S(1)}, bf16[480,128]{1,0:T(8,128)(2,1)S(1)}, u32[]{:S(2)}, u32[]{:S(2)}) %collective-permute-start.12) | collective-permute-done | bytes 122912 | tf_op jit(solution)/shard_map/ppermute | solution.py:423
  81.6 5.2 %collective-permute-done.16.refs_13_ = bf16[480,128]{1,0:T(8,128)(2,1)S(1)} collective-permute-done((bf16[480,128]{1,0:T(8,128)(2,1)S(1)}, bf16[480,128]{1,0:T(8,128)(2,1)S(1)}, u32[]{:S(2)}, u32[]{:S(2)}) %collective-permute-start.16) | collective-permute-done | bytes 122912 | tf_op jit(solution)/shard_map/ppermute | solution.py:423
  87.0 0.5 copy-done.15
  87.6 2.2 %collective-permute-start.18 = (bf16[4096,128]{1,0:T(8,128)(2,1)S(1)}, bf16[4096,128]{1,0:T(8,128)(2,1)S(1)}, u32[]{:S(2)}, u32[]{:S(2)}) collective-permute-start(bf16[4096,128]{1,0:T(8,128)(2,1)S(1)} %hold.1), channel_id=1, source_target_pairs={{0,1},{1,2},{2,3},{3,4},{4,5},{5,6},{6,7},{7,8},{8,9},{9,10},{10,1... | collective-permute-start | bytes 3145736 | tf_op jit(solution)/shard_map/ppermute | solution.py:450
  89.9 0.6 copy-done.21
  90.5 17.1 %tower.1 = f32[8,128]{1,0:T(8,128)} custom-call(f32[8,128]{1,0:T(8,128)} %copy-done.21, s32[1]{0:T(128)} %bitcast.2.me_ref, s32[5120]{0:T(1024)} %copy-done.18, bf16[3,640,640]{2,1,0:T(8,128)(2,1)} %cross_hbm.1, bf16[3,640]{1,0:T(4,128)(2,1)} %cross_bias_ref.1, bf16[640,4096]{1,0:T(8,128)(2,1)} %tower_hbm.1, bf16[1,4096]{1,0:T(2,128)(2,1)} %copy-done.19, ...), custom_call_target="tpu_custom_call" | custom-call | tf_op jit(solution)/shard_map/tower/pallas_call | solution.py:451
  107.6 1.0 deliver.1
  (81 shorter events, 1.0 us)
Async XLA Ops:
  0.6 23.5 %copy-start = (bf16[4096,128]{1,0:T(8,128)(2,1)S(1)}, bf16[4096,128]{1,0:T(8,128)(2,1)}, u32[]{:S(2)}) copy-start(bf16[4096,128]{1,0:T(8,128)(2,1)} %serving_hbm.3) | copy-start | bytes 3145732
  0.7 25.2 %copy-start.22 = (f32[4096]{0:T(1024)S(1)}, f32[4096]{0:T(1024)}, u32[]{:S(2)}) copy-start(f32[4096]{0:T(1024)} %param.14) | copy-start | bytes 49156
  0.7 25.2 %copy-start.13 = (bf16[4096,128]{1,0:T(8,128)(2,1)S(1)}, bf16[4096,128]{1,0:T(8,128)(2,1)}, u32[]{:S(2)}) copy-start(bf16[4096,128]{1,0:T(8,128)(2,1)} %item_hbm.1) | copy-start | bytes 3145732
  3.8 22.2 %all-to-all-start = ((bf16[16,144,128]{2,1,0:T(8,128)(2,1)}), bf16[16,144,128]{2,1,0:T(8,128)(2,1)S(1)}, u32[]{:S(2)}, u32[]{:S(2)}) async-start(bf16[16,144,128]{2,1,0:T(8,128)(2,1)} %get-tuple-element.26), calls=%async_computation | async-start | bytes 1179648 | tf_op jit(solution)/shard_map/all_to_all | solution.py:345
  10.4 13.8 %collective-permute-start = (bf16[2048,128]{1,0:T(8,128)(2,1)}, bf16[2048,128]{1,0:T(8,128)(2,1)S(1)}, u32[]{:S(2)}, u32[]{:S(2)}) collective-permute-start(bf16[2048,128]{1,0:T(8,128)(2,1)} %get-tuple-element.30), channel_id=1, source_target_pairs={{1,0},{2,1},{3,2},{5,4},{6,5},{7,6},{9,8},{10,9},{11,10},{13,12},{... | collective-permute-start | bytes 1572872 | tf_op jit(solution)/shard_map/ppermute | solution.py:353
  10.8 24.3 %copy-start.18 = (s32[5120]{0:T(1024)}, s32[5120]{0:T(1024)S(1)}, u32[]{:S(2)}) copy-start(s32[5120]{0:T(1024)S(1)} %reshape.35.refs_1_.slots_ref) | copy-start | bytes 61444
  10.8 24.3 %copy-start.19 = (bf16[1,4096]{1,0:T(2,128)(2,1)}, bf16[1,4096]{1,0:T(2,128)(2,1)S(1)}, u32[]{:S(2)}) copy-start(bf16[1,4096]{1,0:T(2,128)(2,1)S(1)} %reshape.36.refs_2_.tower_bias_ref) | copy-start | bytes 24580
  10.8 24.3 %copy-start.20 = (bf16[1,4096]{1,0:T(2,128)(2,1)}, bf16[1,4096]{1,0:T(2,128)(2,1)S(1)}, u32[]{:S(2)}) copy-start(bf16[1,4096]{1,0:T(2,128)(2,1)S(1)} %reshape.37.refs_3_.score_ref) | copy-start | bytes 24580
  25.0 8.9 %collective-permute-start.1 = (bf16[2048,128]{1,0:T(8,128)(2,1)}, bf16[2048,128]{1,0:T(8,128)(2,1)S(1)}, u32[]{:S(2)}, u32[]{:S(2)}) collective-permute-start(bf16[2048,128]{1,0:T(8,128)(2,1)} %stage.1), channel_id=1, source_target_pairs={{0,15},{1,0},{2,1},{3,2},{4,3},{5,4},{6,5},{7,6},{8,7},{9,8},{10,9... | collective-permute-start | bytes 1572872 | tf_op jit(solution)/shard_map/ppermute | solution.py:362
  25.1 8.8 %collective-permute-start.2 = (bf16[2048,128]{1,0:T(8,128)(2,1)S(1)}, bf16[2048,128]{1,0:T(8,128)(2,1)S(1)}, u32[]{:S(2)}, u32[]{:S(2)}) collective-permute-start(bf16[2048,128]{1,0:T(8,128)(2,1)S(1)} %collective-permute-done.refs_0_.lower_ref), channel_id=1, source_target_pairs={{3,15},{7,3},{11,7},{15,11},{19,31},{23,19},{27,23},{31,27}} | collective-permute-start | bytes 1572872 | tf_op jit(solution)/shard_map/ppermute | solution.py:363
  37.7 17.7 %collective-permute-start.4 = (bf16[480,128]{1,0:T(8,128)(2,1)S(1)}, bf16[480,128]{1,0:T(8,128)(2,1)S(1)}, u32[]{:S(2)}, u32[]{:S(2)}) collective-permute-start(bf16[480,128]{1,0:T(8,128)(2,1)S(1)} %get-tuple-element.33), channel_id=1, source_target_pairs={{0,9},{1,8},{2,11},{3,10},{4,13},{5,12},{6,15},{7,14},{8,1},{9,0},... | collective-permute-start | bytes 368648 | tf_op jit(solution)/shard_map/ppermute | solution.py:423
  39.5 17.5 %collective-permute-start.5 = (bf16[480,128]{1,0:T(8,128)(2,1)S(1)}, bf16[480,128]{1,0:T(8,128)(2,1)S(1)}, u32[]{:S(2)}, u32[]{:S(2)}) collective-permute-start(bf16[480,128]{1,0:T(8,128)(2,1)S(1)} %get-tuple-element.34), channel_id=1, source_target_pairs={{0,1},{1,0},{2,3},{3,2},{4,5},{5,4},{6,7},{7,6},{8,9},{9,8},{10,11... | collective-permute-start | bytes 368648 | tf_op jit(solution)/shard_map/ppermute | solution.py:423
  42.3 14.8 %collective-permute-start.3 = (bf16[480,128]{1,0:T(8,128)(2,1)S(1)}, bf16[480,128]{1,0:T(8,128)(2,1)S(1)}, u32[]{:S(2)}, u32[]{:S(2)}) collective-permute-start(bf16[480,128]{1,0:T(8,128)(2,1)S(1)} %gather.6), channel_id=1, source_target_pairs={{0,8},{1,9},{2,10},{3,11},{4,12},{5,13},{6,14},{7,15},{8,0},{9,1},... | collective-permute-start | bytes 368648 | tf_op jit(solution)/shard_map/ppermute | solution.py:423
  44.9 15.5 %collective-permute-start.7 = (bf16[480,128]{1,0:T(8,128)(2,1)S(1)}, bf16[480,128]{1,0:T(8,128)(2,1)S(1)}, u32[]{:S(2)}, u32[]{:S(2)}) collective-permute-start(bf16[480,128]{1,0:T(8,128)(2,1)S(1)} %get-tuple-element.36), channel_id=1, source_target_pairs={{0,2},{1,3},{2,0},{3,1},{4,6},{5,7},{6,4},{7,5},{8,10},{9,11},{10,... | collective-permute-start | bytes 368648 | tf_op jit(solution)/shard_map/ppermute | solution.py:423
  48.0 13.2 %collective-permute-start.8 = (bf16[480,128]{1,0:T(8,128)(2,1)S(1)}, bf16[480,128]{1,0:T(8,128)(2,1)S(1)}, u32[]{:S(2)}, u32[]{:S(2)}) collective-permute-start(bf16[480,128]{1,0:T(8,128)(2,1)S(1)} %get-tuple-element.37), channel_id=1, source_target_pairs={{0,11},{1,10},{2,9},{3,8},{4,15},{5,14},{6,13},{7,12},{8,3},{9,2},... | collective-permute-start | bytes 368648 | tf_op jit(solution)/shard_map/ppermute | solution.py:423
  55.4 34.4 %copy-start.1 = (bf16[480,128]{1,0:T(8,128)(2,1)}, bf16[480,128]{1,0:T(8,128)(2,1)S(1)}, u32[]{:S(2)}) copy-start(bf16[480,128]{1,0:T(8,128)(2,1)S(1)} %collective-permute-done.4.refs_1_) | copy-start | bytes 368644
  55.4 10.0 %collective-permute-start.6 = (bf16[480,128]{1,0:T(8,128)(2,1)S(1)}, bf16[480,128]{1,0:T(8,128)(2,1)S(1)}, u32[]{:S(2)}, u32[]{:S(2)}) collective-permute-start(bf16[480,128]{1,0:T(8,128)(2,1)S(1)} %get-tuple-element.35), channel_id=1, source_target_pairs={{0,10},{1,11},{2,8},{3,9},{4,14},{5,15},{6,12},{7,13},{8,2},{9,3},... | collective-permute-start | bytes 368648 | tf_op jit(solution)/shard_map/ppermute | solution.py:423
  57.0 32.7 %copy-start.2 = (bf16[480,128]{1,0:T(8,128)(2,1)}, bf16[480,128]{1,0:T(8,128)(2,1)S(1)}, u32[]{:S(2)}) copy-start(bf16[480,128]{1,0:T(8,128)(2,1)S(1)} %collective-permute-done.5.refs_2_) | copy-start | bytes 368644
  57.0 11.2 %collective-permute-start.10 = (bf16[480,128]{1,0:T(8,128)(2,1)S(1)}, bf16[480,128]{1,0:T(8,128)(2,1)S(1)}, u32[]{:S(2)}, u32[]{:S(2)}) collective-permute-start(bf16[480,128]{1,0:T(8,128)(2,1)S(1)} %get-tuple-element.39), channel_id=1, source_target_pairs={{0,12},{1,13},{2,14},{3,15},{4,8},{5,9},{6,10},{7,11},{8,4},{9,5},... | collective-permute-start | bytes 368648 | tf_op jit(solution)/shard_map/ppermute | solution.py:423
  57.1 32.7 %copy-start.3 = (bf16[480,128]{1,0:T(8,128)(2,1)}, bf16[480,128]{1,0:T(8,128)(2,1)S(1)}, u32[]{:S(2)}) copy-start(bf16[480,128]{1,0:T(8,128)(2,1)S(1)} %collective-permute-done.3.refs_0_) | copy-start | bytes 368644
  57.1 13.7 %collective-permute-start.11 = (bf16[480,128]{1,0:T(8,128)(2,1)S(1)}, bf16[480,128]{1,0:T(8,128)(2,1)S(1)}, u32[]{:S(2)}, u32[]{:S(2)}) collective-permute-start(bf16[480,128]{1,0:T(8,128)(2,1)S(1)} %get-tuple-element.40), channel_id=1, source_target_pairs={{0,4},{1,5},{2,6},{3,7},{4,0},{5,1},{6,2},{7,3},{8,12},{9,13},{10,... | collective-permute-start | bytes 368648 | tf_op jit(solution)/shard_map/ppermute | solution.py:423
  60.4 29.4 %copy-start.4 = (bf16[480,128]{1,0:T(8,128)(2,1)}, bf16[480,128]{1,0:T(8,128)(2,1)S(1)}, u32[]{:S(2)}) copy-start(bf16[480,128]{1,0:T(8,128)(2,1)S(1)} %collective-permute-done.7.refs_4_.refs_1_) | copy-start | bytes 368644
  60.4 10.3 %collective-permute-start.9 = (bf16[480,128]{1,0:T(8,128)(2,1)S(1)}, bf16[480,128]{1,0:T(8,128)(2,1)S(1)}, u32[]{:S(2)}, u32[]{:S(2)}) collective-permute-start(bf16[480,128]{1,0:T(8,128)(2,1)S(1)} %get-tuple-element.38), channel_id=1, source_target_pairs={{0,3},{1,2},{2,1},{3,0},{4,7},{5,6},{6,5},{7,4},{8,11},{9,10},{10,... | collective-permute-start | bytes 368648 | tf_op jit(solution)/shard_map/ppermute | solution.py:423
  61.2 28.6 %copy-start.5 = (bf16[480,128]{1,0:T(8,128)(2,1)}, bf16[480,128]{1,0:T(8,128)(2,1)S(1)}, u32[]{:S(2)}) copy-start(bf16[480,128]{1,0:T(8,128)(2,1)S(1)} %collective-permute-done.8.refs_5_.refs_2_) | copy-start | bytes 368644
  61.2 14.7 %collective-permute-start.13 = (bf16[480,128]{1,0:T(8,128)(2,1)S(1)}, bf16[480,128]{1,0:T(8,128)(2,1)S(1)}, u32[]{:S(2)}, u32[]{:S(2)}) collective-permute-start(bf16[480,128]{1,0:T(8,128)(2,1)S(1)} %get-tuple-element.42), channel_id=1, source_target_pairs={{0,5},{1,4},{2,7},{3,6},{4,1},{5,0},{6,3},{7,2},{8,13},{9,12},{10,... | collective-permute-start | bytes 368648 | tf_op jit(solution)/shard_map/ppermute | solution.py:423
  65.3 24.5 %copy-start.6 = (bf16[480,128]{1,0:T(8,128)(2,1)}, bf16[480,128]{1,0:T(8,128)(2,1)S(1)}, u32[]{:S(2)}) copy-start(bf16[480,128]{1,0:T(8,128)(2,1)S(1)} %collective-permute-done.6.refs_3_.refs_0_) | copy-start | bytes 368644
  65.3 10.5 %collective-permute-start.14 = (bf16[480,128]{1,0:T(8,128)(2,1)S(1)}, bf16[480,128]{1,0:T(8,128)(2,1)S(1)}, u32[]{:S(2)}, u32[]{:S(2)}) collective-permute-start(bf16[480,128]{1,0:T(8,128)(2,1)S(1)} %get-tuple-element.43), channel_id=1, source_target_pairs={{0,14},{1,15},{2,12},{3,13},{4,10},{5,11},{6,8},{7,9},{8,6},{9,7},... | collective-permute-start | bytes 368648 | tf_op jit(solution)/shard_map/ppermute | solution.py:423
  68.2 13.4 %collective-permute-start.12 = (bf16[480,128]{1,0:T(8,128)(2,1)S(1)}, bf16[480,128]{1,0:T(8,128)(2,1)S(1)}, u32[]{:S(2)}, u32[]{:S(2)}) collective-permute-start(bf16[480,128]{1,0:T(8,128)(2,1)S(1)} %get-tuple-element.41), channel_id=1, source_target_pairs={{0,13},{1,12},{2,15},{3,14},{4,9},{5,8},{6,11},{7,10},{8,5},{9,4},... | collective-permute-start | bytes 368648 | tf_op jit(solution)/shard_map/ppermute | solution.py:423
  70.7 16.1 %collective-permute-start.16 = (bf16[480,128]{1,0:T(8,128)(2,1)S(1)}, bf16[480,128]{1,0:T(8,128)(2,1)S(1)}, u32[]{:S(2)}, u32[]{:S(2)}) collective-permute-start(bf16[480,128]{1,0:T(8,128)(2,1)S(1)} %get-tuple-element.45), channel_id=1, source_target_pairs={{0,15},{1,14},{2,13},{3,12},{4,11},{5,10},{6,9},{7,8},{8,7},{9,6},... | collective-permute-start | bytes 368648 | tf_op jit(solution)/shard_map/ppermute | solution.py:423
  70.8 16.1 %collective-permute-start.17 = (bf16[480,128]{1,0:T(8,128)(2,1)S(1)}, bf16[480,128]{1,0:T(8,128)(2,1)S(1)}, u32[]{:S(2)}, u32[]{:S(2)}) collective-permute-start(bf16[480,128]{1,0:T(8,128)(2,1)S(1)} %get-tuple-element.46), channel_id=1, source_target_pairs={{0,7},{1,6},{2,5},{3,4},{4,3},{5,2},{6,1},{7,0},{8,15},{9,14},{10,... | collective-permute-start | bytes 368648 | tf_op jit(solution)/shard_map/ppermute | solution.py:423
  75.8 11.0 %collective-permute-start.15 = (bf16[480,128]{1,0:T(8,128)(2,1)S(1)}, bf16[480,128]{1,0:T(8,128)(2,1)S(1)}, u32[]{:S(2)}, u32[]{:S(2)}) collective-permute-start(bf16[480,128]{1,0:T(8,128)(2,1)S(1)} %get-tuple-element.44), channel_id=1, source_target_pairs={{0,6},{1,7},{2,4},{3,5},{4,2},{5,3},{6,0},{7,1},{8,14},{9,15},{10,... | collective-permute-start | bytes 368648 | tf_op jit(solution)/shard_map/ppermute | solution.py:423
  87.6 20.0 %collective-permute-start.18 = (bf16[4096,128]{1,0:T(8,128)(2,1)S(1)}, bf16[4096,128]{1,0:T(8,128)(2,1)S(1)}, u32[]{:S(2)}, u32[]{:S(2)}) collective-permute-start(bf16[4096,128]{1,0:T(8,128)(2,1)S(1)} %hold.1), channel_id=1, source_target_pairs={{0,1},{1,2},{2,3},{3,4},{4,5},{5,6},{6,7},{7,8},{8,9},{9,10},{10,1... | collective-permute-start | bytes 3145736 | tf_op jit(solution)/shard_map/ppermute | solution.py:450
  (14 other events, 152.4 us)

commit v5 on v4

--- a/solution.py
+++ b/solution.py
@@ -19,7 +19,7 @@
     return -(-value // unit) * unit
 
 
-SENDS = ((8,), (9, 1, 10), (2, 11, 3), (12, 4, 13), (5, 14, 6), (15, 7, 0))
+SENDS = ((8,), (9, 1), (10, 2, 11), (3, 12, 4), (13, 5, 14), (6, 15, 7, 0))
 TAKES = ((8, 9, 1), (10, 2, 11), (3, 12, 4), (13, 5, 14))
 
 
@@ -169,14 +169,13 @@
     load.wait()
 
 
-def apply_kernel(me_ref, change_ref, upper_ref, lower_ref, around_ref, serving_out, live_out):
+def apply_kernel(me_ref, change_ref, upper_ref, lower_ref, around_ref, live_out):
     f32 = jnp.float32
     half = upper_ref.shape[0]
     turned = lax.rem(me_ref[0], 4) == 3
     lower = jnp.where(turned, around_ref[...].astype(f32), lower_ref[...].astype(f32))
     for start, old in ((0, upper_ref[...].astype(f32)), (half, lower)):
         serving = (old + change_ref[start : start + half, :]).astype(jnp.bfloat16)
-        serving_out[start : start + half, :] = serving
         live_out[start : start + half, :] = serving.astype(f32)
 
 
@@ -392,19 +391,15 @@
             pltpu.SemaphoreType.DMA((2,)),
         ],
     )(joined, recv, row_accum.reshape(-1, LANES), item_table)
-    serving_next, live = call(
+    live = call(
         apply_kernel, "apply", 8,
-        out_shape=(
-            jax.ShapeDtypeStruct((row_count, emb), bf16),
-            jax.ShapeDtypeStruct((row_count, emb), f32),
-        ),
+        out_shape=jax.ShapeDtypeStruct((row_count, emb), f32),
         in_specs=[smem] + [vmem] * 4,
-        out_specs=(vmem, vmem),
+        out_specs=vmem,
     )(me, change, *serving_parts)
     req = req.reshape(-1)
 
     pitch = req_rows * LANES
-    serving_next = live
     if shards == 16:
         moves, pieces = [], []
         for sends in SENDS:

time: 109 us -> 107 us (0.982)
  starting transfers between devices: 31.7 us -> 27.9 us
  waiting for transfers between devices: 30.2 us -> 33.2 us
    ppermute x15, starting transfers between devices: 21.8 us -> 18.2 us  [body(): lax.ppermute(rows, 'shard', [(i, i ^ move) for i in range(shards)])]
    ppermute x15, waiting for transfers between devices: 15.5 us -> 18.5 us  [body(): lax.ppermute(rows, 'shard', [(i, i ^ move) for i in range(shards)])]
  transfers between devices with their start and end apart: 20 -> 20, of which waited for: 7 -> 8; matrix products, arithmetic and copies ran while one was open for 0% -> 0% of each run, Pallas kernels for 33% -> 34%
where the time goes in v5:
time: 107 us
  Pallas kernels  43.4 us (41%)
  waiting for transfers between devices  33.2 us (31%)
  starting transfers between devices  27.9 us (26%)
  local copies, waits for them, and re-layouts  1.27 us (1%)
  between operations  1.27 us (1%)
    ppermute x15, waiting for transfers between devices, body(): lax.ppermute(rows, 'shard', [(i, i ^ move) for i in range(shards)])  18.5 us
    ppermute x15, starting transfers between devices, body(): lax.ppermute(rows, 'shard', [(i, i ^ move) for i in range(shards)])  18.2 us
    pallas_call x1, Pallas kernels, body(): call(functools.partial(tower_kernel, moves, (feats, requests)), 'tower',...  17.1 us
    pallas_call x6, Pallas kernels, body(): call(functools.partial(gather_kernel, sends, pitch), 'gather', 4, out_sha...  14.3 us
    ppermute x1, waiting for transfers between devices, body(): lax.ppermute(aside, 'shard', straight + [(i, i + 3) for i in range(0, sha...  13.3 us
    pallas_call x1, Pallas kernels, body(): call(functools.partial(update_kernel, LANES, cap + 2, req_rows), 'update'...  6.71 us
    all_to_all x1, starting transfers between devices, body(): lax.all_to_all(packed, 'shard', split_axis=0, concat_axis=0, tiled=True)  6.62 us
    pallas_call x1, Pallas kernels, body(): call(functools.partial(pack_kernel, cap, req_rows), 'pack', 56, out_shape...  3.05 us
  transfers between devices with their start and end apart: 20, of which 8 were waited for; matrix products, arithmetic and copies ran while one was open for 0% of the time, Pallas kernels for 34%

profile of v5, /device:TPU:9, one launch (start us, length us, event | category | flops | bytes accessed | tf_op | source)
XLA Modules:
  0.0 107.1 jit_solution(12589783779573212526)
XLA Ops:
  0.7 3.1 %pack.1 = (bf16[16,144,128]{2,1,0:T(8,128)(2,1)}, bf16[2048,128]{1,0:T(8,128)(2,1)}) custom-call(bf16[16,128,128]{2,1,0:T(8,128)(2,1)} %rows_hbm.1, s32[16,128]{1,0:T(8,128)} %ids_hbm.1, s32[16,480]{1,0:T(8,128)} %req_hbm.1, bf16[4096,128]{1,0:T(8,128)(2,1)} %serving_hbm.3, s32[16]{0:T(128)} %counts_ref.1), custom_call_target="tpu_custom_call" | custom-call | tf_op jit(solution)/shard_map/pack/pallas_call | solution.py:329
  3.8 6.6 %all-to-all-start = ((bf16[16,144,128]{2,1,0:T(8,128)(2,1)}), bf16[16,144,128]{2,1,0:T(8,128)(2,1)S(1)}, u32[]{:S(2)}, u32[]{:S(2)}) async-start(bf16[16,144,128]{2,1,0:T(8,128)(2,1)} %get-tuple-element.25), calls=%async_computation | async-start | bytes 1179648 | tf_op jit(solution)/shard_map/all_to_all | solution.py:344
  10.4 0.4 collective-permute-start
  10.8 13.3 %collective-permute-done.refs_0_.lower_ref = bf16[2048,128]{1,0:T(8,128)(2,1)S(1)} collective-permute-done((bf16[2048,128]{1,0:T(8,128)(2,1)}, bf16[2048,128]{1,0:T(8,128)(2,1)S(1)}, u32[]{:S(2)}, u32[]{:S(2)}) %collective-permute-start) | collective-permute-done | bytes 524320 | tf_op jit(solution)/shard_map/ppermute | solution.py:352
  24.2 0.8 stage.1
  25.1 0.7 collective-permute-start.2
  25.9 6.7 %update.1 = (bf16[4096,128]{1,0:T(8,128)(2,1)}, f32[32,128]{1,0:T(8,128)}, f32[4096,128]{1,0:T(8,128)S(1)}, s32[16,4,128]{2,1,0:T(4,128)S(1)}) custom-call(bf16[16,144,128]{2,1,0:T(8,128)(2,1)S(1)} %all-to-all-done.recv_ref.req_ref, bf16[16,144,128]{2,1,0:T(8,128)(2,1)S(1)} %all-to-all-done.recv_ref.req_ref, f32[32,128]{1,0:T(8,128)S(1)} %bitcast.12, ...), custom_call_target="tpu_custom_call" | custom-call | tf_op jit(solution)/shard_map/update/pallas_call | solution.py:376
  32.6 1.2 %collective-permute-done.1.upper_ref = bf16[2048,128]{1,0:T(8,128)(2,1)S(1)} collective-permute-done((bf16[2048,128]{1,0:T(8,128)(2,1)}, bf16[2048,128]{1,0:T(8,128)(2,1)S(1)}, u32[]{:S(2)}, u32[]{:S(2)}) %collective-permute-start.1) | collective-permute-done | bytes 524320 | tf_op jit(solution)/shard_map/ppermute | solution.py:361
  34.2 2.1 %gather.7 = (bf16[480,128]{1,0:T(8,128)(2,1)S(1)}, bf16[480,128]{1,0:T(8,128)(2,1)S(1)}) custom-call(s32[1]{0:T(128)} %bitcast.2.me_ref, s32[8192]{0:T(1024)S(1)} %bitcast.6, f32[4096,128]{1,0:T(8,128)S(1)} %apply.1.live_ref), custom_call_target="tpu_custom_call" | custom-call | bytes 3600000 | tf_op jit(solution)/shard_map/gather/pallas_call | solution.py:406
  36.3 1.9 %collective-permute-start.4 = (bf16[480,128]{1,0:T(8,128)(2,1)S(1)}, bf16[480,128]{1,0:T(8,128)(2,1)S(1)}, u32[]{:S(2)}, u32[]{:S(2)}) collective-permute-start(bf16[480,128]{1,0:T(8,128)(2,1)S(1)} %get-tuple-element.31), channel_id=1, source_target_pairs={{0,9},{1,8},{2,11},{3,10},{4,13},{5,12},{6,15},{7,14},{8,1},{9,0},... | collective-permute-start | bytes 368648 | tf_op jit(solution)/shard_map/ppermute | solution.py:418
  38.1 1.2 %collective-permute-start.5 = (bf16[480,128]{1,0:T(8,128)(2,1)S(1)}, bf16[480,128]{1,0:T(8,128)(2,1)S(1)}, u32[]{:S(2)}, u32[]{:S(2)}) collective-permute-start(bf16[480,128]{1,0:T(8,128)(2,1)S(1)} %get-tuple-element.32), channel_id=1, source_target_pairs={{0,1},{1,0},{2,3},{3,2},{4,5},{5,4},{6,7},{7,6},{8,9},{9,8},{10,11... | collective-permute-start | bytes 368648 | tf_op jit(solution)/shard_map/ppermute | solution.py:418
  39.3 1.6 %gather.6 = bf16[480,128]{1,0:T(8,128)(2,1)S(1)} custom-call(s32[1]{0:T(128)} %bitcast.2.me_ref, s32[8192]{0:T(1024)S(1)} %bitcast.7, f32[4096,128]{1,0:T(8,128)S(1)} %apply.1.live_ref), custom_call_target="tpu_custom_call" | custom-call | bytes 1800000 | tf_op jit(solution)/shard_map/gather/pallas_call | solution.py:406
  41.0 2.5 %gather.8 = (bf16[480,128]{1,0:T(8,128)(2,1)S(1)}, bf16[480,128]{1,0:T(8,128)(2,1)S(1)}, bf16[480,128]{1,0:T(8,128)(2,1)S(1)}) custom-call(s32[1]{0:T(128)} %bitcast.2.me_ref, s32[8192]{0:T(1024)S(1)} %bitcast.8, f32[4096,128]{1,0:T(8,128)S(1)} %apply.1.live_ref), custom_call_target="tpu_custom_call" | custom-call | bytes 5399999 | tf_op jit(solution)/shard_map/gather/pallas_call | solution.py:406
  43.5 5.1 %collective-permute-start.6 = (bf16[480,128]{1,0:T(8,128)(2,1)S(1)}, bf16[480,128]{1,0:T(8,128)(2,1)S(1)}, u32[]{:S(2)}, u32[]{:S(2)}) collective-permute-start(bf16[480,128]{1,0:T(8,128)(2,1)S(1)} %get-tuple-element.33), channel_id=1, source_target_pairs={{0,10},{1,11},{2,8},{3,9},{4,14},{5,15},{6,12},{7,13},{8,2},{9,3},... | collective-permute-start | bytes 368648 | tf_op jit(solution)/shard_map/ppermute | solution.py:418
  48.6 2.5 %gather.9 = (bf16[480,128]{1,0:T(8,128)(2,1)S(1)}, bf16[480,128]{1,0:T(8,128)(2,1)S(1)}, bf16[480,128]{1,0:T(8,128)(2,1)S(1)}) custom-call(s32[1]{0:T(128)} %bitcast.2.me_ref, s32[8192]{0:T(1024)S(1)} %bitcast.9, f32[4096,128]{1,0:T(8,128)S(1)} %apply.1.live_ref), custom_call_target="tpu_custom_call" | custom-call | bytes 5399999 | tf_op jit(solution)/shard_map/gather/pallas_call | solution.py:406
  51.2 2.5 %gather.10 = (bf16[480,128]{1,0:T(8,128)(2,1)S(1)}, bf16[480,128]{1,0:T(8,128)(2,1)S(1)}, bf16[480,128]{1,0:T(8,128)(2,1)S(1)}) custom-call(s32[1]{0:T(128)} %bitcast.2.me_ref, s32[8192]{0:T(1024)S(1)} %bitcast.10, f32[4096,128]{1,0:T(8,128)S(1)} %apply.1.live_ref), custom_call_target="tpu_custom_call" | custom-call | bytes 5399999 | tf_op jit(solution)/shard_map/gather/pallas_call | solution.py:406
  53.8 2.2 %collective-permute-start.8 = (bf16[480,128]{1,0:T(8,128)(2,1)S(1)}, bf16[480,128]{1,0:T(8,128)(2,1)S(1)}, u32[]{:S(2)}, u32[]{:S(2)}) collective-permute-start(bf16[480,128]{1,0:T(8,128)(2,1)S(1)} %get-tuple-element.35), channel_id=1, source_target_pairs={{0,11},{1,10},{2,9},{3,8},{4,15},{5,14},{6,13},{7,12},{8,3},{9,2},... | collective-permute-start | bytes 368648 | tf_op jit(solution)/shard_map/ppermute | solution.py:418
  56.0 3.3 %collective-permute-start.11 = (bf16[480,128]{1,0:T(8,128)(2,1)S(1)}, bf16[480,128]{1,0:T(8,128)(2,1)S(1)}, u32[]{:S(2)}, u32[]{:S(2)}) collective-permute-start(bf16[480,128]{1,0:T(8,128)(2,1)S(1)} %get-tuple-element.38), channel_id=1, source_target_pairs={{0,4},{1,5},{2,6},{3,7},{4,0},{5,1},{6,2},{7,3},{8,12},{9,13},{10,... | collective-permute-start | bytes 368648 | tf_op jit(solution)/shard_map/ppermute | solution.py:418
  59.4 3.0 %gather.11 = (bf16[480,128]{1,0:T(8,128)(2,1)S(1)}, bf16[480,128]{1,0:T(8,128)(2,1)S(1)}, bf16[480,128]{1,0:T(8,128)(2,1)S(1)}, bf16[480,128]{1,0:T(8,128)(2,1)S(1)}) custom-call(s32[1]{0:T(128)} %bitcast.2.me_ref, s32[8192]{0:T(1024)S(1)} %bitcast.11, f32[4096,128]{1,0:T(8,128)S(1)} %apply.1.live_ref), custom_call_target="tpu_custom_call" | custom-call | bytes 7200000 | tf_op jit(solution)/shard_map/gather/pallas_call | solution.py:406
  62.5 1.9 %collective-permute-done.8.refs_5_.refs_2_ = bf16[480,128]{1,0:T(8,128)(2,1)S(1)} collective-permute-done((bf16[480,128]{1,0:T(8,128)(2,1)S(1)}, bf16[480,128]{1,0:T(8,128)(2,1)S(1)}, u32[]{:S(2)}, u32[]{:S(2)}) %collective-permute-start.8) | collective-permute-done | bytes 122912 | tf_op jit(solution)/shard_map/ppermute | solution.py:418
  64.4 5.7 %collective-permute-done.10.refs_7_.refs_1_ = bf16[480,128]{1,0:T(8,128)(2,1)S(1)} collective-permute-done((bf16[480,128]{1,0:T(8,128)(2,1)S(1)}, bf16[480,128]{1,0:T(8,128)(2,1)S(1)}, u32[]{:S(2)}, u32[]{:S(2)}) %collective-permute-start.10) | collective-permute-done | bytes 122912 | tf_op jit(solution)/shard_map/ppermute | solution.py:418
  70.1 1.3 %collective-permute-start.14 = (bf16[480,128]{1,0:T(8,128)(2,1)S(1)}, bf16[480,128]{1,0:T(8,128)(2,1)S(1)}, u32[]{:S(2)}, u32[]{:S(2)}) collective-permute-start(bf16[480,128]{1,0:T(8,128)(2,1)S(1)} %get-tuple-element.41), channel_id=1, source_target_pairs={{0,14},{1,15},{2,12},{3,13},{4,10},{5,11},{6,8},{7,9},{8,6},{9,7},... | collective-permute-start | bytes 368648 | tf_op jit(solution)/shard_map/ppermute | solution.py:418
  71.4 1.9 %collective-permute-start.16 = (bf16[480,128]{1,0:T(8,128)(2,1)S(1)}, bf16[480,128]{1,0:T(8,128)(2,1)S(1)}, u32[]{:S(2)}, u32[]{:S(2)}) collective-permute-start(bf16[480,128]{1,0:T(8,128)(2,1)S(1)} %get-tuple-element.43), channel_id=1, source_target_pairs={{0,15},{1,14},{2,13},{3,12},{4,11},{5,10},{6,9},{7,8},{8,7},{9,6},... | collective-permute-start | bytes 368648 | tf_op jit(solution)/shard_map/ppermute | solution.py:418
  73.3 1.6 %collective-permute-done.12.refs_9_.refs_0_ = bf16[480,128]{1,0:T(8,128)(2,1)S(1)} collective-permute-done((bf16[480,128]{1,0:T(8,128)(2,1)S(1)}, bf16[480,128]{1,0:T(8,128)(2,1)S(1)}, u32[]{:S(2)}, u32[]{:S(2)}) %collective-permute-start.12) | collective-permute-done | bytes 122912 | tf_op jit(solution)/shard_map/ppermute | solution.py:418
  74.9 1.1 %collective-permute-start.17 = (bf16[480,128]{1,0:T(8,128)(2,1)S(1)}, bf16[480,128]{1,0:T(8,128)(2,1)S(1)}, u32[]{:S(2)}, u32[]{:S(2)}) collective-permute-start(bf16[480,128]{1,0:T(8,128)(2,1)S(1)} %get-tuple-element.44), channel_id=1, source_target_pairs={{0,7},{1,6},{2,5},{3,4},{4,3},{5,2},{6,1},{7,0},{8,15},{9,14},{10,... | collective-permute-start | bytes 368648 | tf_op jit(solution)/shard_map/ppermute | solution.py:418
  76.0 5.3 %collective-permute-done.14.refs_11_.refs_2_ = bf16[480,128]{1,0:T(8,128)(2,1)S(1)} collective-permute-done((bf16[480,128]{1,0:T(8,128)(2,1)S(1)}, bf16[480,128]{1,0:T(8,128)(2,1)S(1)}, u32[]{:S(2)}, u32[]{:S(2)}) %collective-permute-start.14) | collective-permute-done | bytes 122912 | tf_op jit(solution)/shard_map/ppermute | solution.py:418
  81.3 4.0 %collective-permute-done.16.refs_13_ = bf16[480,128]{1,0:T(8,128)(2,1)S(1)} collective-permute-done((bf16[480,128]{1,0:T(8,128)(2,1)S(1)}, bf16[480,128]{1,0:T(8,128)(2,1)S(1)}, u32[]{:S(2)}, u32[]{:S(2)}) %collective-permute-start.16) | collective-permute-done | bytes 122912 | tf_op jit(solution)/shard_map/ppermute | solution.py:418
  85.5 0.5 copy-done.16
  86.0 2.0 %collective-permute-start.18 = (bf16[4096,128]{1,0:T(8,128)(2,1)S(1)}, bf16[4096,128]{1,0:T(8,128)(2,1)S(1)}, u32[]{:S(2)}, u32[]{:S(2)}) collective-permute-start(bf16[4096,128]{1,0:T(8,128)(2,1)S(1)} %hold.1), channel_id=1, source_target_pairs={{0,1},{1,2},{2,3},{3,4},{4,5},{5,6},{6,7},{7,8},{8,9},{9,10},{10,1... | collective-permute-start | bytes 3145736 | tf_op jit(solution)/shard_map/ppermute | solution.py:445
  88.2 0.6 copy-done.21
  88.8 17.1 %tower.1 = f32[8,128]{1,0:T(8,128)} custom-call(f32[8,128]{1,0:T(8,128)} %copy-done.21, s32[1]{0:T(128)} %bitcast.2.me_ref, s32[5120]{0:T(1024)} %copy-done.18, bf16[3,640,640]{2,1,0:T(8,128)(2,1)} %cross_hbm.1, bf16[3,640]{1,0:T(4,128)(2,1)} %cross_bias_ref.1, bf16[640,4096]{1,0:T(8,128)(2,1)} %tower_hbm.1, bf16[1,4096]{1,0:T(2,128)(2,1)} %copy-done.19, ...), custom_call_target="tpu_custom_call" | custom-call | tf_op jit(solution)/shard_map/tower/pallas_call | solution.py:446
  106.0 1.0 deliver.1
  (81 shorter events, 1.0 us)
Async XLA Ops:
  0.6 23.5 %copy-start = (bf16[4096,128]{1,0:T(8,128)(2,1)S(1)}, bf16[4096,128]{1,0:T(8,128)(2,1)}, u32[]{:S(2)}) copy-start(bf16[4096,128]{1,0:T(8,128)(2,1)} %serving_hbm.3) | copy-start | bytes 3145732
  0.7 25.2 %copy-start.22 = (f32[4096]{0:T(1024)S(1)}, f32[4096]{0:T(1024)}, u32[]{:S(2)}) copy-start(f32[4096]{0:T(1024)} %param.14) | copy-start | bytes 49156
  0.7 25.2 %copy-start.13 = (bf16[4096,128]{1,0:T(8,128)(2,1)S(1)}, bf16[4096,128]{1,0:T(8,128)(2,1)}, u32[]{:S(2)}) copy-start(bf16[4096,128]{1,0:T(8,128)(2,1)} %item_hbm.1) | copy-start | bytes 3145732
  3.8 22.2 %all-to-all-start = ((bf16[16,144,128]{2,1,0:T(8,128)(2,1)}), bf16[16,144,128]{2,1,0:T(8,128)(2,1)S(1)}, u32[]{:S(2)}, u32[]{:S(2)}) async-start(bf16[16,144,128]{2,1,0:T(8,128)(2,1)} %get-tuple-element.25), calls=%async_computation | async-start | bytes 1179648 | tf_op jit(solution)/shard_map/all_to_all | solution.py:344
  10.4 13.8 %collective-permute-start = (bf16[2048,128]{1,0:T(8,128)(2,1)}, bf16[2048,128]{1,0:T(8,128)(2,1)S(1)}, u32[]{:S(2)}, u32[]{:S(2)}) collective-permute-start(bf16[2048,128]{1,0:T(8,128)(2,1)} %get-tuple-element.29), channel_id=1, source_target_pairs={{1,0},{2,1},{3,2},{5,4},{6,5},{7,6},{9,8},{10,9},{11,10},{13,12},{... | collective-permute-start | bytes 1572872 | tf_op jit(solution)/shard_map/ppermute | solution.py:352
  10.8 23.4 %copy-start.18 = (s32[5120]{0:T(1024)}, s32[5120]{0:T(1024)S(1)}, u32[]{:S(2)}) copy-start(s32[5120]{0:T(1024)S(1)} %reshape.35.refs_1_.slots_ref) | copy-start | bytes 61444
  10.8 23.4 %copy-start.19 = (bf16[1,4096]{1,0:T(2,128)(2,1)}, bf16[1,4096]{1,0:T(2,128)(2,1)S(1)}, u32[]{:S(2)}) copy-start(bf16[1,4096]{1,0:T(2,128)(2,1)S(1)} %reshape.36.refs_2_.tower_bias_ref) | copy-start | bytes 24580
  10.8 23.4 %copy-start.20 = (bf16[1,4096]{1,0:T(2,128)(2,1)}, bf16[1,4096]{1,0:T(2,128)(2,1)S(1)}, u32[]{:S(2)}) copy-start(bf16[1,4096]{1,0:T(2,128)(2,1)S(1)} %reshape.37.refs_3_.score_ref) | copy-start | bytes 24580
  25.0 8.9 %collective-permute-start.1 = (bf16[2048,128]{1,0:T(8,128)(2,1)}, bf16[2048,128]{1,0:T(8,128)(2,1)S(1)}, u32[]{:S(2)}, u32[]{:S(2)}) collective-permute-start(bf16[2048,128]{1,0:T(8,128)(2,1)} %stage.1), channel_id=1, source_target_pairs={{0,15},{1,0},{2,1},{3,2},{4,3},{5,4},{6,5},{7,6},{8,7},{9,8},{10,9... | collective-permute-start | bytes 1572872 | tf_op jit(solution)/shard_map/ppermute | solution.py:361
  25.1 8.8 %collective-permute-start.2 = (bf16[2048,128]{1,0:T(8,128)(2,1)S(1)}, bf16[2048,128]{1,0:T(8,128)(2,1)S(1)}, u32[]{:S(2)}, u32[]{:S(2)}) collective-permute-start(bf16[2048,128]{1,0:T(8,128)(2,1)S(1)} %collective-permute-done.refs_0_.lower_ref), channel_id=1, source_target_pairs={{3,15},{7,3},{11,7},{15,11},{19,31},{23,19},{27,23},{31,27}} | collective-permute-start | bytes 1572872 | tf_op jit(solution)/shard_map/ppermute | solution.py:362
  36.3 17.5 %collective-permute-start.4 = (bf16[480,128]{1,0:T(8,128)(2,1)S(1)}, bf16[480,128]{1,0:T(8,128)(2,1)S(1)}, u32[]{:S(2)}, u32[]{:S(2)}) collective-permute-start(bf16[480,128]{1,0:T(8,128)(2,1)S(1)} %get-tuple-element.31), channel_id=1, source_target_pairs={{0,9},{1,8},{2,11},{3,10},{4,13},{5,12},{6,15},{7,14},{8,1},{9,0},... | collective-permute-start | bytes 368648 | tf_op jit(solution)/shard_map/ppermute | solution.py:418
  38.1 17.8 %collective-permute-start.5 = (bf16[480,128]{1,0:T(8,128)(2,1)S(1)}, bf16[480,128]{1,0:T(8,128)(2,1)S(1)}, u32[]{:S(2)}, u32[]{:S(2)}) collective-permute-start(bf16[480,128]{1,0:T(8,128)(2,1)S(1)} %get-tuple-element.32), channel_id=1, source_target_pairs={{0,1},{1,0},{2,3},{3,2},{4,5},{5,4},{6,7},{7,6},{8,9},{9,8},{10,11... | collective-permute-start | bytes 368648 | tf_op jit(solution)/shard_map/ppermute | solution.py:418
  40.9 15.1 %collective-permute-start.3 = (bf16[480,128]{1,0:T(8,128)(2,1)S(1)}, bf16[480,128]{1,0:T(8,128)(2,1)S(1)}, u32[]{:S(2)}, u32[]{:S(2)}) collective-permute-start(bf16[480,128]{1,0:T(8,128)(2,1)S(1)} %gather.6), channel_id=1, source_target_pairs={{0,8},{1,9},{2,10},{3,11},{4,12},{5,13},{6,14},{7,15},{8,0},{9,1},... | collective-permute-start | bytes 368648 | tf_op jit(solution)/shard_map/ppermute | solution.py:418
  43.5 15.8 %collective-permute-start.6 = (bf16[480,128]{1,0:T(8,128)(2,1)S(1)}, bf16[480,128]{1,0:T(8,128)(2,1)S(1)}, u32[]{:S(2)}, u32[]{:S(2)}) collective-permute-start(bf16[480,128]{1,0:T(8,128)(2,1)S(1)} %get-tuple-element.33), channel_id=1, source_target_pairs={{0,10},{1,11},{2,8},{3,9},{4,14},{5,15},{6,12},{7,13},{8,2},{9,3},... | collective-permute-start | bytes 368648 | tf_op jit(solution)/shard_map/ppermute | solution.py:418
  48.6 10.8 %collective-permute-start.7 = (bf16[480,128]{1,0:T(8,128)(2,1)S(1)}, bf16[480,128]{1,0:T(8,128)(2,1)S(1)}, u32[]{:S(2)}, u32[]{:S(2)}) collective-permute-start(bf16[480,128]{1,0:T(8,128)(2,1)S(1)} %get-tuple-element.34), channel_id=1, source_target_pairs={{0,2},{1,3},{2,0},{3,1},{4,6},{5,7},{6,4},{7,5},{8,10},{9,11},{10,... | collective-permute-start | bytes 368648 | tf_op jit(solution)/shard_map/ppermute | solution.py:418
  53.8 34.3 %copy-start.1 = (bf16[480,128]{1,0:T(8,128)(2,1)}, bf16[480,128]{1,0:T(8,128)(2,1)S(1)}, u32[]{:S(2)}) copy-start(bf16[480,128]{1,0:T(8,128)(2,1)S(1)} %collective-permute-done.4.refs_1_) | copy-start | bytes 368644
  53.8 10.6 %collective-permute-start.8 = (bf16[480,128]{1,0:T(8,128)(2,1)S(1)}, bf16[480,128]{1,0:T(8,128)(2,1)S(1)}, u32[]{:S(2)}, u32[]{:S(2)}) collective-permute-start(bf16[480,128]{1,0:T(8,128)(2,1)S(1)} %get-tuple-element.35), channel_id=1, source_target_pairs={{0,11},{1,10},{2,9},{3,8},{4,15},{5,14},{6,13},{7,12},{8,3},{9,2},... | collective-permute-start | bytes 368648 | tf_op jit(solution)/shard_map/ppermute | solution.py:418
  55.9 32.1 %copy-start.2 = (bf16[480,128]{1,0:T(8,128)(2,1)}, bf16[480,128]{1,0:T(8,128)(2,1)S(1)}, u32[]{:S(2)}) copy-start(bf16[480,128]{1,0:T(8,128)(2,1)S(1)} %collective-permute-done.5.refs_2_) | copy-start | bytes 368644
  55.9 14.1 %collective-permute-start.10 = (bf16[480,128]{1,0:T(8,128)(2,1)S(1)}, bf16[480,128]{1,0:T(8,128)(2,1)S(1)}, u32[]{:S(2)}, u32[]{:S(2)}) collective-permute-start(bf16[480,128]{1,0:T(8,128)(2,1)S(1)} %get-tuple-element.37), channel_id=1, source_target_pairs={{0,12},{1,13},{2,14},{3,15},{4,8},{5,9},{6,10},{7,11},{8,4},{9,5},... | collective-permute-start | bytes 368648 | tf_op jit(solution)/shard_map/ppermute | solution.py:418
  56.0 32.1 %copy-start.3 = (bf16[480,128]{1,0:T(8,128)(2,1)}, bf16[480,128]{1,0:T(8,128)(2,1)S(1)}, u32[]{:S(2)}) copy-start(bf16[480,128]{1,0:T(8,128)(2,1)S(1)} %collective-permute-done.3.refs_0_) | copy-start | bytes 368644
  56.0 15.4 %collective-permute-start.11 = (bf16[480,128]{1,0:T(8,128)(2,1)S(1)}, bf16[480,128]{1,0:T(8,128)(2,1)S(1)}, u32[]{:S(2)}, u32[]{:S(2)}) collective-permute-start(bf16[480,128]{1,0:T(8,128)(2,1)S(1)} %get-tuple-element.38), channel_id=1, source_target_pairs={{0,4},{1,5},{2,6},{3,7},{4,0},{5,1},{6,2},{7,3},{8,12},{9,13},{10,... | collective-permute-start | bytes 368648 | tf_op jit(solution)/shard_map/ppermute | solution.py:418
  59.3 28.8 %copy-start.4 = (bf16[480,128]{1,0:T(8,128)(2,1)}, bf16[480,128]{1,0:T(8,128)(2,1)S(1)}, u32[]{:S(2)}) copy-start(bf16[480,128]{1,0:T(8,128)(2,1)S(1)} %collective-permute-done.6.refs_3_.refs_0_) | copy-start | bytes 368644
  59.3 12.1 %collective-permute-start.9 = (bf16[480,128]{1,0:T(8,128)(2,1)S(1)}, bf16[480,128]{1,0:T(8,128)(2,1)S(1)}, u32[]{:S(2)}, u32[]{:S(2)}) collective-permute-start(bf16[480,128]{1,0:T(8,128)(2,1)S(1)} %get-tuple-element.36), channel_id=1, source_target_pairs={{0,3},{1,2},{2,1},{3,0},{4,7},{5,6},{6,5},{7,4},{8,11},{9,10},{10,... | collective-permute-start | bytes 368648 | tf_op jit(solution)/shard_map/ppermute | solution.py:418
  59.4 28.7 %copy-start.5 = (bf16[480,128]{1,0:T(8,128)(2,1)}, bf16[480,128]{1,0:T(8,128)(2,1)S(1)}, u32[]{:S(2)}) copy-start(bf16[480,128]{1,0:T(8,128)(2,1)S(1)} %collective-permute-done.7.refs_4_.refs_1_) | copy-start | bytes 368644
  59.4 15.5 %collective-permute-start.12 = (bf16[480,128]{1,0:T(8,128)(2,1)S(1)}, bf16[480,128]{1,0:T(8,128)(2,1)S(1)}, u32[]{:S(2)}, u32[]{:S(2)}) collective-permute-start(bf16[480,128]{1,0:T(8,128)(2,1)S(1)} %get-tuple-element.39), channel_id=1, source_target_pairs={{0,13},{1,12},{2,15},{3,14},{4,9},{5,8},{6,11},{7,10},{8,5},{9,4},... | collective-permute-start | bytes 368648 | tf_op jit(solution)/shard_map/ppermute | solution.py:418
  64.4 23.7 %copy-start.6 = (bf16[480,128]{1,0:T(8,128)(2,1)}, bf16[480,128]{1,0:T(8,128)(2,1)S(1)}, u32[]{:S(2)}) copy-start(bf16[480,128]{1,0:T(8,128)(2,1)S(1)} %collective-permute-done.8.refs_5_.refs_2_) | copy-start | bytes 368644
  64.4 11.6 %collective-permute-start.13 = (bf16[480,128]{1,0:T(8,128)(2,1)S(1)}, bf16[480,128]{1,0:T(8,128)(2,1)S(1)}, u32[]{:S(2)}, u32[]{:S(2)}) collective-permute-start(bf16[480,128]{1,0:T(8,128)(2,1)S(1)} %get-tuple-element.40), channel_id=1, source_target_pairs={{0,5},{1,4},{2,7},{3,6},{4,1},{5,0},{6,3},{7,2},{8,13},{9,12},{10,... | collective-permute-start | bytes 368648 | tf_op jit(solution)/shard_map/ppermute | solution.py:418
  70.1 11.2 %collective-permute-start.14 = (bf16[480,128]{1,0:T(8,128)(2,1)S(1)}, bf16[480,128]{1,0:T(8,128)(2,1)S(1)}, u32[]{:S(2)}, u32[]{:S(2)}) collective-permute-start(bf16[480,128]{1,0:T(8,128)(2,1)S(1)} %get-tuple-element.41), channel_id=1, source_target_pairs={{0,14},{1,15},{2,12},{3,13},{4,10},{5,11},{6,8},{7,9},{8,6},{9,7},... | collective-permute-start | bytes 368648 | tf_op jit(solution)/shard_map/ppermute | solution.py:418
  71.4 9.9 %collective-permute-start.15 = (bf16[480,128]{1,0:T(8,128)(2,1)S(1)}, bf16[480,128]{1,0:T(8,128)(2,1)S(1)}, u32[]{:S(2)}, u32[]{:S(2)}) collective-permute-start(bf16[480,128]{1,0:T(8,128)(2,1)S(1)} %get-tuple-element.42), channel_id=1, source_target_pairs={{0,6},{1,7},{2,4},{3,5},{4,2},{5,3},{6,0},{7,1},{8,14},{9,15},{10,... | collective-permute-start | bytes 368648 | tf_op jit(solution)/shard_map/ppermute | solution.py:418
  71.4 13.9 %collective-permute-start.16 = (bf16[480,128]{1,0:T(8,128)(2,1)S(1)}, bf16[480,128]{1,0:T(8,128)(2,1)S(1)}, u32[]{:S(2)}, u32[]{:S(2)}) collective-permute-start(bf16[480,128]{1,0:T(8,128)(2,1)S(1)} %get-tuple-element.43), channel_id=1, source_target_pairs={{0,15},{1,14},{2,13},{3,12},{4,11},{5,10},{6,9},{7,8},{8,7},{9,6},... | collective-permute-start | bytes 368648 | tf_op jit(solution)/shard_map/ppermute | solution.py:418
  74.9 10.4 %collective-permute-start.17 = (bf16[480,128]{1,0:T(8,128)(2,1)S(1)}, bf16[480,128]{1,0:T(8,128)(2,1)S(1)}, u32[]{:S(2)}, u32[]{:S(2)}) collective-permute-start(bf16[480,128]{1,0:T(8,128)(2,1)S(1)} %get-tuple-element.44), channel_id=1, source_target_pairs={{0,7},{1,6},{2,5},{3,4},{4,3},{5,2},{6,1},{7,0},{8,15},{9,14},{10,... | collective-permute-start | bytes 368648 | tf_op jit(solution)/shard_map/ppermute | solution.py:418
  86.0 19.9 %collective-permute-start.18 = (bf16[4096,128]{1,0:T(8,128)(2,1)S(1)}, bf16[4096,128]{1,0:T(8,128)(2,1)S(1)}, u32[]{:S(2)}, u32[]{:S(2)}) collective-permute-start(bf16[4096,128]{1,0:T(8,128)(2,1)S(1)} %hold.1), channel_id=1, source_target_pairs={{0,1},{1,2},{2,3},{3,4},{4,5},{5,6},{6,7},{7,8},{8,9},{9,10},{10,1... | collective-permute-start | bytes 3145736 | tf_op jit(solution)/shard_map/ppermute | solution.py:445
  (14 other events, 143.2 us)
